TPU v7x, 512 devices: a whole 4x4x16 slice. The times are simulated.
512 devices in a mesh: real: 2 (over y_hi), gx: 64 (over z, x), gy: 4 (over y_lo, core).
Axes of the slice: x: 4, y: 4 (y_hi: 2, y_lo: 2; y = y_hi * 2 + y_lo), z: 16, core: 2. Of those that a mesh axis runs over, the one named last changes fastest.
Arguments:
- design: float32 [512, 16, 512], P('gx', 'real', 'gy'), may hold values from 0.05 to 0.95
- load: float32 [512, 16, 512], P('gx', 'real', 'gy'), may hold values from -6 to 6
- void_mask: int32 [512, 16, 512], P('gx', 'real', 'gy'), may hold values 0 or 1
- solid_mask: int32 [512, 16, 512], P('gx', 'real', 'gy'), may hold values 0 or 1
Outputs:
- sensitivity: float32 [512, 16, 512], P('gx', 'real', 'gy')
- compliance: float32 [3], replicated
All inputs are finite; a program needn't handle non-finite values. No bound on the sum of `void_mask` or of `solid_mask` on one device may be relied on, other than what follows from the above.
Results may differ from a plain program's by a relative error of at most 0.0003.
Values sent between devices are 32-bit elements; how exact they have to be, the bound alone decides.
No kernel may reach another device: no remote copies, remote signals or barrier semaphores. Data moves between devices by JAX's collectives and lax.ppermute only.
A program may use at most 128 MiB of HBM per device.

v0:
```python
import jax
import jax.numpy as jnp
from jax import lax
from jax.sharding import PartitionSpec as P

LEVELS = 4


EMIN = 0.01
BETA = 8.0
OMEGA = 0.6
DIRECTIONS = ((-3, 1), (-3, -1), (-2, 1), (-2, -1), (-1, 1), (-1, -1))


def extended(block, sides, width):
    for axis, dim in sides:
        count = lax.axis_size(axis)
        forward = [(i, i + 1) for i in range(count - 1)]
        backward = [(target, source) for source, target in forward]
        low = lax.ppermute(
            lax.slice_in_dim(block, block.shape[dim] - width, None, axis=dim), axis, forward
        )
        high = lax.ppermute(lax.slice_in_dim(block, 0, width, axis=dim), axis, backward)
        block = jnp.concatenate([low, block, high], axis=dim)
    return block


def shifted(padded, along, offset):
    picker = [slice(None)] * padded.ndim
    for chosen_dim in (-3, -2, -1):
        extent = padded.shape[chosen_dim]
        if chosen_dim == along:
            picker[chosen_dim] = slice(1 + offset, extent - 1 + offset)
        else:
            picker[chosen_dim] = slice(1, extent - 1)
    return padded[tuple(picker)]


def filter_apply(padded):
    total = 2.0 * shifted(padded, 0, 0)
    for along, offset in DIRECTIONS:
        total = total + shifted(padded, along, offset)
    return total


def conductances(padded, factor):
    middle = shifted(padded, 0, 0)
    return [
        factor * 0.5 * (middle + shifted(padded, along, offset)) for along, offset in DIRECTIONS
    ]


def apply_operator(padded, links):
    middle = shifted(padded, 0, 0)
    total = jnp.zeros(middle.shape, jnp.float32)
    for link, (along, offset) in zip(links, DIRECTIONS):
        total = total + link * (middle - shifted(padded, along, offset))
    return total


def pool(values, span):
    shape_now = values.shape
    lead = shape_now[:-3]
    blocks = values.reshape(
        lead
        + (shape_now[-3] // span, span, shape_now[-2] // span, span, shape_now[-1] // span, span)
    )
    return jnp.mean(blocks, axis=(-5, -3, -1))


def widen(values):
    return jnp.repeat(jnp.repeat(jnp.repeat(values, 2, -3), 2, -2), 2, -1)


def field_halo(values):
    return extended(values, (("real", 2), ("gx", 1), ("gy", 3)), 1)


def global_dot(first, second):
    return lax.psum(jnp.sum(first * second, axis=(-3, -2, -1), keepdims=True), ("real", "gx", "gy"))


def body(design, load, void_mask, solid_mask):
    both = extended(
        jnp.stack([design, jnp.ones_like(design)]), (("real", 2), ("gx", 1), ("gy", 3)), 1
    )
    smoothed = filter_apply(both)
    weights = smoothed[1]
    filtered = smoothed[0] / weights
    etas = jnp.array([0.7, 0.5, 0.3], jnp.float32).reshape(3, 1, 1, 1)
    tanh_eta = jnp.tanh(BETA * etas)
    denominator = tanh_eta + jnp.tanh(BETA * (1.0 - etas))
    inner_tanh = jnp.tanh(BETA * (filtered[None] - etas))
    projected = (tanh_eta + inner_tanh) / denominator
    slope = BETA * (1.0 - inner_tanh * inner_tanh) / denominator
    voids = void_mask.astype(jnp.float32)
    solids = solid_mask.astype(jnp.float32)
    physical = (1.0 - voids) * (solids + (1.0 - solids) * projected)
    stiffness = EMIN + (1.0 - EMIN) * physical**3
    operators = []
    level_field = stiffness
    for depth_level in range(LEVELS):
        if depth_level > 0:
            level_field = pool(level_field, 2)
        padded_level = extended(level_field, (("real", 2), ("gx", 1), ("gy", 3)), 1)
        links = conductances(padded_level, 0.25**depth_level)
        diag_sum = links[0]
        for link in links[1:]:
            diag_sum = diag_sum + link
        operators.append((links, diag_sum))

    def precondition(rhs, depth_level):
        links, diag_sum = operators[depth_level]
        approx = OMEGA * rhs / diag_sum
        if depth_level < LEVELS - 1:
            leftover = rhs - apply_operator(field_halo(approx), links)
            approx = approx + widen(precondition(pool(leftover, 2), depth_level + 1))
        return approx + OMEGA * (rhs - apply_operator(field_halo(approx), links)) / diag_sum

    fine_links = operators[0][0]
    residual = jnp.broadcast_to(load, (3,) + load.shape)
    state = jnp.zeros(residual.shape, jnp.float32)
    precond = precondition(residual, 0)
    direction = precond
    rz_now = global_dot(residual, precond)
    for step in range(2):
        image = apply_operator(field_halo(direction), fine_links)
        alpha = rz_now / global_dot(direction, image)
        state = state + alpha * direction
        residual = residual - alpha * image
        if step == 0:
            precond = precondition(residual, 0)
            rz_next = global_dot(residual, precond)
            direction = precond + rz_next / rz_now * direction
            rz_now = rz_next
    compliance = global_dot(load[None], state).reshape(3)
    state_pad = field_halo(state)
    middle = shifted(state_pad, 0, 0)
    dcde = jnp.zeros(state.shape, jnp.float32)
    for along, offset in DIRECTIONS:
        gap = middle - shifted(state_pad, along, offset)
        dcde = dcde - 0.5 * gap * gap
    combined = jnp.sum(
        dcde * 3.0 * physical * physical * (1.0 - EMIN) * (1.0 - voids) * (1.0 - solids) * slope,
        axis=0,
    )
    spread = extended(combined / weights, (("real", 1), ("gx", 0), ("gy", 2)), 1)
    sensitivity = filter_apply(spread)
    return (sensitivity, compliance)


def solution(mesh):
    in_specs = (
        P("gx", "real", "gy"),
        P("gx", "real", "gy"),
        P("gx", "real", "gy"),
        P("gx", "real", "gy"),
    )
    out_specs = (P("gx", "real", "gy"), P())
    return jax.shard_map(body, mesh=mesh, in_specs=in_specs, out_specs=out_specs, check_vma=False)
```

profile of v0, /device:TPU:1, one launch (start us, length us, event | category | flops | bytes accessed | tf_op | source)
XLA Modules:
  0.0 1091.2 jit_solution(3032074964031282673)
XLA Ops:
  1.5 5.6 collective-permute-start
  21.6 5.4 collective-permute-start.4
  45.2 5.5 collective-permute-start.42
  54.8 5.5 collective-permute-start.18
  61.7 5.5 collective-permute-start.30
  76.1 4.7 collective-permute-start.45
  81.1 6.1 collective-permute-start.11
  99.0 4.6 collective-permute-start.21
  103.6 5.8 collective-permute-start.15
  125.0 7.7 reshape.149
  136.2 6.0 collective-permute-start.24
  144.8 6.4 collective-permute-start.33
  162.8 3.7 collective-permute-start.29
  174.3 6.4 collective-permute-start.36
  182.1 4.5 collective-permute-done.37
  186.6 5.7 collective-permute-start.39
  209.4 5.5 collective-permute-start.48
  215.6 3.8 collective-permute-start.51
  226.5 3.9 collective-permute-start.53
  231.6 6.0 collective-permute-start.54
  238.9 4.5 collective-permute-done.55
  254.3 5.8 collective-permute-start.59
  265.0 4.6 collective-permute-done.61
  269.6 5.7 collective-permute-start.63
  282.1 6.2 collective-permute-start.65
  294.4 4.6 collective-permute-done.67
  299.1 3.7 collective-permute-start.69
  309.8 6.3 collective-permute-start.71
  320.6 5.5 collective-permute-start.72
  326.9 3.7 collective-permute-start.75
  337.7 6.7 collective-permute-start.77
  347.6 125.7 %all-reduce.1 = (f32[3,1,1,1]{0,3,2,1:T(1,128)S(1)}, f32[3,1,1,1]{0,3,2,1:T(1,128)S(1)}) all-reduce(f32[3,1,1,1]{0,3,2,1:T(1,128)S(1)} %bitcast.176, f32[3,1,1,1]{0,3,2,1:T(1,128)S(1)} %bitcast.175), channel_id=1, replica_groups=mesh['real'=2,'gx'=64,'gy'=4] {'real','gx','gy'}, use_global_device_ids=true, to_apply=%region_9.0 | all-reduce | flops 6 | bytes 48 | tf_op jit(solution)/shard_map/psum | solution.py:80
  477.8 4.6 collective-permute-done.79
  490.8 5.5 collective-permute-start.82
  496.2 11.8 %collective-permute-start.83 = (f32[3,10,10,1]{3,0,2,1:T(4,128)S(1)}, f32[3,10,10,1]{3,0,2,1:T(4,128)S(1)}, u32[]{:S(2)}, u32[]{:S(2)}) collective-permute-start(f32[3,10,10,1]{3,0,2,1:T(4,128)S(1)} %get-tuple-element.54), channel_id=1, source_target_pairs={{0,1},{1,2},{2,3},{4,5},{5,6},{6,7},{8,9},{9,10},{10,11},{12,13},{... | collective-permute-start | bytes 3608 | tf_op jit(solution)/shard_map/ppermute | solution.py:20
  508.5 7.7 reshape.157
  522.4 4.6 collective-permute-done.85
  534.7 3.7 collective-permute-start.88
  547.0 4.5 collective-permute-done.91
  551.6 3.9 collective-permute-start.93
  562.9 5.5 collective-permute-start.95
  571.0 5.5 collective-permute-start.96
  577.2 3.7 collective-permute-start.99
  587.6 6.5 collective-permute-start.101
  595.9 6.0 collective-permute-start.102
  603.3 4.5 collective-permute-done.103
  607.8 3.7 collective-permute-start.105
  618.3 6.2 collective-permute-start.107
  629.4 4.6 collective-permute-done.109
  634.0 3.7 collective-permute-start.111
  644.5 6.2 collective-permute-start.113
  654.7 5.5 collective-permute-start.114
  661.1 3.7 collective-permute-start.117
  671.8 6.6 collective-permute-start.119
  681.6 115.5 %psum.37 = f32[3,1,1,1]{0,3,2,1:T(1,128)S(1)} all-reduce(f32[3,1,1,1]{0,3,2,1:T(1,128)S(1)} %bitcast.177), channel_id=1, replica_groups=mesh['real'=2,'gx'=64,'gy'=4] {'real','gx','gy'}, use_global_device_ids=true, to_apply=%region_17.0 | all-reduce | flops 3 | bytes 24 | tf_op jit(solution)/shard_map/psum | solution.py:80
  801.6 4.6 collective-permute-done.121
  814.6 5.5 collective-permute-start.124
  825.2 104.6 %psum.38 = f32[3,1,1,1]{0,3,2,1:T(1,128)S(1)} all-reduce(f32[3,1,1,1]{0,3,2,1:T(1,128)S(1)} %bitcast.174), channel_id=1, replica_groups=mesh['real'=2,'gx'=64,'gy'=4] {'real','gx','gy'}, use_global_device_ids=true, to_apply=%region_19.0 | all-reduce | flops 3 | bytes 24 | tf_op jit(solution)/shard_map/psum | solution.py:80
  931.3 5.5 collective-permute-start.126
  945.7 5.2 collective-permute-start.130
  956.1 5.4 collective-permute-start.132
  962.8 4.5 collective-permute-done.133
  977.8 6.2 collective-permute-start.137
  984.0 106.2 %psum.39 = f32[3]{0:T(128)} all-reduce(f32[3]{0:T(128)S(1)} %get-tuple-element.12), channel_id=1, replica_groups=mesh['real'=2,'gx'=64,'gy'=4] {'real','gx','gy'}, use_global_device_ids=true, to_apply=%region_22.23 | all-reduce | flops 3 | bytes 24 | tf_op jit(solution)/shard_map/psum | solution.py:80
  (527 shorter events, 314.4 us)
Async XLA Ops:
  1.5 9.1 collective-permute-start
  21.6 17.6 %collective-permute-start.4 = (f32[2,10,10,1]{3,0,2,1:T(2,128)S(1)}, f32[2,10,10,1]{3,0,2,1:T(2,128)S(1)}, u32[]{:S(2)}, u32[]{:S(2)}) collective-permute-start(f32[2,10,10,1]{3,0,2,1:T(2,128)S(1)} %get-tuple-element.91), channel_id=1, source_target_pairs={{1,0},{2,1},{3,2},{5,4},{6,5},{7,6},{9,8},{10,9},{11,10},{13,12},{... | collective-permute-start | bytes 2408 | tf_op jit(solution)/shard_map/ppermute | solution.py:23
  27.1 12.1 %collective-permute-start.5 = (f32[2,10,10,1]{3,0,2,1:T(2,128)S(1)}, f32[2,10,10,1]{3,0,2,1:T(2,128)S(1)}, u32[]{:S(2)}, u32[]{:S(2)}) collective-permute-start(f32[2,10,10,1]{3,0,2,1:T(2,128)S(1)} %get-tuple-element.92), channel_id=1, source_target_pairs={{0,1},{1,2},{2,3},{4,5},{5,6},{6,7},{8,9},{9,10},{10,11},{12,13},{... | collective-permute-start | bytes 2408 | tf_op jit(solution)/shard_map/ppermute | solution.py:20
  43.9 17.7 %collective-permute-start.43 = (f32[3,1,1,16]{3,0,2,1:T(4,128)S(1)}, f32[3,1,1,16]{3,0,2,1:T(4,128)S(1)}, u32[]{:S(2)}, u32[]{:S(2)}) collective-permute-start(f32[3,1,1,16]{3,0,2,1:T(4,128)S(1)} %multiply_bitcast_fusion), channel_id=1, source_target_pairs={{256,0},{257,1},{258,2},{259,3},{260,4},{261,5},{262,6},{263,7},{2... | collective-permute-start | bytes 584 | tf_op jit(solution)/shard_map/ppermute | solution.py:23
  45.2 22.0 %collective-permute-start.42 = (f32[3,1,1,16]{3,0,2,1:T(4,128)S(1)}, f32[3,1,1,16]{3,0,2,1:T(4,128)S(1)}, u32[]{:S(2)}, u32[]{:S(2)}) collective-permute-start(f32[3,1,1,16]{3,0,2,1:T(4,128)S(1)} %multiply_bitcast_fusion), channel_id=1, source_target_pairs={{0,256},{1,257},{2,258},{3,259},{4,260},{5,261},{6,262},{7,263},{8... | collective-permute-start | bytes 584 | tf_op jit(solution)/shard_map/ppermute | solution.py:20
  52.2 8.1 collective-permute-start.7
  53.5 42.9 %collective-permute-start.19 = (f32[3,4,1,64]{3,2,1,0:T(1,128)S(1)}, f32[3,4,1,64]{3,2,1,0:T(1,128)S(1)}, u32[]{:S(2)}, u32[]{:S(2)}) collective-permute-start(f32[3,4,1,64]{3,2,1,0:T(1,128)S(1)} %get-tuple-element.157), channel_id=1, source_target_pairs={{256,0},{257,1},{258,2},{259,3},{260,4},{261,5},{262,6},{263,7},{2... | collective-permute-start | bytes 9224 | tf_op jit(solution)/shard_map/ppermute | solution.py:23
  54.8 42.9 %collective-permute-start.18 = (f32[3,4,1,64]{3,2,1,0:T(1,128)S(1)}, f32[3,4,1,64]{3,2,1,0:T(1,128)S(1)}, u32[]{:S(2)}, u32[]{:S(2)}) collective-permute-start(f32[3,4,1,64]{3,2,1,0:T(1,128)S(1)} %get-tuple-element.158), channel_id=1, source_target_pairs={{0,256},{1,257},{2,258},{3,259},{4,260},{5,261},{6,262},{7,263},{8... | collective-permute-start | bytes 9224 | tf_op jit(solution)/shard_map/ppermute | solution.py:20
  60.3 20.8 %collective-permute-start.31 = (f32[3,2,1,32]{3,2,1,0:T(1,128)S(1)}, f32[3,2,1,32]{3,2,1,0:T(1,128)S(1)}, u32[]{:S(2)}, u32[]{:S(2)}) collective-permute-start(f32[3,2,1,32]{3,2,1,0:T(1,128)S(1)} %get-tuple-element.185), channel_id=1, source_target_pairs={{256,0},{257,1},{258,2},{259,3},{260,4},{261,5},{262,6},{263,7},{2... | collective-permute-start | bytes 2312 | tf_op jit(solution)/shard_map/ppermute | solution.py:23
  61.7 25.5 %collective-permute-start.30 = (f32[3,2,1,32]{3,2,1,0:T(1,128)S(1)}, f32[3,2,1,32]{3,2,1,0:T(1,128)S(1)}, u32[]{:S(2)}, u32[]{:S(2)}) collective-permute-start(f32[3,2,1,32]{3,2,1,0:T(1,128)S(1)} %get-tuple-element.186), channel_id=1, source_target_pairs={{0,256},{1,257},{2,258},{3,259},{4,260},{5,261},{6,262},{7,263},{8... | collective-permute-start | bytes 2312 | tf_op jit(solution)/shard_map/ppermute | solution.py:20
  76.1 105.9 %collective-permute-start.45 = (f32[3,1,3,16]{3,0,2,1:T(4,128)S(1)}, f32[3,1,3,16]{3,0,2,1:T(4,128)S(1)}, u32[]{:S(2)}, u32[]{:S(2)}) collective-permute-start(f32[3,1,3,16]{3,0,2,1:T(4,128)S(1)} %pad_maximum_fusion.334), channel_id=1, source_target_pairs={{0,4},{4,8},{8,12},{12,16},{16,20},{20,24},{24,28},{28,32},{32,36}... | collective-permute-start | bytes 1736 | tf_op jit(solution)/shard_map/ppermute | solution.py:20
  81.1 8.8 collective-permute-start.11
  87.2 7.2 collective-permute-start.10
  89.9 92.2 %collective-permute-start.44 = (f32[3,1,3,16]{3,0,2,1:T(4,128)S(1)}, f32[3,1,3,16]{3,0,2,1:T(4,128)S(1)}, u32[]{:S(2)}, u32[]{:S(2)}) collective-permute-start(f32[3,1,3,16]{3,0,2,1:T(4,128)S(1)} %pad_maximum_fusion.334), channel_id=1, source_target_pairs={{4,0},{8,4},{12,8},{16,12},{20,16},{24,20},{28,24},{32,28},{36,32}... | collective-permute-start | bytes 1736 | tf_op jit(solution)/shard_map/ppermute | solution.py:23
  96.4 7.2 collective-permute-start.13
  97.7 11.7 %collective-permute-start.20 = (f32[3,1,6,64]{3,2,1,0:T(8,128)S(1)}, f32[3,1,6,64]{3,2,1,0:T(8,128)S(1)}, u32[]{:S(2)}, u32[]{:S(2)}) collective-permute-start(f32[3,1,6,64]{3,2,1,0:T(8,128)S(1)} %get-tuple-element.131), channel_id=1, source_target_pairs={{4,0},{8,4},{12,8},{16,12},{20,16},{24,20},{28,24},{32,28},{36,32}... | collective-permute-start | bytes 13832 | tf_op jit(solution)/shard_map/ppermute | solution.py:23
  99.0 10.4 collective-permute-start.21
  103.6 7.1 collective-permute-start.15
  114.2 7.7 collective-permute-start.16
  116.2 8.3 collective-permute-start.17
  119.9 16.0 %collective-permute-start.23 = (f32[3,6,6,1]{3,2,1,0:T(8,128)S(1)}, f32[3,6,6,1]{3,2,1,0:T(8,128)S(1)}, u32[]{:S(2)}, u32[]{:S(2)}) collective-permute-start(f32[3,6,6,1]{3,2,1,0:T(8,128)S(1)} %get-tuple-element.119), channel_id=1, source_target_pairs={{0,1},{1,2},{2,3},{4,5},{5,6},{6,7},{8,9},{9,10},{10,11},{12,13},{... | collective-permute-start | bytes 1304 | tf_op jit(solution)/shard_map/ppermute | solution.py:20
  122.0 14.0 %collective-permute-start.22 = (f32[3,6,6,1]{3,2,1,0:T(8,128)S(1)}, f32[3,6,6,1]{3,2,1,0:T(8,128)S(1)}, u32[]{:S(2)}, u32[]{:S(2)}) collective-permute-start(f32[3,6,6,1]{3,2,1,0:T(8,128)S(1)} %get-tuple-element.120), channel_id=1, source_target_pairs={{1,0},{2,1},{3,2},{5,4},{6,5},{7,6},{9,8},{10,9},{11,10},{13,12},{... | collective-permute-start | bytes 1304 | tf_op jit(solution)/shard_map/ppermute | solution.py:23
  136.2 8.6 collective-permute-start.24
  142.2 9.0 collective-permute-start.25
  143.5 11.4 %collective-permute-start.32 = (f32[3,1,4,32]{3,2,1,0:T(4,128)S(1)}, f32[3,1,4,32]{3,2,1,0:T(4,128)S(1)}, u32[]{:S(2)}, u32[]{:S(2)}) collective-permute-start(f32[3,1,4,32]{3,2,1,0:T(4,128)S(1)} %get-tuple-element.173), channel_id=1, source_target_pairs={{4,0},{8,4},{12,8},{16,12},{20,16},{24,20},{28,24},{32,28},{36,32}... | collective-permute-start | bytes 4616 | tf_op jit(solution)/shard_map/ppermute | solution.py:23
  144.8 11.4 %collective-permute-start.33 = (f32[3,1,4,32]{3,2,1,0:T(4,128)S(1)}, f32[3,1,4,32]{3,2,1,0:T(4,128)S(1)}, u32[]{:S(2)}, u32[]{:S(2)}) collective-permute-start(f32[3,1,4,32]{3,2,1,0:T(4,128)S(1)} %get-tuple-element.174), channel_id=1, source_target_pairs={{0,4},{4,8},{8,12},{12,16},{16,20},{20,24},{24,28},{28,32},{32,36}... | collective-permute-start | bytes 4616 | tf_op jit(solution)/shard_map/ppermute | solution.py:20
  159.8 9.2 collective-permute-start.28
  162.8 8.1 collective-permute-start.29
  174.3 7.7 collective-permute-start.36
  186.6 10.2 collective-permute-start.39
  193.7 11.5 %collective-permute-start.47 = (f32[3,3,3,1]{3,0,2,1:T(4,128)S(1)}, f32[3,3,3,1]{3,0,2,1:T(4,128)S(1)}, u32[]{:S(2)}, u32[]{:S(2)}) collective-permute-start(f32[3,3,3,1]{3,0,2,1:T(4,128)S(1)} %get-tuple-element.163), channel_id=1, source_target_pairs={{0,1},{1,2},{2,3},{4,5},{5,6},{6,7},{8,9},{9,10},{10,11},{12,13},{... | collective-permute-start | bytes 332 | tf_op jit(solution)/shard_map/ppermute | solution.py:20
  197.2 7.6 collective-permute-start.40
  208.1 6.8 collective-permute-start.49
  231.6 7.3 collective-permute-start.54
  252.0 8.1 collective-permute-start.58
  254.3 6.7 collective-permute-start.59
  269.6 7.1 collective-permute-start.63
  280.2 8.2 collective-permute-start.64
  282.1 7.6 collective-permute-start.65
  307.9 9.7 collective-permute-start.70
  309.8 8.9 collective-permute-start.71
  319.3 6.8 collective-permute-start.73
  335.7 10.1 collective-permute-start.76
  337.7 9.4 collective-permute-start.77
  490.8 17.3 %collective-permute-start.82 = (f32[3,10,10,1]{3,0,2,1:T(4,128)S(1)}, f32[3,10,10,1]{3,0,2,1:T(4,128)S(1)}, u32[]{:S(2)}, u32[]{:S(2)}) collective-permute-start(f32[3,10,10,1]{3,0,2,1:T(4,128)S(1)} %get-tuple-element.53), channel_id=1, source_target_pairs={{1,0},{2,1},{3,2},{5,4},{6,5},{7,6},{9,8},{10,9},{11,10},{13,12},{... | collective-permute-start | bytes 3608 | tf_op jit(solution)/shard_map/ppermute | solution.py:23
  496.2 11.9 %collective-permute-start.83 = (f32[3,10,10,1]{3,0,2,1:T(4,128)S(1)}, f32[3,10,10,1]{3,0,2,1:T(4,128)S(1)}, u32[]{:S(2)}, u32[]{:S(2)}) collective-permute-start(f32[3,10,10,1]{3,0,2,1:T(4,128)S(1)} %get-tuple-element.54), channel_id=1, source_target_pairs={{0,1},{1,2},{2,3},{4,5},{5,6},{6,7},{8,9},{9,10},{10,11},{12,13},{... | collective-permute-start | bytes 3608 | tf_op jit(solution)/shard_map/ppermute | solution.py:20
  560.2 8.2 collective-permute-start.94
  569.7 6.8 collective-permute-start.97
  585.7 8.4 collective-permute-start.100
  587.6 7.4 collective-permute-start.101
  595.9 7.3 collective-permute-start.102
  616.4 8.1 collective-permute-start.106
  618.3 7.1 collective-permute-start.107
  642.5 8.2 collective-permute-start.112
  644.5 7.6 collective-permute-start.113
  653.4 6.8 collective-permute-start.115
  669.9 10.0 collective-permute-start.118
  671.8 9.2 collective-permute-start.119
  814.6 8.3 collective-permute-start.124
  930.0 6.8 collective-permute-start.127
  945.7 7.9 collective-permute-start.130
  956.1 6.7 collective-permute-start.132
  975.4 114.8 %collective-permute-start.136 = (f32[10,10,1]{2,1,0:T(8,128)S(1)}, f32[10,10,1]{2,1,0:T(8,128)S(1)}, u32[]{:S(2)}, u32[]{:S(2)}) collective-permute-start(f32[10,10,1]{2,1,0:T(8,128)S(1)} %get-tuple-element.109), channel_id=1, source_target_pairs={{1,0},{2,1},{3,2},{5,4},{6,5},{7,6},{9,8},{10,9},{11,10},{13,12},{... | collective-permute-start | bytes 1208 | tf_op jit(solution)/shard_map/ppermute | solution.py:23
  977.8 112.5 %collective-permute-start.137 = (f32[10,10,1]{2,1,0:T(8,128)S(1)}, f32[10,10,1]{2,1,0:T(8,128)S(1)}, u32[]{:S(2)}, u32[]{:S(2)}) collective-permute-start(f32[10,10,1]{2,1,0:T(8,128)S(1)} %get-tuple-element.110), channel_id=1, source_target_pairs={{0,1},{1,2},{2,3},{4,5},{5,6},{6,7},{8,9},{9,10},{10,11},{12,13},{... | collective-permute-start | bytes 1208 | tf_op jit(solution)/shard_map/ppermute | solution.py:20
  (114 other events, 3538.2 us)
where the time goes:
time: 1100 us; the launch traced here: 1090 us
  blocking collectives  452 us (41%)
  starting transfers between devices  425 us (39%)
  waiting for transfers between devices  152 us (14%)
  local copies, waits for them, and re-layouts  38.5 us (4%)
  other arithmetic  20.1 us (2%)
    psum x4, blocking collectives, global_dot(): lax.psum(jnp.sum(first * second, axis=(-3, -2, -1), keepdims=True), ('rea...  452 us
    ppermute x69, starting transfers between devices, extended(): lax.ppermute(lax.slice_in_dim(block, block.shape[dim] - width, None, axis...  302 us
    ppermute x69, waiting for transfers between devices, extended(): lax.ppermute(lax.slice_in_dim(block, 0, width, axis=dim), axis, backward)  131 us
    ppermute x69, starting transfers between devices, extended(): lax.ppermute(lax.slice_in_dim(block, 0, width, axis=dim), axis, backward)  123 us
  transfers between devices with their start and end apart: 138, of which 63 were waited for; matrix products, arithmetic and copies ran while one was open for 3% of the time, Pallas kernels for 0%

commit v1 on v0

v1 whole, which is shorter than its diff:
```python
import jax
import jax.numpy as jnp
from jax import lax
from jax.experimental import pallas as pl
from jax.experimental.pallas import tpu as pltpu
from jax.sharding import Mesh
from jax.sharding import PartitionSpec as P

EMIN = 0.01
BETA = 8.0
OMEGA = 0.6
ETAS = (0.7, 0.5, 0.3)
NBX = 64
VMEM_LIMIT = 48 * 1024 * 1024
F32 = jnp.float32
HI = lax.Precision.HIGHEST


def call(body, out_shape, scratch=(), flops=1000000):
    return pl.pallas_call(
        body,
        out_shape=out_shape,
        scratch_shapes=list(scratch),
        compiler_params=pltpu.CompilerParams(vmem_limit_bytes=VMEM_LIMIT),
        cost_estimate=pl.CostEstimate(flops=flops, bytes_accessed=1000000, transcendentals=0),
    )


def shaped(*dims):
    return jax.ShapeDtypeStruct(dims, F32)


def rolled(v, amount, axis):
    return pltpu.roll(v, amount % v.shape[axis], axis)


def iota(shape, axis):
    return lax.broadcasted_iota(jnp.int32, shape, axis)


def pool_matrix():
    return (iota((256, 128), 0) // 2 == iota((256, 128), 1)).astype(F32)


def widen_matrix():
    return (iota((128, 256), 1) // 2 == iota((128, 256), 0)).astype(F32)


def y_edges(rows, stride):
    y = iota((rows, 1), 0)
    low = (y >= stride).astype(F32)
    outer = 0.5 * ((y < stride).astype(F32) + (y >= rows - stride).astype(F32))
    return low, outer


def face_y(e, low, stride):
    return 0.5 * low * (e + rolled(e, stride, e.ndim - 2))


def face_z(e, stride):
    return 0.5 * (e + rolled(e, stride, e.ndim - 1))


def through(c, u, stride, axis):
    flow = c * (u - rolled(u, stride, axis))
    return flow - rolled(flow, -stride, axis)


def operate(prev, u, after, cx, cx_after, cy, cz, side, stride):
    n = u.ndim
    total = cx * (u - prev) - cx_after * (after - u)
    total = total + through(cy, u, stride, n - 2) + through(cz, u, stride, n - 1)
    return total + side * u


def inverse(e, diag):
    return jnp.where(e > 0.0, 1.0 / jnp.where(e > 0.0, diag, 1.0), 0.0)


def prepare(e_ref, cx_ref, cy_ref, cz_ref, inv_ref, first, last):
    low, outer = y_edges(16, 1)

    def step(i, _):
        for r in range(3):
            e = e_ref[r, i]
            cx = 0.5 * (e + e_ref[r, i - 1])
            cx_after = 0.5 * (e + e_ref[r, i + 1])
            cy = face_y(e, low, 1)
            cz = face_z(e, 1)
            diag = cx + cx_after + (cy + rolled(cy, -1, 0)) + (cz + rolled(cz, -1, 1)) + outer * e
            cx_ref[r, i] = cx
            cy_ref[r, i] = cy
            cz_ref[r, i] = cz
            inv_ref[r, i] = inverse(e, diag)
        return 0

    lax.fori_loop(first, last, step, 0)
    for r in range(3):
        cx_ref[r, last] = 0.5 * (e_ref[r, last] + e_ref[r, last - 1])


def operate0(u_ref, i, r, e_ref, cx_ref, cy_ref, cz_ref, outer):
    return operate(
        u_ref[r, i - 1], u_ref[r, i], u_ref[r, i + 1],
        cx_ref[r, i], cx_ref[r, i + 1], cy_ref[r, i], cz_ref[r, i], outer * e_ref[r, i], 1,
    )


def pool_own(src_of, many, big_ref, half_ref, scale):
    for f in range(many):
        for k in range(4):
            at = (f * 4 + k) * 16
            big_ref[at : at + 16, :] = (0.125 * scale) * (src_of(f, 8 + 2 * k) + src_of(f, 9 + 2 * k))
    rows = many * 64
    half_ref[0:rows, :] = jnp.dot(big_ref[0:rows, :], pool_matrix(), precision=HI, preferred_element_type=F32)
    return half_ref[pl.ds(0, rows // 2, stride=2), :] + half_ref[pl.ds(1, rows // 2, stride=2), :]


def stack_level(e, stride):
    low, outer = y_edges(8, stride)
    before = jnp.concatenate([e[:1], e[:-1]], 0)
    cx = 0.5 * (e + before)
    cx_after = jnp.concatenate([cx[1:], cx[:1]], 0)
    cy = face_y(e, low[None], stride)
    cz = face_z(e, stride)
    side = outer[None] * e
    diag = cx + cx_after + (cy + rolled(cy, -stride, 1)) + (cz + rolled(cz, -stride, 2)) + side
    return cx, cx_after, cy, cz, side, inverse(e, diag)


def stack_operate(level, u, stride):
    cx, cx_after, cy, cz, side, _ = level
    before = jnp.concatenate([u[:1], u[:-1]], 0)
    after = jnp.concatenate([u[1:], u[-1:]], 0)
    return operate(before, u, after, cx, cx_after, cy, cz, side, stride)


def stack_pool(v, stride):
    n = v.shape[0] // 2
    v = v.reshape(n, 2, 8, 128)
    v = v[:, 0] + v[:, 1]
    y = iota((1, 8, 1), 1)
    v = v + jnp.where((y // stride) % 2 == 0, rolled(v, -stride, 1), rolled(v, stride, 1))
    z = iota((1, 1, 128), 2)
    v = v + jnp.where((z // stride) % 2 == 0, rolled(v, -stride, 2), rolled(v, stride, 2))
    return 0.125 * v


def twice(v):
    n = v.shape[0]
    return jnp.broadcast_to(v[:, None], (n, 2, 8, 128)).reshape(2 * n, 8, 128)


def coarse(e1, rhs1):
    e2 = 0.25 * stack_pool(e1, 1)
    e3 = 0.25 * stack_pool(e2, 2)
    one, two, three = stack_level(e1, 1), stack_level(e2, 2), stack_level(e3, 4)
    x1 = OMEGA * rhs1 * one[5]
    rhs2 = stack_pool(rhs1 - stack_operate(one, x1, 1), 1)
    x2 = OMEGA * rhs2 * two[5]
    rhs3 = stack_pool(rhs2 - stack_operate(two, x2, 2), 2)
    x3 = OMEGA * rhs3 * three[5]
    x3 = x3 + OMEGA * (rhs3 - stack_operate(three, x3, 4)) * three[5]
    x2 = x2 + twice(x3)
    x2 = x2 + OMEGA * (rhs2 - stack_operate(two, x2, 2)) * two[5]
    x1 = x1 + twice(x2)
    return x1 + OMEGA * (rhs1 - stack_operate(one, x1, 1)) * one[5]


def coarse_all(e1_ref, rhs1_ref, out_ref):
    def step(r, _):
        out_ref[r] = coarse(e1_ref[r], rhs1_ref[r])
        return 0

    lax.fori_loop(0, 3, step, 0)


def widen_into(e1_ref, first, count, wide_ref):
    rows = 3 * count * 8
    src = jnp.concatenate([e1_ref[r, first : first + count].reshape(count * 8, 128) for r in range(3)], 0)
    wide = jnp.dot(src, widen_matrix(), precision=HI, preferred_element_type=F32)
    for h in range(2):
        part = wide[:, 128 * h : 128 * h + 128]
        wide_ref[h, pl.ds(0, rows, stride=2), :] = part
        wide_ref[h, pl.ds(1, rows, stride=2), :] = part


def widened(wide_ref, r, k, count):
    at = pl.multiple_of((r * count + k) * 16, 16)
    return jnp.concatenate([wide_ref[0, pl.ds(at, 16), :], wide_ref[1, pl.ds(at, 16), :]], 1)


REACH = (7, 6, 6, 5)
OFFS = (0, 7, 13, 19)


def select_kernel(c_ref, l_ref, r_ref, own_ref, up_ref, down_ref):
    right = iota((8, 128), 1) < 64
    for f in range(4):
        for i in range(8):
            for h in range(2):
                halo = jnp.where(right, r_ref[h, f, i], l_ref[h, f, i])
                piece = jnp.concatenate([c_ref[h, f, i], halo], 1)
                own_ref[f, i, 8 * h : 8 * h + 8, :] = piece
                if i >= 8 - REACH[f]:
                    up_ref[OFFS[f] + i - (8 - REACH[f]), 8 * h : 8 * h + 8, :] = piece
                if i < REACH[f]:
                    down_ref[OFFS[f] + i, 8 * h : 8 * h + 8, :] = piece


def first_kernel(
    place_ref, own_ref, lo_ref, hi_ref, e_ref, f_ref, load_ref, g_ref,
    d_ref, v_ref, s_ref, cx_ref, cy_ref, cz_ref, inv_ref, x_ref, rest_ref, big_ref, half_ref,
):
    block, gy = place_ref[0], place_ref[1]
    for f, ref in enumerate((d_ref, v_ref, s_ref, load_ref)):
        n = REACH[f]
        for j in range(n):
            ref[8 - n + j] = lo_ref[OFFS[f] + j]
            ref[16 + j] = hi_ref[OFFS[f] + j]
        for j in range(8):
            ref[8 + j] = own_ref[f, j]
    lane = iota((1, 256), 1)
    z = gy * 128 + jnp.where(lane < 192, lane, lane - 256)
    z_in = ((z >= 0) & (z < 512)).astype(F32)
    z_count = ((z >= 1) & (z < 513)).astype(F32) + ((z >= -1) & (z < 511)).astype(F32)
    y = iota((16, 1), 0)
    low, high = (y >= 1).astype(F32), (y < 15).astype(F32)
    yz_count = (low + high) + z_count
    shifts = [(jnp.tanh(jnp.full((1, 1), BETA * eta, F32)), jnp.tanh(jnp.full((1, 1), BETA * (1.0 - eta), F32))) for eta in ETAS]

    def step(i, _):
        x = 8 * block + i - 8
        inside = lambda at: ((at >= 0) & (at < 8 * NBX)).astype(F32)
        d = d_ref[i]
        total = 2.0 * d + d_ref[i + 1] + d_ref[i - 1]
        total = total + low * rolled(d, 1, 0) + high * rolled(d, -1, 0) + rolled(d, 1, 1) + rolled(d, -1, 1)
        weights = yz_count + (2.0 + inside(x - 1) + inside(x + 1))
        here = z_in * inside(x)
        filtered = total / weights
        void, solid = v_ref[i], s_ref[i]
        open_ = 1.0 - void
        free = open_ * (1.0 - solid)
        scale = here * free / weights
        for r, eta in enumerate(ETAS):
            t0, t1 = shifts[r]
            den = t0 + t1
            t = jnp.tanh(BETA * (filtered - eta))
            projected = (t0 + t) / den
            slope = BETA * (1.0 - t * t) / den
            physical = open_ * (solid + (1.0 - solid) * projected)
            square = physical * physical
            e_ref[r, i] = here * (EMIN + (1.0 - EMIN) * (square * physical))
            f_ref[r, i] = (3.0 * (1.0 - EMIN)) * square * scale * slope
        return 0

    lax.fori_loop(2, 22, step, 0)
    prepare(e_ref, cx_ref, cy_ref, cz_ref, inv_ref, 7, 17)

    def start(i, _):
        for r in range(3):
            x_ref[r, i] = OMEGA * load_ref[i] * inv_ref[r, i]
        return 0

    lax.fori_loop(7, 17, start, 0)
    _, outer = y_edges(16, 1)

    def leftover(i, _):
        for r in range(3):
            rest_ref[r, i - 8] = load_ref[i] - operate0(x_ref, i, r, e_ref, cx_ref, cy_ref, cz_ref, outer)
        return 0

    lax.fori_loop(8, 16, leftover, 0)
    g_ref[0:3] = pool_own(lambda f, i: rest_ref[f, i - 8], 3, big_ref, half_ref, 1.0).reshape(3, 4, 8, 128)
    g_ref[3:6] = pool_own(lambda f, i: e_ref[f, i], 3, big_ref, half_ref, 0.25).reshape(3, 4, 8, 128)


def triple_kernel(lo_ref, c_ref, hi_ref, out_ref):
    out_ref[0] = lo_ref[...]
    out_ref[1] = c_ref[...]
    out_ref[2] = hi_ref[...]


def window(refs, block, first, into_ref, index):
    for b in range(9):
        at = block - 4 + b
        keep = ((at >= 0) & (at < NBX)).astype(F32)
        for r in range(3):
            into_ref[r, 4 * b : 4 * b + 4] = keep * refs[b // 3][b % 3, first + r]


def second_kernel(
    place_ref, e_ref, load_ref, lo_ref, c_ref, hi_ref, e1_ref, z0_ref, q0_ref, g_ref,
    cx_ref, cy_ref, cz_ref, inv_ref, x_ref, y_ref, rhs_ref, out1_ref, wide_ref, big_ref, half_ref,
):
    block = place_ref[0]
    refs = (lo_ref, c_ref, hi_ref)
    window(refs, block, 0, rhs_ref, 0)
    window(refs, block, 3, e1_ref, 0)
    prepare(e_ref, cx_ref, cy_ref, cz_ref, inv_ref, 3, 21)
    coarse_all(e1_ref, rhs_ref, out1_ref)
    widen_into(out1_ref, 13, 10, wide_ref)
    _, outer = y_edges(16, 1)

    def start(i, _):
        for r in range(3):
            x_ref[r, i] = OMEGA * load_ref[i] * inv_ref[r, i] + widened(wide_ref, r, (i - 2) // 2, 10)
        return 0

    lax.fori_loop(3, 21, start, 0)

    def smooth(i, _):
        for r in range(3):
            image = operate0(x_ref, i, r, e_ref, cx_ref, cy_ref, cz_ref, outer)
            z0_ref[r, i] = x_ref[r, i] + OMEGA * (load_ref[i] - image) * inv_ref[r, i]
        return 0

    lax.fori_loop(4, 20, smooth, 0)

    def apply(i, _):
        for r in range(3):
            image = operate0(z0_ref, i, r, e_ref, cx_ref, cy_ref, cz_ref, outer)
            q0_ref[r, i] = image
            y_ref[r, i] = OMEGA * image * inv_ref[r, i]
        return 0

    lax.fori_loop(5, 19, apply, 0)

    def leftover(i, _):
        for r in range(3):
            x_ref[r, i] = q0_ref[r, i] - operate0(y_ref, i, r, e_ref, cx_ref, cy_ref, cz_ref, outer)
        return 0

    lax.fori_loop(8, 16, leftover, 0)
    g_ref[...] = pool_own(lambda f, i: x_ref[f, i], 3, big_ref, half_ref, 1.0).reshape(3, 4, 8, 128)


def third_kernel(
    place_ref, e_ref, load_ref, e1_ref, z0_ref, q0_ref, lo_ref, c_ref, hi_ref, w_ref, dots_ref,
    cx_ref, cy_ref, cz_ref, inv_ref, x_ref, rhs_ref, out1_ref, wide_ref,
):
    block = place_ref[0]
    window((lo_ref, c_ref, hi_ref), block, 0, rhs_ref, 0)
    prepare(e_ref, cx_ref, cy_ref, cz_ref, inv_ref, 5, 19)
    coarse_all(e1_ref, rhs_ref, out1_ref)
    widen_into(out1_ref, 14, 8, wide_ref)
    _, outer = y_edges(16, 1)

    def start(i, _):
        for r in range(3):
            x_ref[r, i] = OMEGA * q0_ref[r, i] * inv_ref[r, i] + widened(wide_ref, r, (i - 4) // 2, 8)
        return 0

    lax.fori_loop(5, 19, start, 0)

    def smooth(i, _):
        for r in range(3):
            image = operate0(x_ref, i, r, e_ref, cx_ref, cy_ref, cz_ref, outer)
            w_ref[r, i] = x_ref[r, i] + OMEGA * (q0_ref[r, i] - image) * inv_ref[r, i]
        return 0

    lax.fori_loop(6, 18, smooth, 0)

    def add(i, sums):
        new = []
        for r in range(3):
            image = operate0(w_ref, i, r, e_ref, cx_ref, cy_ref, cz_ref, outer)[:, :128]
            b, z0, q0, w = load_ref[i, :, :128], z0_ref[r, i, :, :128], q0_ref[r, i, :, :128], w_ref[r, i, :, :128]
            for q, term in enumerate((b * z0, z0 * q0, b * w, q0 * w, w * image)):
                new.append(sums[r * 5 + q] + (term[:8] + term[8:]))
        return tuple(new)

    sums = lax.fori_loop(8, 16, add, tuple(jnp.zeros((8, 128), F32) for _ in range(15)))
    rows = [jnp.sum(v, 0, keepdims=True) for v in sums] + [jnp.zeros((1, 128), F32)]
    tile = jnp.concatenate(rows, 0)
    for d in range(16):
        dots_ref[d] = tile


def sum_kernel(in_ref, out_ref):
    tile = jnp.sum(in_ref[...], 0)
    for d in range(16):
        out_ref[d] = tile


def last_kernel(place_ref, f_ref, z0_ref, w_ref, dots_ref, sens_ref, comp_ref, u_ref, comb_ref):
    real = place_ref[2]
    totals = jnp.sum(jnp.sum(dots_ref[...], 0), 1, keepdims=True)
    factors = []
    for r in range(3):
        bz, zq, bw, qw, wa = (totals[r * 5 + q : r * 5 + q + 1] for q in range(5))
        a0 = bz / zq
        rz1 = bz - a0 * bw - a0 * zq + (a0 * a0) * qw
        grow = 1.0 + rz1 / bz
        a1 = rz1 / ((grow * grow) * zq - 2.0 * (a0 * grow) * qw + (a0 * a0) * wa)
        c0, c1 = a0 + a1 * grow, -(a1 * a0)
        factors.append((c0, c1))
        comp_ref[r : r + 1, :] = jnp.broadcast_to(c0 * bz + c1 * bw, (1, 128))
    comp_ref[3:8, :] = jnp.zeros((5, 128), F32)
    y = iota((16, 1), 0)
    low, high = (y >= 1).astype(F32), (y < 15).astype(F32)

    def state(i, _):
        for r in range(3):
            u_ref[r, i] = factors[r][0] * z0_ref[r, i] + factors[r][1] * w_ref[r, i]
        return 0

    lax.fori_loop(6, 18, state, 0)

    def energy(i, _):
        total = jnp.zeros((16, 256), F32)
        for r in range(3):
            u = u_ref[r, i]
            gaps = (
                u - u_ref[r, i - 1],
                u - u_ref[r, i + 1],
                u - low * rolled(u, 1, 0),
                u - high * rolled(u, -1, 0),
                u - rolled(u, 1, 1),
                u - rolled(u, -1, 1),
            )
            square = gaps[0] * gaps[0]
            for gap in gaps[1:]:
                square = square + gap * gap
            total = total - (0.5 * square) * f_ref[r, i]
        comb_ref[i] = total
        return 0

    lax.fori_loop(7, 17, energy, 0)

    def spread(i, _):
        c = comb_ref[i]
        total = 2.0 * c + comb_ref[i + 1] + comb_ref[i - 1]
        total = total + low * rolled(c, 1, 0) + high * rolled(c, -1, 0) + rolled(c, 1, 1) + rolled(c, -1, 1)
        sens_ref[i - 8] = jnp.where(real == 0, total[:8, :128], total[8:, :128])
        return 0

    lax.fori_loop(8, 16, spread, 0)


def kernel_call(body, outs, scratch, place, *args, flops=1000000):
    return pl.pallas_call(
        body,
        out_shape=outs,
        in_specs=[pl.BlockSpec(memory_space=pltpu.SMEM)] + [pl.BlockSpec(memory_space=pltpu.VMEM)] * len(args),
        scratch_shapes=[pltpu.VMEM(dims, F32) for dims in scratch],
        compiler_params=pltpu.CompilerParams(vmem_limit_bytes=VMEM_LIMIT),
    )(place, *args)


X_AXES = ("zc", "xc")
Y_AXES = ("yl", "core")
FIELD = (3, 24, 16, 256)
LEVEL1 = (3, 36, 8, 128)


def neighbours(count, step, wrap):
    return [(i, (i + step) % count) for i in range(count) if wrap or 0 <= i + step < count]


def reach(own):
    lo = lax.ppermute(own, X_AXES, neighbours(NBX, 1, True))
    hi = lax.ppermute(own, X_AXES, neighbours(NBX, -1, True))
    triple = call(triple_kernel, shaped(3, *own.shape))(lo, own, hi)
    return (
        lax.ppermute(triple, X_AXES, neighbours(NBX, 3, True)),
        triple,
        lax.ppermute(triple, X_AXES, neighbours(NBX, -3, True)),
    )


def body(design, load, void_mask, solid_mask):
    place = jnp.stack([lax.axis_index(X_AXES), lax.axis_index(Y_AXES), lax.axis_index("real")]).astype(jnp.int32)
    own = jnp.stack([design, void_mask.astype(F32), solid_mask.astype(F32), load])
    both = lax.all_gather(own, "real")
    left = lax.ppermute(both, Y_AXES, neighbours(4, 1, False))
    right = lax.ppermute(both, Y_AXES, neighbours(4, -1, False))
    mine, up, down = call(select_kernel, (shaped(4, 8, 16, 256), shaped(24, 16, 256), shaped(24, 16, 256)))(both, left, right)
    lo = lax.ppermute(up, X_AXES, neighbours(NBX, 1, False))
    hi = lax.ppermute(down, X_AXES, neighbours(NBX, -1, False))
    one = (24, 16, 256)
    e, f, wide_load, g = kernel_call(
        first_kernel,
        (shaped(*FIELD), shaped(*FIELD), shaped(*one), shaped(6, 4, 8, 128)),
        [one] * 3 + [FIELD] * 5 + [(3, 8, 16, 256), (192, 256), (192, 128)],
        place, mine, lo, hi,
    )
    e1, z0, q0, g2 = kernel_call(
        second_kernel,
        (shaped(*LEVEL1), shaped(*FIELD), shaped(*FIELD), shaped(3, 4, 8, 128)),
        [FIELD] * 6 + [LEVEL1] * 2 + [(2, 480, 128), (192, 256), (192, 128)],
        place, e, wide_load, *reach(g),
    )
    w, dots = kernel_call(
        third_kernel,
        (shaped(*FIELD), shaped(16, 16, 128)),
        [FIELD] * 5 + [LEVEL1] * 2 + [(2, 384, 128)],
        place, e, wide_load, e1, z0, q0, *reach(g2),
    )
    dots = lax.all_to_all(dots, ("xc", "yl", "core"), 0, 0, tiled=True)
    dots = call(sum_kernel, shaped(16, 16, 128))(dots)
    dots = lax.all_to_all(dots, "zc", 0, 0, tiled=True)
    sens, comp = kernel_call(
        last_kernel,
        (shaped(8, 8, 128), shaped(8, 128)),
        [FIELD, one],
        place, f, z0, w, dots,
    )
    return sens, comp[:3, 0]


def solution(mesh):
    split = Mesh(mesh.devices.reshape(2, 16, 4, 2, 2), ("real", "zc", "xc", "yl", "core"))
    spec = P(X_AXES, "real", Y_AXES)
    return jax.shard_map(body, mesh=split, in_specs=(spec,) * 4, out_specs=(spec, P()), check_vma=False)
```

time: 1100 us -> 164 us (0.15)
  blocking collectives: 452 us -> 40.8 us
  starting transfers between devices: 425 us -> 44.9 us
  waiting for transfers between devices: 152 us -> 38.3 us
  local copies, waits for them, and re-layouts: 38.5 us -> 0.63 us
  Pallas kernels: 0 us -> 35 us
  other arithmetic: 20.1 us -> 1.64 us
    psum x4 -> x0, blocking collectives: 452 us -> none  [global_dot(): lax.psum(jnp.sum(first * second, axis=(-3, -2, -1), keepdims=True), ('rea...]
    ppermute x138 -> x12, starting transfers between devices: 425 us -> 44.9 us  [the longest x2 14.3 us: reach(): hi = lax.ppermute(own, X_AXES, neighbours(NBX, -1, True))]
    ppermute x138 -> x12, waiting for transfers between devices: 152 us -> 38.3 us  [the longest x2 13 us: reach(): lo = lax.ppermute(own, X_AXES, neighbours(NBX, 1, True))]
    pallas_call x0 -> x8, Pallas kernels: none -> 35 us  [the longest x4 34.9 us: kernel_call(): pl.pallas_call(body, out_shape=outs, in_specs=[pl.BlockSpec(memory_space=...]
    all_to_all x0 -> x2, blocking collectives: none -> 34 us  [the longest x1 19.9 us: body(): dots = lax.all_to_all(dots, 'zc', 0, 0, tiled=True)]
    reshape x12 -> x0, local copies, waits for them, and re-layouts: 19.2 us -> none  [the longest x4 17 us: pool(): values.reshape(lead + (shape_now[-3] // span, span, shape_now[-2] // span...]
  transfers between devices with their start and end apart: 138 -> 12, of which waited for: 63 -> 9; matrix products, arithmetic and copies ran while one was open for 3% -> 0% of each run, Pallas kernels for 0% -> 0%
where the time goes in v1:
time: 164 us; the launch traced here: 162 us
  starting transfers between devices  44.9 us (27%)
  blocking collectives  40.8 us (25%)
  waiting for transfers between devices  38.3 us (23%)
  Pallas kernels  35 us (21%)
    pallas_call x4, Pallas kernels, kernel_call(): pl.pallas_call(body, out_shape=outs, in_specs=[pl.BlockSpec(memory_space=...  34.9 us
    all_to_all x1, blocking collectives, body(): dots = lax.all_to_all(dots, 'zc', 0, 0, tiled=True)  19.9 us
    ppermute x2, starting transfers between devices, reach(): hi = lax.ppermute(own, X_AXES, neighbours(NBX, -1, True))  14.3 us
    all_to_all x1, blocking collectives, body(): dots = lax.all_to_all(dots, ('xc', 'yl', 'core'), 0, 0, tiled=True)  14.1 us
    ppermute x2, waiting for transfers between devices, reach(): lo = lax.ppermute(own, X_AXES, neighbours(NBX, 1, True))  13 us
    ppermute x1, starting transfers between devices, body(): right = lax.ppermute(both, Y_AXES, neighbours(4, -1, False))  9.17 us
    ppermute x2, starting transfers between devices, reach(): lax.ppermute(triple, X_AXES, neighbours(NBX, 3, True))  8.8 us
    all_gather x1, blocking collectives, body(): both = lax.all_gather(own, 'real')  6.76 us
  transfers between devices with their start and end apart: 12, of which 9 were waited for; matrix products, arithmetic and copies ran while one was open for 0% of the time, Pallas kernels for 0%

profile of v1, /device:TPU:1, one launch (start us, length us, event | category | flops | bytes accessed | tf_op | source)
XLA Modules:
  0.0 162.0 jit_solution(12051273154760988382)
XLA Ops:
  0.6 0.8 convert_bitcast_fusion
  1.4 0.8 pad_maximum_fusion
  2.2 6.8 %all-gather = f32[8,8,8,128]{3,2,1,0:T(8,128)S(1)} all-gather(f32[4,8,8,128]{3,2,1,0:T(8,128)S(1)} %pad_maximum_fusion), channel_id=2, replica_groups=mesh['real'=2,'zc'=16,'xc'=4,'yl'=2,'core'=2] {'real'}, dimensions={0}, use_global_device_ids=true | all-gather | bytes 393216 | tf_op jit(solution)/shard_map/all_gather | solution.py:475
  9.0 9.2 %collective-permute-start.1 = (f32[2,4,8,8,128]{4,3,2,1,0:T(8,128)S(1)}, f32[2,4,8,8,128]{4,3,2,1,0:T(8,128)S(1)}, u32[]{:S(2)}, u32[]{:S(2)}) collective-permute-start(f32[2,4,8,8,128]{4,3,2,1,0:T(8,128)S(1)} %bitcast.10), channel_id=1, source_target_pairs={{1,0},{2,1},{3,2},{5,4},{6,5},{7,6},{9,8},{10,9},{11,10},{13,12},{... | collective-permute-start | bytes 786440 | tf_op jit(solution)/shard_map/ppermute | solution.py:477
  18.1 1.9 %collective-permute-start = (f32[2,4,8,8,128]{4,3,2,1,0:T(8,128)S(1)}, f32[2,4,8,8,128]{4,3,2,1,0:T(8,128)S(1)}, u32[]{:S(2)}, u32[]{:S(2)}) collective-permute-start(f32[2,4,8,8,128]{4,3,2,1,0:T(8,128)S(1)} %bitcast.11), channel_id=1, source_target_pairs={{0,1},{1,2},{2,3},{4,5},{5,6},{6,7},{8,9},{9,10},{10,11},{12,13},{... | collective-permute-start | bytes 786440 | tf_op jit(solution)/shard_map/ppermute | solution.py:476
  20.1 0.0 collective-permute-done.1.r_ref
  20.1 3.3 %collective-permute-done.l_ref = f32[2,4,8,8,128]{4,3,2,1,0:T(8,128)S(1)} collective-permute-done((f32[2,4,8,8,128]{4,3,2,1,0:T(8,128)S(1)}, f32[2,4,8,8,128]{4,3,2,1,0:T(8,128)S(1)}, u32[]{:S(2)}, u32[]{:S(2)}) %collective-permute-start) | collective-permute-done | bytes 262176 | tf_op jit(solution)/shard_map/ppermute | solution.py:476
  23.4 0.1 shard_map.59
  23.4 1.3 collective-permute-start.2
  24.8 1.3 collective-permute-start.3
  26.1 0.1 pad_add_fusion.place_ref
  26.2 6.0 %collective-permute-done.2.lo_ref = f32[24,16,256]{2,1,0:T(8,128)S(1)} collective-permute-done((f32[24,16,256]{2,1,0:T(8,128)S(1)}, f32[24,16,256]{2,1,0:T(8,128)S(1)}, u32[]{:S(2)}, u32[]{:S(2)}) %collective-permute-start.2) | collective-permute-done | bytes 393248 | tf_op jit(solution)/shard_map/ppermute | solution.py:479
  32.2 4.1 %collective-permute-done.3.hi_ref = f32[24,16,256]{2,1,0:T(8,128)S(1)} collective-permute-done((f32[24,16,256]{2,1,0:T(8,128)S(1)}, f32[24,16,256]{2,1,0:T(8,128)S(1)}, u32[]{:S(2)}, u32[]{:S(2)}) %collective-permute-start.3) | collective-permute-done | bytes 393248 | tf_op jit(solution)/shard_map/ppermute | solution.py:480
  36.3 6.5 %shard_map.60 = (f32[3,24,16,256]{3,2,1,0:T(8,128)S(1)}, f32[3,24,16,256]{3,2,1,0:T(8,128)S(1)}, f32[24,16,256]{2,1,0:T(8,128)S(1)}, f32[6,4,8,128]{3,2,1,0:T(8,128)S(1)}) custom-call(s32[3]{0:T(128)S(1)} %pad_add_fusion.place_ref, f32[4,8,16,256]{3,2,1,0:T(8,128)S(1)} %get-tuple-element.17.own_ref, f32[24,16,256]{2,1,0:T(8,128)S(1)} %collective-permute-done.2.lo_ref, ...), custom_call_target="tpu_custom_call" | custom-call | tf_op jit(solution)/shard_map/pallas_call | solution.py:442
  42.8 8.6 %collective-permute-start.5 = (f32[6,4,8,128]{3,2,1,0:T(8,128)S(1)}, f32[6,4,8,128]{3,2,1,0:T(8,128)S(1)}, u32[]{:S(2)}, u32[]{:S(2)}) collective-permute-start(f32[6,4,8,128]{3,2,1,0:T(8,128)S(1)} %get-tuple-element.23.c_ref), channel_id=1, source_target_pairs={{0,252},{4,0},{8,4},{12,8},{16,12},{20,16},{24,20},{28,24},{32,28}... | collective-permute-start | bytes 294920 | tf_op jit(solution)/shard_map/ppermute | solution.py:463
  51.5 1.9 %collective-permute-start.4 = (f32[6,4,8,128]{3,2,1,0:T(8,128)S(1)}, f32[6,4,8,128]{3,2,1,0:T(8,128)S(1)}, u32[]{:S(2)}, u32[]{:S(2)}) collective-permute-start(f32[6,4,8,128]{3,2,1,0:T(8,128)S(1)} %get-tuple-element.23.c_ref), channel_id=1, source_target_pairs={{0,4},{4,8},{8,12},{12,16},{16,20},{20,24},{24,28},{28,32},{32,36}... | collective-permute-start | bytes 294920 | tf_op jit(solution)/shard_map/ppermute | solution.py:462
  53.4 0.0 collective-permute-done.5.hi_ref
  53.4 6.8 %collective-permute-done.4.lo_ref = f32[6,4,8,128]{3,2,1,0:T(8,128)S(1)} collective-permute-done((f32[6,4,8,128]{3,2,1,0:T(8,128)S(1)}, f32[6,4,8,128]{3,2,1,0:T(8,128)S(1)}, u32[]{:S(2)}, u32[]{:S(2)}) %collective-permute-start.4) | collective-permute-done | bytes 98336 | tf_op jit(solution)/shard_map/ppermute | solution.py:462
  60.2 2.3 %collective-permute-start.7 = (f32[3,6,4,8,128]{4,3,2,1,0:T(8,128)S(1)}, f32[3,6,4,8,128]{4,3,2,1,0:T(8,128)S(1)}, u32[]{:S(2)}, u32[]{:S(2)}) collective-permute-start(f32[3,6,4,8,128]{4,3,2,1,0:T(8,128)S(1)} %shard_map.61.c_ref), channel_id=1, source_target_pairs={{0,244},{4,248},{8,252},{12,0},{16,4},{20,8},{24,12},{28,16},{32,2... | collective-permute-start | bytes 884744 | tf_op jit(solution)/shard_map/ppermute | solution.py:468
  62.5 4.2 %collective-permute-start.6 = (f32[3,6,4,8,128]{4,3,2,1,0:T(8,128)S(1)}, f32[3,6,4,8,128]{4,3,2,1,0:T(8,128)S(1)}, u32[]{:S(2)}, u32[]{:S(2)}) collective-permute-start(f32[3,6,4,8,128]{4,3,2,1,0:T(8,128)S(1)} %shard_map.61.c_ref), channel_id=1, source_target_pairs={{0,12},{4,16},{8,20},{12,24},{16,28},{20,32},{24,36},{28,40},{32,4... | collective-permute-start | bytes 884744 | tf_op jit(solution)/shard_map/ppermute | solution.py:466
  66.7 5.5 %collective-permute-done.7.hi_ref = f32[3,6,4,8,128]{4,3,2,1,0:T(8,128)S(1)} collective-permute-done((f32[3,6,4,8,128]{4,3,2,1,0:T(8,128)S(1)}, f32[3,6,4,8,128]{4,3,2,1,0:T(8,128)S(1)}, u32[]{:S(2)}, u32[]{:S(2)}) %collective-permute-start.7) | collective-permute-done | bytes 294944 | tf_op jit(solution)/shard_map/ppermute | solution.py:468
  72.2 3.0 %collective-permute-done.6.lo_ref = f32[3,6,4,8,128]{4,3,2,1,0:T(8,128)S(1)} collective-permute-done((f32[3,6,4,8,128]{4,3,2,1,0:T(8,128)S(1)}, f32[3,6,4,8,128]{4,3,2,1,0:T(8,128)S(1)}, u32[]{:S(2)}, u32[]{:S(2)}) %collective-permute-start.6) | collective-permute-done | bytes 294944 | tf_op jit(solution)/shard_map/ppermute | solution.py:466
  75.2 14.6 %shard_map.62 = (f32[3,36,8,128]{3,2,1,0:T(8,128)S(1)}, f32[3,24,16,256]{3,2,1,0:T(8,128)S(1)}, f32[3,24,16,256]{3,2,1,0:T(8,128)S(1)}, f32[3,4,8,128]{3,2,1,0:T(8,128)S(1)}) custom-call(s32[3]{0:T(128)S(1)} %pad_add_fusion.place_ref, f32[3,24,16,256]{3,2,1,0:T(8,128)S(1)} %get-tuple-element.21.e_ref, f32[24,16,256]{2,1,0:T(8,128)S(1)} %get-tuple-element.22.load_ref, ...), custom_call_target="tpu_custom_call" | custom-call | tf_op jit(solution)/shard_map/pallas_call | solution.py:442
  89.8 5.7 %collective-permute-start.9 = (f32[3,4,8,128]{3,2,1,0:T(8,128)S(1)}, f32[3,4,8,128]{3,2,1,0:T(8,128)S(1)}, u32[]{:S(2)}, u32[]{:S(2)}) collective-permute-start(f32[3,4,8,128]{3,2,1,0:T(8,128)S(1)} %get-tuple-element.27.c_ref), channel_id=1, source_target_pairs={{0,252},{4,0},{8,4},{12,8},{16,12},{20,16},{24,20},{28,24},{32,28}... | collective-permute-start | bytes 147464 | tf_op jit(solution)/shard_map/ppermute | solution.py:463
  95.5 1.9 %collective-permute-start.8 = (f32[3,4,8,128]{3,2,1,0:T(8,128)S(1)}, f32[3,4,8,128]{3,2,1,0:T(8,128)S(1)}, u32[]{:S(2)}, u32[]{:S(2)}) collective-permute-start(f32[3,4,8,128]{3,2,1,0:T(8,128)S(1)} %get-tuple-element.27.c_ref), channel_id=1, source_target_pairs={{0,4},{4,8},{8,12},{12,16},{16,20},{20,24},{24,28},{28,32},{32,36}... | collective-permute-start | bytes 147464 | tf_op jit(solution)/shard_map/ppermute | solution.py:462
  97.4 0.0 collective-permute-done.9.hi_ref
  97.4 6.2 %collective-permute-done.8.lo_ref = f32[3,4,8,128]{3,2,1,0:T(8,128)S(1)} collective-permute-done((f32[3,4,8,128]{3,2,1,0:T(8,128)S(1)}, f32[3,4,8,128]{3,2,1,0:T(8,128)S(1)}, u32[]{:S(2)}, u32[]{:S(2)}) %collective-permute-start.8) | collective-permute-done | bytes 49184 | tf_op jit(solution)/shard_map/ppermute | solution.py:462
  103.6 1.9 %collective-permute-start.11 = (f32[3,3,4,8,128]{4,3,2,1,0:T(8,128)S(1)}, f32[3,3,4,8,128]{4,3,2,1,0:T(8,128)S(1)}, u32[]{:S(2)}, u32[]{:S(2)}) collective-permute-start(f32[3,3,4,8,128]{4,3,2,1,0:T(8,128)S(1)} %shard_map.63.c_ref), channel_id=1, source_target_pairs={{0,244},{4,248},{8,252},{12,0},{16,4},{20,8},{24,12},{28,16},{32,2... | collective-permute-start | bytes 442376 | tf_op jit(solution)/shard_map/ppermute | solution.py:468
  105.6 4.6 %collective-permute-start.10 = (f32[3,3,4,8,128]{4,3,2,1,0:T(8,128)S(1)}, f32[3,3,4,8,128]{4,3,2,1,0:T(8,128)S(1)}, u32[]{:S(2)}, u32[]{:S(2)}) collective-permute-start(f32[3,3,4,8,128]{4,3,2,1,0:T(8,128)S(1)} %shard_map.63.c_ref), channel_id=1, source_target_pairs={{0,12},{4,16},{8,20},{12,24},{16,28},{20,32},{24,36},{28,40},{32,4... | collective-permute-start | bytes 442376 | tf_op jit(solution)/shard_map/ppermute | solution.py:466
  110.1 0.6 collective-permute-done.11.hi_ref
  110.7 2.8 %collective-permute-done.10.lo_ref = f32[3,3,4,8,128]{4,3,2,1,0:T(8,128)S(1)} collective-permute-done((f32[3,3,4,8,128]{4,3,2,1,0:T(8,128)S(1)}, f32[3,3,4,8,128]{4,3,2,1,0:T(8,128)S(1)}, u32[]{:S(2)}, u32[]{:S(2)}) %collective-permute-start.10) | collective-permute-done | bytes 147488 | tf_op jit(solution)/shard_map/ppermute | solution.py:466
  113.6 10.3 %shard_map.64 = (f32[3,24,16,256]{3,2,1,0:T(8,128)S(1)}, f32[16,16,128]{2,1,0:T(8,128)S(1)}) custom-call(s32[3]{0:T(128)S(1)} %pad_add_fusion.place_ref, f32[3,24,16,256]{3,2,1,0:T(8,128)S(1)} %get-tuple-element.21.e_ref, f32[24,16,256]{2,1,0:T(8,128)S(1)} %get-tuple-element.22.load_ref, f32[3,36,8,128]{3,2,1,0:T(8,128)S(1)} %get-tuple-element.25.e1_ref, ...), custom_call_target="tpu_custom_call" | custom-call | tf_op jit(solution)/shard_map/pallas_call | solution.py:442
  123.9 14.1 %all_to_all.10.in_ref = f32[16,16,128]{2,1,0:T(8,128)S(1)} all-to-all(f32[16,16,128]{2,1,0:T(8,128)S(1)} %get-tuple-element.29), channel_id=1, replica_groups=mesh['real'=2,'zc'=16,'xc'=4,'yl'=2,'core'=2] {'xc','yl','core'}, dimensions={0} | all-to-all | bytes 262144 | tf_op jit(solution)/shard_map/all_to_all | solution.py:500
  138.0 19.9 %all_to_all.11.dots_ref = f32[16,16,128]{2,1,0:T(8,128)S(1)} all-to-all(f32[16,16,128]{2,1,0:T(8,128)S(1)} %shard_map.65), channel_id=1, replica_groups=mesh['real'=2,'zc'=16,'xc'=4,'yl'=2,'core'=2] {'zc'}, dimensions={0} | all-to-all | bytes 262144 | tf_op jit(solution)/shard_map/all_to_all | solution.py:502
  157.9 3.5 %shard_map.66 = (f32[8,8,128]{2,1,0:T(8,128)}, f32[8,128]{1,0:T(8,128)S(1)}) custom-call(s32[3]{0:T(128)S(1)} %pad_add_fusion.place_ref, f32[3,24,16,256]{3,2,1,0:T(8,128)S(1)} %get-tuple-element.20.f_ref, f32[3,24,16,256]{3,2,1,0:T(8,128)S(1)} %get-tuple-element.24.z0_ref, f32[3,24,16,256]{3,2,1,0:T(8,128)S(1)} %get-tuple-element.28.w_ref, ...), custom_call_target="tpu_custom_call" | custom-call | tf_op jit(solution)/shard_map/pallas_call | solution.py:442
  161.4 0.6 slice_reduce_fusion
  (3 shorter events, 0.1 us)
Async XLA Ops:
  9.0 11.1 %collective-permute-start.1 = (f32[2,4,8,8,128]{4,3,2,1,0:T(8,128)S(1)}, f32[2,4,8,8,128]{4,3,2,1,0:T(8,128)S(1)}, u32[]{:S(2)}, u32[]{:S(2)}) collective-permute-start(f32[2,4,8,8,128]{4,3,2,1,0:T(8,128)S(1)} %bitcast.10), channel_id=1, source_target_pairs={{1,0},{2,1},{3,2},{5,4},{6,5},{7,6},{9,8},{10,9},{11,10},{13,12},{... | collective-permute-start | bytes 786440 | tf_op jit(solution)/shard_map/ppermute | solution.py:477
  18.1 5.2 %collective-permute-start = (f32[2,4,8,8,128]{4,3,2,1,0:T(8,128)S(1)}, f32[2,4,8,8,128]{4,3,2,1,0:T(8,128)S(1)}, u32[]{:S(2)}, u32[]{:S(2)}) collective-permute-start(f32[2,4,8,8,128]{4,3,2,1,0:T(8,128)S(1)} %bitcast.11), channel_id=1, source_target_pairs={{0,1},{1,2},{2,3},{4,5},{5,6},{6,7},{8,9},{9,10},{10,11},{12,13},{... | collective-permute-start | bytes 786440 | tf_op jit(solution)/shard_map/ppermute | solution.py:476
  23.4 8.7 %collective-permute-start.2 = (f32[24,16,256]{2,1,0:T(8,128)S(1)}, f32[24,16,256]{2,1,0:T(8,128)S(1)}, u32[]{:S(2)}, u32[]{:S(2)}) collective-permute-start(f32[24,16,256]{2,1,0:T(8,128)S(1)} %get-tuple-element.18), channel_id=1, source_target_pairs={{0,4},{4,8},{8,12},{12,16},{16,20},{20,24},{24,28},{28,32},{32,36}... | collective-permute-start | bytes 1179656 | tf_op jit(solution)/shard_map/ppermute | solution.py:479
  24.8 11.5 %collective-permute-start.3 = (f32[24,16,256]{2,1,0:T(8,128)S(1)}, f32[24,16,256]{2,1,0:T(8,128)S(1)}, u32[]{:S(2)}, u32[]{:S(2)}) collective-permute-start(f32[24,16,256]{2,1,0:T(8,128)S(1)} %get-tuple-element.19), channel_id=1, source_target_pairs={{4,0},{8,4},{12,8},{16,12},{20,16},{24,20},{28,24},{32,28},{36,32}... | collective-permute-start | bytes 1179656 | tf_op jit(solution)/shard_map/ppermute | solution.py:480
  42.8 10.6 %collective-permute-start.5 = (f32[6,4,8,128]{3,2,1,0:T(8,128)S(1)}, f32[6,4,8,128]{3,2,1,0:T(8,128)S(1)}, u32[]{:S(2)}, u32[]{:S(2)}) collective-permute-start(f32[6,4,8,128]{3,2,1,0:T(8,128)S(1)} %get-tuple-element.23.c_ref), channel_id=1, source_target_pairs={{0,252},{4,0},{8,4},{12,8},{16,12},{20,16},{24,20},{28,24},{32,28}... | collective-permute-start | bytes 294920 | tf_op jit(solution)/shard_map/ppermute | solution.py:463
  51.5 8.7 %collective-permute-start.4 = (f32[6,4,8,128]{3,2,1,0:T(8,128)S(1)}, f32[6,4,8,128]{3,2,1,0:T(8,128)S(1)}, u32[]{:S(2)}, u32[]{:S(2)}) collective-permute-start(f32[6,4,8,128]{3,2,1,0:T(8,128)S(1)} %get-tuple-element.23.c_ref), channel_id=1, source_target_pairs={{0,4},{4,8},{8,12},{12,16},{16,20},{20,24},{24,28},{28,32},{32,36}... | collective-permute-start | bytes 294920 | tf_op jit(solution)/shard_map/ppermute | solution.py:462
  60.2 12.0 %collective-permute-start.7 = (f32[3,6,4,8,128]{4,3,2,1,0:T(8,128)S(1)}, f32[3,6,4,8,128]{4,3,2,1,0:T(8,128)S(1)}, u32[]{:S(2)}, u32[]{:S(2)}) collective-permute-start(f32[3,6,4,8,128]{4,3,2,1,0:T(8,128)S(1)} %shard_map.61.c_ref), channel_id=1, source_target_pairs={{0,244},{4,248},{8,252},{12,0},{16,4},{20,8},{24,12},{28,16},{32,2... | collective-permute-start | bytes 884744 | tf_op jit(solution)/shard_map/ppermute | solution.py:468
  62.5 12.7 %collective-permute-start.6 = (f32[3,6,4,8,128]{4,3,2,1,0:T(8,128)S(1)}, f32[3,6,4,8,128]{4,3,2,1,0:T(8,128)S(1)}, u32[]{:S(2)}, u32[]{:S(2)}) collective-permute-start(f32[3,6,4,8,128]{4,3,2,1,0:T(8,128)S(1)} %shard_map.61.c_ref), channel_id=1, source_target_pairs={{0,12},{4,16},{8,20},{12,24},{16,28},{20,32},{24,36},{28,40},{32,4... | collective-permute-start | bytes 884744 | tf_op jit(solution)/shard_map/ppermute | solution.py:466
  89.8 7.6 %collective-permute-start.9 = (f32[3,4,8,128]{3,2,1,0:T(8,128)S(1)}, f32[3,4,8,128]{3,2,1,0:T(8,128)S(1)}, u32[]{:S(2)}, u32[]{:S(2)}) collective-permute-start(f32[3,4,8,128]{3,2,1,0:T(8,128)S(1)} %get-tuple-element.27.c_ref), channel_id=1, source_target_pairs={{0,252},{4,0},{8,4},{12,8},{16,12},{20,16},{24,20},{28,24},{32,28}... | collective-permute-start | bytes 147464 | tf_op jit(solution)/shard_map/ppermute | solution.py:463
  95.5 8.2 %collective-permute-start.8 = (f32[3,4,8,128]{3,2,1,0:T(8,128)S(1)}, f32[3,4,8,128]{3,2,1,0:T(8,128)S(1)}, u32[]{:S(2)}, u32[]{:S(2)}) collective-permute-start(f32[3,4,8,128]{3,2,1,0:T(8,128)S(1)} %get-tuple-element.27.c_ref), channel_id=1, source_target_pairs={{0,4},{4,8},{8,12},{12,16},{16,20},{20,24},{24,28},{28,32},{32,36}... | collective-permute-start | bytes 147464 | tf_op jit(solution)/shard_map/ppermute | solution.py:462
  103.6 7.1 %collective-permute-start.11 = (f32[3,3,4,8,128]{4,3,2,1,0:T(8,128)S(1)}, f32[3,3,4,8,128]{4,3,2,1,0:T(8,128)S(1)}, u32[]{:S(2)}, u32[]{:S(2)}) collective-permute-start(f32[3,3,4,8,128]{4,3,2,1,0:T(8,128)S(1)} %shard_map.63.c_ref), channel_id=1, source_target_pairs={{0,244},{4,248},{8,252},{12,0},{16,4},{20,8},{24,12},{28,16},{32,2... | collective-permute-start | bytes 442376 | tf_op jit(solution)/shard_map/ppermute | solution.py:468
  105.6 8.0 %collective-permute-start.10 = (f32[3,3,4,8,128]{4,3,2,1,0:T(8,128)S(1)}, f32[3,3,4,8,128]{4,3,2,1,0:T(8,128)S(1)}, u32[]{:S(2)}, u32[]{:S(2)}) collective-permute-start(f32[3,3,4,8,128]{4,3,2,1,0:T(8,128)S(1)} %shard_map.63.c_ref), channel_id=1, source_target_pairs={{0,12},{4,16},{8,20},{12,24},{16,28},{20,32},{24,36},{28,40},{32,4... | collective-permute-start | bytes 442376 | tf_op jit(solution)/shard_map/ppermute | solution.py:466

commit v2 on v1

v2 whole, which is shorter than its diff:
```python
import jax
import jax.numpy as jnp
from jax import lax
from jax.experimental import pallas as pl
from jax.experimental.pallas import tpu as pltpu
from jax.sharding import Mesh
from jax.sharding import PartitionSpec as P

EMIN = 0.01
BETA = 8.0
OMEGA = 0.6
ETAS = (0.7, 0.5, 0.3)
NBX = 64
VMEM_LIMIT = 16 * 1024 * 1024
F32 = jnp.float32
HI = lax.Precision.HIGHEST


GROUP = 4


def loop(first, last, step, group=None):
    group = group or GROUP
    turns = (last - first) // group

    def turn(t, _):
        for j in range(group):
            step(first + t * group + j)
        return 0

    lax.fori_loop(0, turns, turn, 0)
    for i in range(first + turns * group, last):
        step(i)


def shaped(*dims):
    return jax.ShapeDtypeStruct(dims, F32)


def rolled(v, amount, axis):
    return pltpu.roll(v, amount % v.shape[axis], axis)


def iota(shape, axis):
    return lax.broadcasted_iota(jnp.int32, shape, axis)


def pool_matrix():
    return (iota((256, 128), 0) // 2 == iota((256, 128), 1)).astype(F32)


def widen_matrix():
    return (iota((128, 256), 1) // 2 == iota((128, 256), 0)).astype(F32)


def y_edges(rows, stride):
    y = iota((rows, 1), 0)
    low = (y >= stride).astype(F32)
    outer = 0.5 * ((y < stride).astype(F32) + (y >= rows - stride).astype(F32))
    return low, outer


def face_y(e, low, stride):
    return 0.5 * low * (e + rolled(e, stride, e.ndim - 2))


def face_z(e, stride):
    return 0.5 * (e + rolled(e, stride, e.ndim - 1))


def through(c, u, stride, axis):
    flow = c * (u - rolled(u, stride, axis))
    return flow - rolled(flow, -stride, axis)


def operate(prev, u, after, cx, cx_after, cy, cz, side, stride):
    n = u.ndim
    total = cx * (u - prev) - cx_after * (after - u)
    total = total + through(cy, u, stride, n - 2) + through(cz, u, stride, n - 1)
    return total + side * u


def inverse(e, diag):
    return jnp.where(e > 0.0, 1.0 / jnp.where(e > 0.0, diag, 1.0), 0.0)


def prepare(e_ref, cx_ref, cy_ref, cz_ref, inv_ref, first, last):
    low, outer = y_edges(16, 1)

    def step(i):
        for r in range(3):
            e = e_ref[r, i]
            cx = 0.5 * (e + e_ref[r, i - 1])
            cx_after = 0.5 * (e + e_ref[r, i + 1])
            cy = face_y(e, low, 1)
            cz = face_z(e, 1)
            diag = cx + cx_after + (cy + rolled(cy, -1, 0)) + (cz + rolled(cz, -1, 1)) + outer * e
            cx_ref[r, i] = cx
            cy_ref[r, i] = cy
            cz_ref[r, i] = cz
            inv_ref[r, i] = inverse(e, diag)

    loop(first, last, step)
    for r in range(3):
        cx_ref[r, last] = 0.5 * (e_ref[r, last] + e_ref[r, last - 1])


def operate0(u_ref, i, r, e_ref, cx_ref, cy_ref, cz_ref, outer):
    return operate(
        u_ref[r, i - 1], u_ref[r, i], u_ref[r, i + 1],
        cx_ref[r, i], cx_ref[r, i + 1], cy_ref[r, i], cz_ref[r, i], outer * e_ref[r, i], 1,
    )


def pool_own(src_of, many, big_ref, half_ref, scale):
    for f in range(many):
        for k in range(4):
            at = (f * 4 + k) * 16
            big_ref[at : at + 16, :] = (0.125 * scale) * (src_of(f, 8 + 2 * k) + src_of(f, 9 + 2 * k))
    rows = many * 64
    half_ref[0:rows, :] = jnp.dot(big_ref[0:rows, :], pool_matrix(), precision=HI, preferred_element_type=F32)
    return half_ref[pl.ds(0, rows // 2, stride=2), :] + half_ref[pl.ds(1, rows // 2, stride=2), :]


def stack_level(e, stride):
    low, outer = y_edges(8, stride)
    before = jnp.concatenate([e[:1], e[:-1]], 0)
    cx = 0.5 * (e + before)
    cx_after = jnp.concatenate([cx[1:], cx[:1]], 0)
    cy = face_y(e, low[None], stride)
    cz = face_z(e, stride)
    side = outer[None] * e
    diag = cx + cx_after + (cy + rolled(cy, -stride, 1)) + (cz + rolled(cz, -stride, 2)) + side
    return cx, cx_after, cy, cz, side, inverse(e, diag)


def stack_operate(level, u, stride, first, last):
    cx, cx_after, cy, cz, side, _ = (v[first:last] for v in level)
    return operate(u[:-2], u[1:-1], u[2:], cx, cx_after, cy, cz, side, stride)


def stack_pool(v, stride):
    n = v.shape[0] // 2
    v = v.reshape(n, 2, 8, 128)
    v = v[:, 0] + v[:, 1]
    y = iota((1, 8, 1), 1)
    v = v + jnp.where((y // stride) % 2 == 0, rolled(v, -stride, 1), rolled(v, stride, 1))
    z = iota((1, 1, 128), 2)
    v = v + jnp.where((z // stride) % 2 == 0, rolled(v, -stride, 2), rolled(v, stride, 2))
    return 0.125 * v


def twice(v):
    n = v.shape[0]
    return jnp.broadcast_to(v[:, None], (n, 2, 8, 128)).reshape(2 * n, 8, 128)


STRIDES = (1, 2, 4)


def set_levels(e1_ref, level_refs):
    def step(r, _):
        e = e1_ref[r]
        for ref, stride in zip(level_refs, STRIDES):
            for q, v in enumerate(stack_level(e, stride)):
                ref[q, r] = v
            e = 0.25 * stack_pool(e, stride) if stride < 4 else e
        return 0

    lax.fori_loop(0, 3, step, 0)


def coarse(levels, rhs1, first, last):
    one, two, three = levels
    x1 = OMEGA * rhs1 * one[5]
    rest1 = rhs1[2:34] - stack_operate(one, x1[1:35], 1, 2, 34)
    rhs2 = stack_pool(rest1, 1)
    x2 = OMEGA * rhs2 * two[5][1:17]
    rest2 = rhs2[1:15] - stack_operate(two, x2, 2, 2, 16)
    rhs3 = stack_pool(rest2, 2)
    x3 = OMEGA * rhs3 * three[5][1:8]
    x3 = x3[1:6] + OMEGA * (rhs3[1:6] - stack_operate(three, x3, 4, 2, 7)) * three[5][2:7]
    x2 = x2[3:13] + twice(x3)
    x2 = x2[1:9] + OMEGA * (rhs2[4:12] - stack_operate(two, x2, 2, 5, 13)) * two[5][5:13]
    x1 = x1[10:26] + twice(x2)
    x1, at = x1[first - 11 : last - 9], slice(first, last)
    return x1[1:-1] + OMEGA * (rhs1[at] - stack_operate(one, x1, 1, first, last)) * one[5][at]


def coarse_all(level_refs, rhs1_ref, out_ref, first, last):
    def step(r, _):
        levels = [[ref[q, r] for q in range(6)] for ref in level_refs]
        out_ref[r, 0 : last - first] = coarse(levels, rhs1_ref[r], first, last)
        return 0

    lax.fori_loop(0, 3, step, 0)


def widen_into(e1_ref, count, wide_ref):
    rows = 3 * count * 8
    src = jnp.concatenate([e1_ref[r, :count].reshape(count * 8, 128) for r in range(3)], 0)
    wide = jnp.dot(src, widen_matrix(), precision=HI, preferred_element_type=F32)
    for h in range(2):
        part = wide[:, 128 * h : 128 * h + 128]
        wide_ref[h, pl.ds(0, rows, stride=2), :] = part
        wide_ref[h, pl.ds(1, rows, stride=2), :] = part


def widened(wide_ref, r, k, count):
    at = pl.multiple_of((r * count + k) * 16, 16)
    return jnp.concatenate([wide_ref[0, pl.ds(at, 16), :], wide_ref[1, pl.ds(at, 16), :]], 1)


REACH = (7, 6, 6, 5)
OFFS = (0, 7, 13, 19)


def pack_kernel(d_ref, v_ref, s_ref, load_ref, out_ref):
    out_ref[0] = d_ref[...]
    out_ref[1] = v_ref[...].astype(F32)
    out_ref[2] = s_ref[...].astype(F32)
    out_ref[3] = load_ref[...]


def select_kernel(c_ref, l_ref, r_ref, own_ref, up_ref, down_ref):
    right = iota((8, 128), 1) < 64
    for f in range(4):
        for i in range(8):
            for h in range(2):
                halo = jnp.where(right, r_ref[h, f, i], l_ref[h, f, i])
                piece = jnp.concatenate([c_ref[h, f, i], halo], 1)
                own_ref[f, i, 8 * h : 8 * h + 8, :] = piece
                if i >= 8 - REACH[f]:
                    up_ref[OFFS[f] + i - (8 - REACH[f]), 8 * h : 8 * h + 8, :] = piece
                if i < REACH[f]:
                    down_ref[OFFS[f] + i, 8 * h : 8 * h + 8, :] = piece


def spread_out(own_ref, lo_ref, hi_ref, refs):
    for f, ref in enumerate(refs):
        n = REACH[f]
        for j in range(n):
            ref[8 - n + j] = lo_ref[OFFS[f] + j]
            ref[16 + j] = hi_ref[OFFS[f] + j]
        for j in range(8):
            ref[8 + j] = own_ref[f, j]


def stiffness(place_ref, d_ref, v_ref, s_ref, e_ref, f_ref, first, last):
    block, gy = place_ref[0], place_ref[1]
    lane = iota((1, 256), 1)
    z = gy * 128 + jnp.where(lane < 192, lane, lane - 256)
    z_in = ((z >= 0) & (z < 512)).astype(F32)
    z_count = ((z >= 1) & (z < 513)).astype(F32) + ((z >= -1) & (z < 511)).astype(F32)
    y = iota((16, 1), 0)
    low, high = (y >= 1).astype(F32), (y < 15).astype(F32)
    yz_count = (low + high) + z_count
    shifts = [(jnp.tanh(jnp.full((1, 1), BETA * eta, F32)), jnp.tanh(jnp.full((1, 1), BETA * (1.0 - eta), F32))) for eta in ETAS]

    def step(i):
        x = 8 * block + i - 8
        inside = lambda at: ((at >= 0) & (at < 8 * NBX)).astype(F32)
        d = d_ref[i]
        total = 2.0 * d + d_ref[i + 1] + d_ref[i - 1]
        total = total + low * rolled(d, 1, 0) + high * rolled(d, -1, 0) + rolled(d, 1, 1) + rolled(d, -1, 1)
        weights = yz_count + (2.0 + inside(x - 1) + inside(x + 1))
        here = z_in * inside(x)
        filtered = total / weights
        void, solid = v_ref[i], s_ref[i]
        open_ = 1.0 - void
        scale = here * (open_ * (1.0 - solid)) / weights
        for r, eta in enumerate(ETAS):
            t0, t1 = shifts[r]
            den = t0 + t1
            t = jnp.tanh(BETA * (filtered - eta))
            projected = (t0 + t) / den
            physical = open_ * (solid + (1.0 - solid) * projected)
            square = physical * physical
            e_ref[r, i] = here * (EMIN + (1.0 - EMIN) * (square * physical))
            if f_ref is not None:
                slope = BETA * (1.0 - t * t) / den
                f_ref[r, i] = (3.0 * (1.0 - EMIN)) * square * scale * slope

    loop(first, last, step)


def first_kernel(
    place_ref, own_ref, lo_ref, hi_ref, g_ref,
    d_ref, v_ref, s_ref, load_ref, e_ref, cx_ref, cy_ref, cz_ref, inv_ref, x_ref, rest_ref, big_ref, half_ref,
):
    spread_out(own_ref, lo_ref, hi_ref, (d_ref, v_ref, s_ref, load_ref))
    stiffness(place_ref, d_ref, v_ref, s_ref, e_ref, None, 6, 18)
    prepare(e_ref, cx_ref, cy_ref, cz_ref, inv_ref, 7, 17)

    def start(i):
        for r in range(3):
            x_ref[r, i] = OMEGA * load_ref[i] * inv_ref[r, i]

    loop(7, 17, start)
    _, outer = y_edges(16, 1)

    def leftover(i):
        for r in range(3):
            rest_ref[r, i - 8] = load_ref[i] - operate0(x_ref, i, r, e_ref, cx_ref, cy_ref, cz_ref, outer)

    loop(8, 16, leftover)
    g_ref[0:3] = pool_own(lambda f, i: rest_ref[f, i - 8], 3, big_ref, half_ref, 1.0).reshape(3, 4, 8, 128)
    g_ref[3:6] = pool_own(lambda f, i: e_ref[f, i], 3, big_ref, half_ref, 0.25).reshape(3, 4, 8, 128)


def wide_kernel(
    place_ref, own_ref, lo_ref, hi_ref, e_ref, f_ref, load_ref, cx_ref, cy_ref, cz_ref, inv_ref, d_ref, v_ref, s_ref,
):
    spread_out(own_ref, lo_ref, hi_ref, (d_ref, v_ref, s_ref, load_ref))
    stiffness(place_ref, d_ref, v_ref, s_ref, e_ref, f_ref, 2, 22)
    prepare(e_ref, cx_ref, cy_ref, cz_ref, inv_ref, 3, 21)


def mix_kernel(place_ref, lo_ref, c_ref, hi_ref, out_ref):
    mine = place_ref[0] % 4
    for to in range(4):
        out_ref[to, 0] = c_ref[...]
        out_ref[to, 1] = jnp.where(mine > to, lo_ref[...], hi_ref[...])


def window(place_ref, lo_ref, c_ref, hi_ref, mixed_ref, first, into_ref):
    block = place_ref[0]
    mine = block % 4
    for b in range(9):
        at = block - 4 + b
        keep = ((at >= 0) & (at < NBX)).astype(F32)
        source = mine + (b - 4)
        for r in range(3):
            if b == 0:
                piece = lo_ref[first + r]
            elif b == 4:
                piece = c_ref[first + r]
            elif b == 8:
                piece = hi_ref[first + r]
            else:
                far = ((source < 0) | (source > 3)).astype(jnp.int32)
                piece = mixed_ref[(source + 4) % 4, far, first + r]
            into_ref[r, 4 * b : 4 * b + 4] = keep * piece


def second_kernel(
    place_ref, e_ref, load_ref, cx_ref, cy_ref, cz_ref, inv_ref, lo_ref, c_ref, hi_ref, mixed_ref,
    one_ref, two_ref, three_ref, z0_ref, q0_ref, g_ref,
    e1_ref, x_ref, y_ref, rhs_ref, out1_ref, wide_ref, big_ref, half_ref,
):
    got = (place_ref, lo_ref, c_ref, hi_ref, mixed_ref)
    window(*got, 3, e1_ref)
    window(*got, 0, rhs_ref)
    levels = (one_ref, two_ref, three_ref)
    set_levels(e1_ref, levels)
    coarse_all(levels, rhs_ref, out1_ref, 13, 23)
    widen_into(out1_ref, 10, wide_ref)
    _, outer = y_edges(16, 1)

    def start(i):
        for r in range(3):
            x_ref[r, i] = OMEGA * load_ref[i] * inv_ref[r, i] + widened(wide_ref, r, (i - 2) // 2, 10)

    loop(3, 21, start)

    def smooth(i):
        for r in range(3):
            image = operate0(x_ref, i, r, e_ref, cx_ref, cy_ref, cz_ref, outer)
            z0_ref[r, i] = x_ref[r, i] + OMEGA * (load_ref[i] - image) * inv_ref[r, i]

    loop(4, 20, smooth)

    def apply(i):
        for r in range(3):
            image = operate0(z0_ref, i, r, e_ref, cx_ref, cy_ref, cz_ref, outer)
            q0_ref[r, i] = image
            y_ref[r, i] = OMEGA * image * inv_ref[r, i]

    loop(5, 19, apply)

    def leftover(i):
        for r in range(3):
            x_ref[r, i] = q0_ref[r, i] - operate0(y_ref, i, r, e_ref, cx_ref, cy_ref, cz_ref, outer)

    loop(8, 16, leftover)
    g_ref[...] = pool_own(lambda f, i: x_ref[f, i], 3, big_ref, half_ref, 1.0).reshape(3, 4, 8, 128)


def third_kernel(
    place_ref, e_ref, load_ref, cx_ref, cy_ref, cz_ref, inv_ref, one_ref, two_ref, three_ref, z0_ref, q0_ref,
    lo_ref, c_ref, hi_ref, mixed_ref, w_ref, dots_ref, x_ref, rhs_ref, out1_ref, wide_ref,
):
    window(place_ref, lo_ref, c_ref, hi_ref, mixed_ref, 0, rhs_ref)
    coarse_all((one_ref, two_ref, three_ref), rhs_ref, out1_ref, 14, 22)
    widen_into(out1_ref, 8, wide_ref)
    _, outer = y_edges(16, 1)

    def start(i):
        for r in range(3):
            x_ref[r, i] = OMEGA * q0_ref[r, i] * inv_ref[r, i] + widened(wide_ref, r, (i - 4) // 2, 8)

    loop(5, 19, start)

    def smooth(i):
        for r in range(3):
            image = operate0(x_ref, i, r, e_ref, cx_ref, cy_ref, cz_ref, outer)
            w_ref[r, i] = x_ref[r, i] + OMEGA * (q0_ref[r, i] - image) * inv_ref[r, i]

    loop(6, 18, smooth)

    def add(t, sums):
        sums = list(sums)
        for i in (8 + 2 * t, 9 + 2 * t):
            for r in range(3):
                image = operate0(w_ref, i, r, e_ref, cx_ref, cy_ref, cz_ref, outer)[:, :128]
                b, z0, q0, w = load_ref[i, :, :128], z0_ref[r, i, :, :128], q0_ref[r, i, :, :128], w_ref[r, i, :, :128]
                for q, term in enumerate((b * z0, z0 * q0, b * w, q0 * w, w * image)):
                    sums[r * 5 + q] = sums[r * 5 + q] + (term[:8] + term[8:])
        return tuple(sums)

    sums = lax.fori_loop(0, 4, add, tuple(jnp.zeros((8, 128), F32) for _ in range(15)))
    lane = iota((1, 128), 1)
    row = jnp.zeros((1, 128), F32)
    for q, v in enumerate(sums):
        row = row + jnp.where(lane == q, jnp.sum(jnp.sum(v, 0, keepdims=True), 1, keepdims=True), 0.0)
    dots_ref[...] = jnp.broadcast_to(row[None], (16, 1, 128))


def sum_kernel(in_ref, out_ref):
    out_ref[...] = jnp.broadcast_to(jnp.sum(in_ref[...], 0, keepdims=True), (16, 1, 128))


def last_kernel(place_ref, f_ref, z0_ref, w_ref, dots_ref, sens_ref, comp_ref, u_ref, comb_ref):
    real = place_ref[2]
    totals = jnp.sum(dots_ref[...], 0)
    lane = iota((1, 128), 1)
    pick = lambda q: jnp.sum(jnp.where(lane == q, totals, 0.0), 1, keepdims=True)
    factors = []
    for r in range(3):
        bz, zq, bw, qw, wa = (pick(r * 5 + q) for q in range(5))
        a0 = bz / zq
        rz1 = bz - a0 * bw - a0 * zq + (a0 * a0) * qw
        grow = 1.0 + rz1 / bz
        a1 = rz1 / ((grow * grow) * zq - 2.0 * (a0 * grow) * qw + (a0 * a0) * wa)
        c0, c1 = a0 + a1 * grow, -(a1 * a0)
        factors.append((c0, c1))
        comp_ref[r] = jnp.sum(c0 * bz + c1 * bw)
    y = iota((16, 1), 0)
    low, high = (y >= 1).astype(F32), (y < 15).astype(F32)

    def state(i):
        for r in range(3):
            u_ref[r, i] = factors[r][0] * z0_ref[r, i] + factors[r][1] * w_ref[r, i]

    loop(6, 18, state)

    def energy(i):
        total = jnp.zeros((16, 256), F32)
        for r in range(3):
            u = u_ref[r, i]
            gaps = (
                u - u_ref[r, i - 1],
                u - u_ref[r, i + 1],
                u - low * rolled(u, 1, 0),
                u - high * rolled(u, -1, 0),
                u - rolled(u, 1, 1),
                u - rolled(u, -1, 1),
            )
            square = gaps[0] * gaps[0]
            for gap in gaps[1:]:
                square = square + gap * gap
            total = total - (0.5 * square) * f_ref[r, i]
        comb_ref[i] = total

    loop(7, 17, energy)

    def spread(i):
        c = comb_ref[i]
        total = 2.0 * c + comb_ref[i + 1] + comb_ref[i - 1]
        total = total + low * rolled(c, 1, 0) + high * rolled(c, -1, 0) + rolled(c, 1, 1) + rolled(c, -1, 1)
        sens_ref[i - 8] = jnp.where(real == 0, total[:8, :128], total[8:, :128])

    loop(8, 16, spread)


def call(body, outs, scratch, *args, place=None, flops=0, out_specs=None):
    in_specs = [pl.BlockSpec(memory_space=pltpu.VMEM)] * len(args)
    if place is not None:
        in_specs, args = [pl.BlockSpec(memory_space=pltpu.SMEM)] + in_specs, (place, *args)
    return pl.pallas_call(
        body,
        out_shape=outs,
        in_specs=in_specs,
        **({} if out_specs is None else {"out_specs": out_specs}),
        scratch_shapes=[pltpu.VMEM(dims, F32) for dims in scratch],
        compiler_params=pltpu.CompilerParams(vmem_limit_bytes=VMEM_LIMIT),
        cost_estimate=pl.CostEstimate(flops=flops, bytes_accessed=0, transcendentals=0),
    )(*args)


Z_AXES = ("zh", "zl")
X_AXES = ("zh", "zl", "xc")
Y_AXES = ("yl", "core")
FIELD = (3, 24, 16, 256)
LEVEL1 = (3, 36, 8, 128)
SLICES = (24, 16, 256)


def neighbours(count, step, wrap):
    return [(i, (i + step) % count) for i in range(count) if wrap or 0 <= i + step < count]


def fetch(place, own):
    lo = lax.ppermute(own, Z_AXES, neighbours(16, 1, True))
    hi = lax.ppermute(own, Z_AXES, neighbours(16, -1, True))
    mixed = call(mix_kernel, shaped(4, 2, *own.shape), [], lo, own, hi, place=place)
    return lo, own, hi, lax.all_to_all(mixed, "xc", 0, 0)


def body(design, load, void_mask, solid_mask):
    place = jnp.stack([lax.axis_index(X_AXES), lax.axis_index(Y_AXES), lax.axis_index("real")]).astype(jnp.int32)
    own = call(pack_kernel, shaped(4, 8, 8, 128), [], design, void_mask, solid_mask, load)
    both = lax.all_gather(own, "real")
    left = lax.ppermute(both, Y_AXES, neighbours(4, 1, False))
    right = lax.ppermute(both, Y_AXES, neighbours(4, -1, False))
    mine, up, down = call(select_kernel, (shaped(4, 8, 16, 256), shaped(*SLICES), shaped(*SLICES)), [], both, left, right)
    lo = lax.ppermute(up, X_AXES, neighbours(NBX, 1, False))
    hi = lax.ppermute(down, X_AXES, neighbours(NBX, -1, False))
    g = call(
        first_kernel,
        shaped(6, 4, 8, 128),
        [SLICES] * 4 + [FIELD] * 6 + [(3, 8, 16, 256), (192, 256), (192, 128)],
        mine, lo, hi, place=place,
    )
    e, f, wide_load, cx, cy, cz, inv = call(
        wide_kernel,
        (shaped(*FIELD), shaped(*FIELD), shaped(*SLICES)) + (shaped(*FIELD),) * 4,
        [SLICES] * 3,
        mine, lo, hi, place=place, flops=2 * 10**7,
    )
    level0 = (e, wide_load, cx, cy, cz, inv)
    levels = tuple(shaped(6, 3, n, 8, 128) for n in (36, 18, 9))
    *levels, z0, q0, g2 = call(
        second_kernel,
        levels + (shaped(*FIELD), shaped(*FIELD), shaped(3, 4, 8, 128)),
        [LEVEL1, FIELD, FIELD, LEVEL1, (3, 10, 8, 128), (2, 480, 128), (192, 256), (192, 128)],
        *level0, *fetch(place, g), place=place,
    )
    w, dots = call(
        third_kernel,
        (shaped(*FIELD), shaped(16, 1, 128)),
        [FIELD, LEVEL1, (3, 8, 8, 128), (2, 384, 128)],
        *level0, *levels, z0, q0, *fetch(place, g2), place=place,
    )
    dots = lax.all_to_all(dots, ("zl", "xc"), 0, 0, tiled=True)
    dots = call(sum_kernel, shaped(16, 1, 128), [], dots)
    dots = lax.all_to_all(dots, ("zh", "yl", "core"), 0, 0, tiled=True)
    return call(
        last_kernel,
        (shaped(8, 8, 128), shaped(3)),
        [FIELD, SLICES],
        f, z0, w, dots, place=place,
        out_specs=(pl.BlockSpec(memory_space=pltpu.VMEM), pl.BlockSpec(memory_space=pltpu.SMEM)),
    )


def solution(mesh):
    split = Mesh(mesh.devices.reshape(2, 4, 4, 4, 2, 2), ("real", "zh", "zl", "xc", "yl", "core"))
    spec = P(X_AXES, "real", Y_AXES)
    return jax.shard_map(body, mesh=split, in_specs=(spec,) * 4, out_specs=(spec, P()), check_vma=False)
```

time: 164 us -> 155 us (0.945)
  local copies, waits for them, and re-layouts: 0.63 us -> 18 us
  waiting for transfers between devices: 38.3 us -> 23.6 us
  blocking collectives: 40.8 us -> 53 us
  starting transfers between devices: 44.9 us -> 33.8 us
  Pallas kernels: 35 us -> 24.3 us
    unnamed x0 -> x52, local copies, waits for them, and re-layouts: none -> 18 us
    ppermute x8 -> x4, waiting for transfers between devices: 24.9 us -> 7.32 us  [the longest x2 7.32 us: fetch(): lo = lax.ppermute(own, Z_AXES, neighbours(16, 1, True))]
    ppermute x8 -> x4, starting transfers between devices: 31.2 us -> 15.9 us  [the longest x2 10.6 us: fetch(): hi = lax.ppermute(own, Z_AXES, neighbours(16, -1, True))]
    all_to_all x2 -> x3, blocking collectives: 34 us -> 46.2 us  [the longest x1 28.3 us: body(): dots = lax.all_to_all(dots, ('zh', 'yl', 'core'), 0, 0, tiled=True)]
    pallas_call x8 -> x10, Pallas kernels: 35 us -> 24.3 us  [call(): pl.pallas_call(body, out_shape=outs, in_specs=in_specs, **{} if out_specs...]
    all_to_all x0 -> x1, starting transfers between devices: none -> 4.19 us  [fetch(): return (lo, own, hi, lax.all_to_all(mixed, 'xc', 0, 0))]
    all_to_all x0 -> x1, waiting for transfers between devices: none -> 2.89 us  [fetch(): return (lo, own, hi, lax.all_to_all(mixed, 'xc', 0, 0))]
  transfers between devices with their start and end apart: 12 -> 9, of which waited for: 9 -> 6; matrix products, arithmetic and copies ran while one was open for 0% -> 0% of each run, Pallas kernels for 0% -> 2%
where the time goes in v2:
time: 155 us; the launch traced here: 154 us
  blocking collectives  53 us (34%)
  starting transfers between devices  33.8 us (22%)
  Pallas kernels  24.3 us (16%)
  waiting for transfers between devices  23.6 us (15%)
  local copies, waits for them, and re-layouts  18 us (12%)
    all_to_all x1, blocking collectives, body(): dots = lax.all_to_all(dots, ('zh', 'yl', 'core'), 0, 0, tiled=True)  28.3 us
    pallas_call x10, Pallas kernels, call(): pl.pallas_call(body, out_shape=outs, in_specs=in_specs, **{} if out_specs...  24.3 us
    unnamed x52, local copies, waits for them, and re-layouts  18 us
    ppermute x2, starting transfers between devices, fetch(): hi = lax.ppermute(own, Z_AXES, neighbours(16, -1, True))  10.6 us
    all_to_all x1, blocking collectives, body(): dots = lax.all_to_all(dots, ('zl', 'xc'), 0, 0, tiled=True)  9.33 us
    ppermute x1, starting transfers between devices, body(): right = lax.ppermute(both, Y_AXES, neighbours(4, -1, False))  9.17 us
    all_to_all x1, blocking collectives, fetch(): return (lo, own, hi, lax.all_to_all(mixed, 'xc', 0, 0))  8.62 us
    ppermute x2, waiting for transfers between devices, fetch(): lo = lax.ppermute(own, Z_AXES, neighbours(16, 1, True))  7.32 us
  transfers between devices with their start and end apart: 9, of which 6 were waited for; matrix products, arithmetic and copies ran while one was open for 0% of the time, Pallas kernels for 2%

profile of v2, /device:TPU:1, one launch (start us, length us, event | category | flops | bytes accessed | tf_op | source)
XLA Modules:
  0.0 153.6 jit_solution(4279421868284547422)
XLA Ops:
  0.6 0.0 copy-start.22
  0.6 0.7 copy-done.22
  1.4 0.0 copy-start.23
  1.4 0.8 copy-done.23
  2.1 0.8 copy-done.24
  2.9 0.8 copy-done.25
  3.7 6.8 %all-gather = f32[8,8,8,128]{3,2,1,0:T(8,128)S(1)} all-gather(f32[4,8,8,128]{3,2,1,0:T(8,128)S(1)} %shard_map.59), channel_id=2, replica_groups=mesh['real'=2,'zh'=4,'zl'=4,'xc'=4,'yl'=2,'core'=2] {'real'}, dimensions={0}, use_global_device_ids=true | all-gather | bytes 393216 | tf_op jit(solution)/shard_map/all_gather | solution.py:523
  10.4 9.2 %collective-permute-start.1 = (f32[2,4,8,8,128]{4,3,2,1,0:T(8,128)S(1)}, f32[2,4,8,8,128]{4,3,2,1,0:T(8,128)S(1)}, u32[]{:S(2)}, u32[]{:S(2)}) collective-permute-start(f32[2,4,8,8,128]{4,3,2,1,0:T(8,128)S(1)} %bitcast.4), channel_id=1, source_target_pairs={{1,0},{2,1},{3,2},{5,4},{6,5},{7,6},{9,8},{10,9},{11,10},{13,12},{... | collective-permute-start | bytes 786440 | tf_op jit(solution)/shard_map/ppermute | solution.py:525
  19.6 1.9 %collective-permute-start = (f32[2,4,8,8,128]{4,3,2,1,0:T(8,128)S(1)}, f32[2,4,8,8,128]{4,3,2,1,0:T(8,128)S(1)}, u32[]{:S(2)}, u32[]{:S(2)}) collective-permute-start(f32[2,4,8,8,128]{4,3,2,1,0:T(8,128)S(1)} %bitcast.5), channel_id=1, source_target_pairs={{0,1},{1,2},{2,3},{4,5},{5,6},{6,7},{8,9},{9,10},{10,11},{12,13},{... | collective-permute-start | bytes 786440 | tf_op jit(solution)/shard_map/ppermute | solution.py:524
  21.5 0.0 collective-permute-done.1.r_ref
  21.6 3.3 %collective-permute-done.l_ref = f32[2,4,8,8,128]{4,3,2,1,0:T(8,128)S(1)} collective-permute-done((f32[2,4,8,8,128]{4,3,2,1,0:T(8,128)S(1)}, f32[2,4,8,8,128]{4,3,2,1,0:T(8,128)S(1)}, u32[]{:S(2)}, u32[]{:S(2)}) %collective-permute-start) | collective-permute-done | bytes 262176 | tf_op jit(solution)/shard_map/ppermute | solution.py:524
  24.8 0.1 shard_map.60
  24.9 0.0 copy-start.6
  24.9 1.3 collective-permute-start.2
  26.3 1.3 collective-permute-start.3
  27.6 0.1 pad_add_fusion.place_ref
  27.6 6.0 %collective-permute-done.2.lo_ref = f32[24,16,256]{2,1,0:T(8,128)S(1)} collective-permute-done((f32[24,16,256]{2,1,0:T(8,128)S(1)}, f32[24,16,256]{2,1,0:T(8,128)S(1)}, u32[]{:S(2)}, u32[]{:S(2)}) %collective-permute-start.2) | collective-permute-done | bytes 393248 | tf_op jit(solution)/shard_map/ppermute | solution.py:527
  33.7 4.1 %collective-permute-done.3.hi_ref = f32[24,16,256]{2,1,0:T(8,128)S(1)} collective-permute-done((f32[24,16,256]{2,1,0:T(8,128)S(1)}, f32[24,16,256]{2,1,0:T(8,128)S(1)}, u32[]{:S(2)}, u32[]{:S(2)}) %collective-permute-start.3) | collective-permute-done | bytes 393248 | tf_op jit(solution)/shard_map/ppermute | solution.py:528
  37.8 2.9 %shard_map.62.c_ref = f32[6,4,8,128]{3,2,1,0:T(8,128)S(1)} custom-call(s32[3]{0:T(128)S(1)} %pad_add_fusion.place_ref, f32[4,8,16,256]{3,2,1,0:T(8,128)S(1)} %get-tuple-element.20.own_ref, f32[24,16,256]{2,1,0:T(8,128)S(1)} %collective-permute-done.2.lo_ref, f32[24,16,256]{2,1,0:T(8,128)S(1)} %collective-permute-done.3.hi_ref), custom_call_target="tpu_custom_call" | custom-call | tf_op jit(solution)/shard_map/pallas_call | solution.py:490
  40.7 8.6 %collective-permute-start.5 = (f32[6,4,8,128]{3,2,1,0:T(8,128)S(1)}, f32[6,4,8,128]{3,2,1,0:T(8,128)S(1)}, u32[]{:S(2)}, u32[]{:S(2)}) collective-permute-start(f32[6,4,8,128]{3,2,1,0:T(8,128)S(1)} %shard_map.62.c_ref), channel_id=1, source_target_pairs={{0,240},{16,0},{32,16},{48,32},{64,48},{80,64},{96,80},{112,96},{1... | collective-permute-start | bytes 294920 | tf_op jit(solution)/shard_map/ppermute | solution.py:515
  49.3 1.9 %collective-permute-start.4 = (f32[6,4,8,128]{3,2,1,0:T(8,128)S(1)}, f32[6,4,8,128]{3,2,1,0:T(8,128)S(1)}, u32[]{:S(2)}, u32[]{:S(2)}) collective-permute-start(f32[6,4,8,128]{3,2,1,0:T(8,128)S(1)} %shard_map.62.c_ref), channel_id=1, source_target_pairs={{0,16},{16,32},{32,48},{48,64},{64,80},{80,96},{96,112},{112,128},... | collective-permute-start | bytes 294920 | tf_op jit(solution)/shard_map/ppermute | solution.py:514
  51.2 0.0 collective-permute-done.5.hi_ref
  51.2 4.7 %collective-permute-done.4.lo_ref = f32[6,4,8,128]{3,2,1,0:T(8,128)S(1)} collective-permute-done((f32[6,4,8,128]{3,2,1,0:T(8,128)S(1)}, f32[6,4,8,128]{3,2,1,0:T(8,128)S(1)}, u32[]{:S(2)}, u32[]{:S(2)}) %collective-permute-start.4) | collective-permute-done | bytes 98336 | tf_op jit(solution)/shard_map/ppermute | solution.py:514
  55.8 1.5 shard_map.63
  57.3 0.0 copy-done.6
  57.3 0.0 copy-done.10
  57.3 0.0 copy-done.12
  57.4 0.0 copy-start.16
  57.4 0.6 copy-done.16
  58.0 0.6 copy-done.18
  58.6 0.6 copy-done.20
  59.3 4.2 %all-to-all-start = ((f32[4,2,6,4,8,128]{5,4,3,2,1,0:T(8,128)}), f32[4,2,6,4,8,128]{5,4,3,2,1,0:T(8,128)}, u32[]{:S(2)}, u32[]{:S(2)}) async-start(f32[4,2,6,4,8,128]{5,4,3,2,1,0:T(8,128)} %shard_map.63), calls=%async_computation | async-start | bytes 1572864 | tf_op jit(solution)/shard_map/all_to_all | solution.py:517
  63.5 0.0 copy-start.7
  63.5 1.0 copy-done.7
  64.5 1.0 copy-done.11
  65.5 1.0 copy-done.13
  66.5 3.0 %shard_map.61 = (f32[3,24,16,256]{3,2,1,0:T(8,128)S(1)}, f32[3,24,16,256]{3,2,1,0:T(8,128)S(1)}, f32[24,16,256]{2,1,0:T(8,128)S(1)}, f32[3,24,16,256]{3,2,1,0:T(...) custom-call(s32[3]{0:T(128)S(1)} %pad_add_fusion.place_ref, ...), custom_call_target="tpu_custom_call" | custom-call | flops 20000000 | tf_op jit(solution)/shard_map/pallas_call | solution.py:490
  69.5 0.0 copy-start
  69.5 1.0 copy-done
  70.6 1.0 copy-done.3
  71.6 0.7 copy-done.8
  72.3 1.0 copy-done.14
  73.3 2.9 %all-to-all-done.mixed_ref = f32[4,2,6,4,8,128]{5,4,3,2,1,0:T(8,128)} async-done(((f32[4,2,6,4,8,128]{5,4,3,2,1,0:T(8,128)}), f32[4,2,6,4,8,128]{5,4,3,2,1,0:T(8,128)}, u32[]{:S(2)}, u32[]{:S(2)}) %all-to-all-start) | async-done | bytes 786464 | tf_op jit(solution)/shard_map/all_to_all | solution.py:517
  76.2 1.3 copy-done.1
  77.5 1.3 copy-done.4
  78.8 1.0 copy-done.9
  79.8 0.9 copy-done.17
  80.7 0.9 copy-done.19
  81.5 0.9 copy-done.21
  82.4 8.7 %shard_map.64 = (f32[6,3,36,8,128]{4,3,2,1,0:T(8,128)S(1)}, f32[6,3,18,8,128]{4,3,2,1,0:T(8,128)S(1)}, f32[6,3,9,8,128]{4,3,2,1,0:T(8,128)S(1)}, f32[3,24,16,256...) custom-call(s32[3]{0:T(128)S(1)} %pad_add_fusion.place_ref, ...), custom_call_target="tpu_custom_call" | custom-call | tf_op jit(solution)/shard_map/pallas_call | solution.py:490
  91.2 0.0 copy-start.2
  91.2 2.1 %collective-permute-start.7 = (f32[3,4,8,128]{3,2,1,0:T(8,128)S(1)}, f32[3,4,8,128]{3,2,1,0:T(8,128)S(1)}, u32[]{:S(2)}, u32[]{:S(2)}) collective-permute-start(f32[3,4,8,128]{3,2,1,0:T(8,128)S(1)} %get-tuple-element.35.c_ref), channel_id=1, source_target_pairs={{0,240},{16,0},{32,16},{48,32},{64,48},{80,64},{96,80},{112,96},{1... | collective-permute-start | bytes 147464 | tf_op jit(solution)/shard_map/ppermute | solution.py:515
  93.2 3.4 %collective-permute-start.6 = (f32[3,4,8,128]{3,2,1,0:T(8,128)S(1)}, f32[3,4,8,128]{3,2,1,0:T(8,128)S(1)}, u32[]{:S(2)}, u32[]{:S(2)}) collective-permute-start(f32[3,4,8,128]{3,2,1,0:T(8,128)S(1)} %get-tuple-element.35.c_ref), channel_id=1, source_target_pairs={{0,16},{16,32},{32,48},{48,64},{64,80},{80,96},{96,112},{112,128},... | collective-permute-start | bytes 147464 | tf_op jit(solution)/shard_map/ppermute | solution.py:514
  96.6 0.0 collective-permute-done.7.hi_ref
  96.6 2.7 %collective-permute-done.6.lo_ref = f32[3,4,8,128]{3,2,1,0:T(8,128)S(1)} collective-permute-done((f32[3,4,8,128]{3,2,1,0:T(8,128)S(1)}, f32[3,4,8,128]{3,2,1,0:T(8,128)S(1)}, u32[]{:S(2)}, u32[]{:S(2)}) %collective-permute-start.6) | collective-permute-done | bytes 49184 | tf_op jit(solution)/shard_map/ppermute | solution.py:514
  99.3 0.6 shard_map.65
  99.9 8.6 %all_to_all.20.mixed_ref = f32[4,2,3,4,8,128]{5,4,3,2,1,0:T(8,128)S(1)} all-to-all(f32[4,2,3,4,8,128]{5,4,3,2,1,0:T(8,128)S(1)} %shard_map.65), channel_id=1, replica_groups=mesh['real'=2,'zh'=4,'zl'=4,'xc'=4,'yl'=2,'core'=2] {'xc'}, dimensions={0} | all-to-all | bytes 786432 | tf_op jit(solution)/shard_map/all_to_all | solution.py:517
  108.5 0.0 copy-done.5
  108.5 0.0 copy-done.2
  108.5 5.4 %shard_map.66 = (f32[3,24,16,256]{3,2,1,0:T(8,128)S(1)}, f32[16,1,128]{2,1,0:T(1,128)S(1)}) custom-call(s32[3]{0:T(128)S(1)} %pad_add_fusion.place_ref, f32[3,24,16,256]{3,2,1,0:T(8,128)S(1)} %get-tuple-element.24.e_ref, f32[24,16,256]{2,1,0:T(8,128)S(1)} %copy-done.9, f32[3,24,16,256]{3,2,1,0:T(8,128)S(1)} %get-tuple-element.26.cx_ref, ...), custom_call_target="tpu_custom_call" | custom-call | tf_op jit(solution)/shard_map/pallas_call | solution.py:490
  113.9 9.3 %all_to_all.21.in_ref = f32[16,1,128]{2,1,0:T(1,128)S(1)} all-to-all(f32[16,1,128]{2,1,0:T(1,128)S(1)} %get-tuple-element.37), channel_id=1, replica_groups=mesh['real'=2,'zh'=4,'zl'=4,'xc'=4,'yl'=2,'core'=2] {'zl','xc'}, dimensions={0} | all-to-all | bytes 16384 | tf_op jit(solution)/shard_map/all_to_all | solution.py:555
  123.2 28.3 %all_to_all.22.dots_ref = f32[16,1,128]{2,1,0:T(1,128)S(1)} all-to-all(f32[16,1,128]{2,1,0:T(1,128)S(1)} %shard_map.67), channel_id=1, replica_groups=mesh['real'=2,'zh'=4,'zl'=4,'xc'=4,'yl'=2,'core'=2] {'zh','yl','core'}, dimensions={0} | all-to-all | bytes 16384 | tf_op jit(solution)/shard_map/all_to_all | solution.py:557
  151.5 0.0 copy-done.15
  151.5 2.1 %shard_map.68 = (f32[8,8,128]{2,1,0:T(8,128)}, f32[3]{0:T(128)}) custom-call(s32[3]{0:T(128)S(1)} %pad_add_fusion.place_ref, f32[3,24,16,256]{3,2,1,0:T(8,128)S(1)} %copy-done.15, f32[3,24,16,256]{3,2,1,0:T(8,128)S(1)} %get-tuple-element.30.z0_ref, f32[3,24,16,256]{3,2,1,0:T(8,128)S(1)} %get-tuple-element.36.w_ref, f32[16,1,128]{2,1,0:T(1,128)S(1)} %all_to_all.22.dots_ref), custom_call_target="tpu_custom_call" | custom-call | tf_op jit(solution)/shard_map/pallas_call | solution.py:490
  (21 shorter events, 0.1 us)
Async XLA Ops:
  0.6 0.8 copy-start.22
  1.4 0.8 copy-start.23
  2.1 0.8 copy-start.24
  2.9 0.8 copy-start.25
  10.4 11.1 %collective-permute-start.1 = (f32[2,4,8,8,128]{4,3,2,1,0:T(8,128)S(1)}, f32[2,4,8,8,128]{4,3,2,1,0:T(8,128)S(1)}, u32[]{:S(2)}, u32[]{:S(2)}) collective-permute-start(f32[2,4,8,8,128]{4,3,2,1,0:T(8,128)S(1)} %bitcast.4), channel_id=1, source_target_pairs={{1,0},{2,1},{3,2},{5,4},{6,5},{7,6},{9,8},{10,9},{11,10},{13,12},{... | collective-permute-start | bytes 786440 | tf_op jit(solution)/shard_map/ppermute | solution.py:525
  19.6 5.2 %collective-permute-start = (f32[2,4,8,8,128]{4,3,2,1,0:T(8,128)S(1)}, f32[2,4,8,8,128]{4,3,2,1,0:T(8,128)S(1)}, u32[]{:S(2)}, u32[]{:S(2)}) collective-permute-start(f32[2,4,8,8,128]{4,3,2,1,0:T(8,128)S(1)} %bitcast.5), channel_id=1, source_target_pairs={{0,1},{1,2},{2,3},{4,5},{5,6},{6,7},{8,9},{9,10},{10,11},{12,13},{... | collective-permute-start | bytes 786440 | tf_op jit(solution)/shard_map/ppermute | solution.py:524
  24.9 32.4 %copy-start.6 = (f32[4,8,16,256]{3,2,1,0:T(8,128)}, f32[4,8,16,256]{3,2,1,0:T(8,128)S(1)}, u32[]{:S(2)}) copy-start(f32[4,8,16,256]{3,2,1,0:T(8,128)S(1)} %get-tuple-element.20.own_ref) | copy-start | bytes 1572868
  24.9 8.7 %collective-permute-start.2 = (f32[24,16,256]{2,1,0:T(8,128)S(1)}, f32[24,16,256]{2,1,0:T(8,128)S(1)}, u32[]{:S(2)}, u32[]{:S(2)}) collective-permute-start(f32[24,16,256]{2,1,0:T(8,128)S(1)} %get-tuple-element.21), channel_id=1, source_target_pairs={{0,4},{4,8},{8,12},{12,16},{16,20},{20,24},{24,28},{28,32},{32,36}... | collective-permute-start | bytes 1179656 | tf_op jit(solution)/shard_map/ppermute | solution.py:527
  26.3 11.5 %collective-permute-start.3 = (f32[24,16,256]{2,1,0:T(8,128)S(1)}, f32[24,16,256]{2,1,0:T(8,128)S(1)}, u32[]{:S(2)}, u32[]{:S(2)}) collective-permute-start(f32[24,16,256]{2,1,0:T(8,128)S(1)} %get-tuple-element.22), channel_id=1, source_target_pairs={{4,0},{8,4},{12,8},{16,12},{20,16},{24,20},{28,24},{32,28},{36,32}... | collective-permute-start | bytes 1179656 | tf_op jit(solution)/shard_map/ppermute | solution.py:528
  33.7 23.7 %copy-start.10 = (f32[24,16,256]{2,1,0:T(8,128)}, f32[24,16,256]{2,1,0:T(8,128)S(1)}, u32[]{:S(2)}) copy-start(f32[24,16,256]{2,1,0:T(8,128)S(1)} %collective-permute-done.2.lo_ref) | copy-start | bytes 1179652
  37.8 19.6 %copy-start.12 = (f32[24,16,256]{2,1,0:T(8,128)}, f32[24,16,256]{2,1,0:T(8,128)S(1)}, u32[]{:S(2)}) copy-start(f32[24,16,256]{2,1,0:T(8,128)S(1)} %collective-permute-done.3.hi_ref) | copy-start | bytes 1179652
  40.7 10.5 %collective-permute-start.5 = (f32[6,4,8,128]{3,2,1,0:T(8,128)S(1)}, f32[6,4,8,128]{3,2,1,0:T(8,128)S(1)}, u32[]{:S(2)}, u32[]{:S(2)}) collective-permute-start(f32[6,4,8,128]{3,2,1,0:T(8,128)S(1)} %shard_map.62.c_ref), channel_id=1, source_target_pairs={{0,240},{16,0},{32,16},{48,32},{64,48},{80,64},{96,80},{112,96},{1... | collective-permute-start | bytes 294920 | tf_op jit(solution)/shard_map/ppermute | solution.py:515
  49.3 6.6 %collective-permute-start.4 = (f32[6,4,8,128]{3,2,1,0:T(8,128)S(1)}, f32[6,4,8,128]{3,2,1,0:T(8,128)S(1)}, u32[]{:S(2)}, u32[]{:S(2)}) collective-permute-start(f32[6,4,8,128]{3,2,1,0:T(8,128)S(1)} %shard_map.62.c_ref), channel_id=1, source_target_pairs={{0,16},{16,32},{32,48},{48,64},{64,80},{80,96},{96,112},{112,128},... | collective-permute-start | bytes 294920 | tf_op jit(solution)/shard_map/ppermute | solution.py:514
  57.4 0.6 copy-start.16
  58.0 0.6 copy-start.18
  58.6 0.6 copy-start.20
  59.3 17.0 %all-to-all-start = ((f32[4,2,6,4,8,128]{5,4,3,2,1,0:T(8,128)}), f32[4,2,6,4,8,128]{5,4,3,2,1,0:T(8,128)}, u32[]{:S(2)}, u32[]{:S(2)}) async-start(f32[4,2,6,4,8,128]{5,4,3,2,1,0:T(8,128)} %shard_map.63), calls=%async_computation | async-start | bytes 1572864 | tf_op jit(solution)/shard_map/all_to_all | solution.py:517
  63.5 1.0 copy-start.7
  64.5 1.0 copy-start.11
  65.5 1.0 copy-start.13
  69.5 1.0 copy-start
  70.6 1.0 copy-start.3
  71.6 0.7 copy-start.8
  72.3 1.0 copy-start.14
  76.2 1.3 copy-start.1
  77.5 1.3 copy-start.4
  78.8 1.0 copy-start.9
  79.8 0.9 copy-start.17
  80.7 0.9 copy-start.19
  81.5 0.9 copy-start.21
  82.4 26.1 %copy-start.5 = (f32[3,24,16,256]{3,2,1,0:T(8,128)S(1)}, f32[3,24,16,256]{3,2,1,0:T(8,128)}, u32[]{:S(2)}) copy-start(f32[3,24,16,256]{3,2,1,0:T(8,128)} %copy-done.3) | copy-start | bytes 3538948
  91.2 17.3 %copy-start.2 = (f32[3,24,16,256]{3,2,1,0:T(8,128)S(1)}, f32[3,24,16,256]{3,2,1,0:T(8,128)}, u32[]{:S(2)}) copy-start(f32[3,24,16,256]{3,2,1,0:T(8,128)} %copy-done) | copy-start | bytes 3538948
  91.2 5.4 %collective-permute-start.7 = (f32[3,4,8,128]{3,2,1,0:T(8,128)S(1)}, f32[3,4,8,128]{3,2,1,0:T(8,128)S(1)}, u32[]{:S(2)}, u32[]{:S(2)}) collective-permute-start(f32[3,4,8,128]{3,2,1,0:T(8,128)S(1)} %get-tuple-element.35.c_ref), channel_id=1, source_target_pairs={{0,240},{16,0},{32,16},{48,32},{64,48},{80,64},{96,80},{112,96},{1... | collective-permute-start | bytes 147464 | tf_op jit(solution)/shard_map/ppermute | solution.py:515
  93.2 6.0 %collective-permute-start.6 = (f32[3,4,8,128]{3,2,1,0:T(8,128)S(1)}, f32[3,4,8,128]{3,2,1,0:T(8,128)S(1)}, u32[]{:S(2)}, u32[]{:S(2)}) collective-permute-start(f32[3,4,8,128]{3,2,1,0:T(8,128)S(1)} %get-tuple-element.35.c_ref), channel_id=1, source_target_pairs={{0,16},{16,32},{32,48},{48,64},{64,80},{80,96},{96,112},{112,128},... | collective-permute-start | bytes 147464 | tf_op jit(solution)/shard_map/ppermute | solution.py:514
  108.5 43.0 %copy-start.15 = (f32[3,24,16,256]{3,2,1,0:T(8,128)S(1)}, f32[3,24,16,256]{3,2,1,0:T(8,128)}, u32[]{:S(2)}) copy-start(f32[3,24,16,256]{3,2,1,0:T(8,128)} %copy-done.14) | copy-start | bytes 3538948

commit v3 on v2

--- a/solution.py
+++ b/solution.py
@@ -215,11 +215,17 @@
 OFFS = (0, 7, 13, 19)
 
 
-def pack_kernel(d_ref, v_ref, s_ref, load_ref, out_ref):
-    out_ref[0] = d_ref[...]
-    out_ref[1] = v_ref[...].astype(F32)
-    out_ref[2] = s_ref[...].astype(F32)
-    out_ref[3] = load_ref[...]
+def pack_kernel(d_ref, v_ref, s_ref, load_ref, out_ref, v_in, s_in, sems):
+    pairs = ((d_ref, out_ref.at[0]), (v_ref, v_in), (s_ref, s_in), (load_ref, out_ref.at[3]))
+    copies = [pltpu.make_async_copy(src, dst, sems.at[q]) for q, (src, dst) in enumerate(pairs)]
+    for copy in copies:
+        copy.start()
+    copies[1].wait()
+    out_ref[1] = v_in[...].astype(F32)
+    copies[2].wait()
+    out_ref[2] = s_in[...].astype(F32)
+    copies[0].wait()
+    copies[3].wait()
 
 
 def select_kernel(c_ref, l_ref, r_ref, own_ref, up_ref, down_ref):
@@ -316,7 +322,8 @@
     prepare(e_ref, cx_ref, cy_ref, cz_ref, inv_ref, 3, 21)
 
 
-def mix_kernel(place_ref, lo_ref, c_ref, hi_ref, out_ref):
+def mix_kernel(place_ref, lo_ref, c_ref, hi_ref, *refs):
+    out_ref = refs[-1]
     mine = place_ref[0] % 4
     for to in range(4):
         out_ref[to, 0] = c_ref[...]
@@ -510,16 +517,21 @@
     return [(i, (i + step) % count) for i in range(count) if wrap or 0 <= i + step < count]
 
 
-def fetch(place, own):
+def fetch(place, own, *after):
     lo = lax.ppermute(own, Z_AXES, neighbours(16, 1, True))
     hi = lax.ppermute(own, Z_AXES, neighbours(16, -1, True))
-    mixed = call(mix_kernel, shaped(4, 2, *own.shape), [], lo, own, hi, place=place)
+    mixed = call(mix_kernel, shaped(4, 2, *own.shape), [], lo, own, hi, *after, place=place)
     return lo, own, hi, lax.all_to_all(mixed, "xc", 0, 0)
 
 
 def body(design, load, void_mask, solid_mask):
     place = jnp.stack([lax.axis_index(X_AXES), lax.axis_index(Y_AXES), lax.axis_index("real")]).astype(jnp.int32)
-    own = call(pack_kernel, shaped(4, 8, 8, 128), [], design, void_mask, solid_mask, load)
+    own = pl.pallas_call(
+        pack_kernel,
+        out_shape=shaped(4, 8, 8, 128),
+        in_specs=[pl.BlockSpec(memory_space=pl.ANY)] * 4,
+        scratch_shapes=[pltpu.VMEM((8, 8, 128), jnp.int32)] * 2 + [pltpu.SemaphoreType.DMA((4,))],
+    )(design, void_mask, solid_mask, load)
     both = lax.all_gather(own, "real")
     left = lax.ppermute(both, Y_AXES, neighbours(4, 1, False))
     right = lax.ppermute(both, Y_AXES, neighbours(4, -1, False))
@@ -544,7 +556,7 @@
         second_kernel,
         levels + (shaped(*FIELD), shaped(*FIELD), shaped(3, 4, 8, 128)),
         [LEVEL1, FIELD, FIELD, LEVEL1, (3, 10, 8, 128), (2, 480, 128), (192, 256), (192, 128)],
-        *level0, *fetch(place, g), place=place,
+        *level0, *fetch(place, g, wide_load), place=place,
     )
     w, dots = call(
         third_kernel,
@@ -552,9 +564,9 @@
         [FIELD, LEVEL1, (3, 8, 8, 128), (2, 384, 128)],
         *level0, *levels, z0, q0, *fetch(place, g2), place=place,
     )
-    dots = lax.all_to_all(dots, ("zl", "xc"), 0, 0, tiled=True)
+    dots = lax.all_to_all(dots, ("xc", "yl", "core"), 0, 0, tiled=True)
     dots = call(sum_kernel, shaped(16, 1, 128), [], dots)
-    dots = lax.all_to_all(dots, ("zh", "yl", "core"), 0, 0, tiled=True)
+    dots = lax.all_to_all(dots, ("zh", "zl"), 0, 0, tiled=True)
     return call(
         last_kernel,
         (shaped(8, 8, 128), shaped(3)),

time: 155 us -> 138 us (0.89)
  local copies, waits for them, and re-layouts: 18 us -> 0 us
  blocking collectives: 53 us -> 63.6 us
  waiting for transfers between devices: 23.6 us -> 18.8 us
  starting transfers between devices: 33.8 us -> 29.4 us
    unnamed x52 -> x0, local copies, waits for them, and re-layouts: 18 us -> none
    all_to_all x1 -> x2, blocking collectives: 8.62 us -> 24.1 us  [fetch(): return (lo, own, hi, lax.all_to_all(mixed, 'xc', 0, 0))]
    all_to_all x2, blocking collectives: 37.6 us -> 32.4 us  [the longest x1 20.8 us: body(): dots = lax.all_to_all(dots, ('zh', 'zl'), 0, 0, tiled=True)]
    all_to_all x1 -> x0, starting transfers between devices: 4.19 us -> none  [fetch(): return (lo, own, hi, lax.all_to_all(mixed, 'xc', 0, 0))]
    all_to_all x1 -> x0, waiting for transfers between devices: 2.89 us -> none  [fetch(): return (lo, own, hi, lax.all_to_all(mixed, 'xc', 0, 0))]
    ppermute x2, waiting for transfers between devices: 7.32 us -> 5.38 us  [fetch(): lo = lax.ppermute(own, Z_AXES, neighbours(16, 1, True))]
    pallas_call x10 -> x9, Pallas kernels: 24.3 us -> 22.7 us  [call(): pl.pallas_call(body, out_shape=outs, in_specs=in_specs, **{} if out_specs...]
  transfers between devices with their start and end apart: 9 -> 8, of which waited for: 6 -> 5; matrix products, arithmetic and copies ran while one was open for 0% -> 0% of each run, Pallas kernels for 2% -> 2%
where the time goes in v3:
time: 138 us; the launch traced here: 137 us
  blocking collectives  63.6 us (46%)
  starting transfers between devices  29.4 us (21%)
  Pallas kernels  24.2 us (18%)
  waiting for transfers between devices  18.8 us (14%)
    all_to_all x2, blocking collectives, fetch(): return (lo, own, hi, lax.all_to_all(mixed, 'xc', 0, 0))  24.1 us
    pallas_call x9, Pallas kernels, call(): pl.pallas_call(body, out_shape=outs, in_specs=in_specs, **{} if out_specs...  22.7 us
    all_to_all x1, blocking collectives, body(): dots = lax.all_to_all(dots, ('zh', 'zl'), 0, 0, tiled=True)  20.8 us
    all_to_all x1, blocking collectives, body(): dots = lax.all_to_all(dots, ('xc', 'yl', 'core'), 0, 0, tiled=True)  11.6 us
    ppermute x2, starting transfers between devices, fetch(): hi = lax.ppermute(own, Z_AXES, neighbours(16, -1, True))  11.6 us
    ppermute x1, starting transfers between devices, body(): right = lax.ppermute(both, Y_AXES, neighbours(4, -1, False))  9.11 us
    all_gather x1, blocking collectives, body(): both = lax.all_gather(own, 'real')  7.03 us
    ppermute x1, waiting for transfers between devices, body(): lo = lax.ppermute(up, X_AXES, neighbours(NBX, 1, False))  6.03 us
  transfers between devices with their start and end apart: 8, of which 5 were waited for; matrix products, arithmetic and copies ran while one was open for 0% of the time, Pallas kernels for 2%

profile of v3, /device:TPU:1, one launch (start us, length us, event | category | flops | bytes accessed | tf_op | source)
XLA Modules:
  0.0 136.9 jit_solution(11055738935163527754)
XLA Ops:
  0.6 1.5 %shard_map.59 = f32[4,8,8,128]{3,2,1,0:T(8,128)} custom-call(f32[8,8,128]{2,1,0:T(8,128)} %d_ref.1, s32[8,8,128]{2,1,0:T(8,128)} %v_ref.1, s32[8,8,128]{2,1,0:T(8,128)} %s_ref.1, f32[8,8,128]{2,1,0:T(8,128)} %load_ref.1), custom_call_target="tpu_custom_call" | custom-call | tf_op jit(solution)/shard_map/pallas_call | solution.py:529
  2.1 7.0 %all-gather = f32[8,8,8,128]{3,2,1,0:T(8,128)S(1)} all-gather(f32[4,8,8,128]{3,2,1,0:T(8,128)} %shard_map.59), channel_id=2, replica_groups=mesh['real'=2,'zh'=4,'zl'=4,'xc'=4,'yl'=2,'core'=2] {'real'}, dimensions={0}, use_global_device_ids=true | all-gather | bytes 393216 | tf_op jit(solution)/shard_map/all_gather | solution.py:535
  9.1 9.1 %collective-permute-start.1 = (f32[2,4,8,8,128]{4,3,2,1,0:T(8,128)S(1)}, f32[2,4,8,8,128]{4,3,2,1,0:T(8,128)S(1)}, u32[]{:S(2)}, u32[]{:S(2)}) collective-permute-start(f32[2,4,8,8,128]{4,3,2,1,0:T(8,128)S(1)} %bitcast.4), channel_id=1, source_target_pairs={{1,0},{2,1},{3,2},{5,4},{6,5},{7,6},{9,8},{10,9},{11,10},{13,12},{... | collective-permute-start | bytes 786440 | tf_op jit(solution)/shard_map/ppermute | solution.py:537
  18.3 1.9 %collective-permute-start = (f32[2,4,8,8,128]{4,3,2,1,0:T(8,128)S(1)}, f32[2,4,8,8,128]{4,3,2,1,0:T(8,128)S(1)}, u32[]{:S(2)}, u32[]{:S(2)}) collective-permute-start(f32[2,4,8,8,128]{4,3,2,1,0:T(8,128)S(1)} %bitcast.5), channel_id=1, source_target_pairs={{0,1},{1,2},{2,3},{4,5},{5,6},{6,7},{8,9},{9,10},{10,11},{12,13},{... | collective-permute-start | bytes 786440 | tf_op jit(solution)/shard_map/ppermute | solution.py:536
  20.2 0.0 collective-permute-done.1.r_ref
  20.2 3.3 %collective-permute-done.l_ref = f32[2,4,8,8,128]{4,3,2,1,0:T(8,128)S(1)} collective-permute-done((f32[2,4,8,8,128]{4,3,2,1,0:T(8,128)S(1)}, f32[2,4,8,8,128]{4,3,2,1,0:T(8,128)S(1)}, u32[]{:S(2)}, u32[]{:S(2)}) %collective-permute-start) | collective-permute-done | bytes 262176 | tf_op jit(solution)/shard_map/ppermute | solution.py:536
  23.5 0.1 shard_map.60
  23.6 1.3 collective-permute-start.2
  24.9 1.3 collective-permute-start.3
  26.2 0.1 pad_add_fusion.place_ref
  26.3 6.0 %collective-permute-done.2.lo_ref = f32[24,16,256]{2,1,0:T(8,128)S(1)} collective-permute-done((f32[24,16,256]{2,1,0:T(8,128)S(1)}, f32[24,16,256]{2,1,0:T(8,128)S(1)}, u32[]{:S(2)}, u32[]{:S(2)}) %collective-permute-start.2) | collective-permute-done | bytes 393248 | tf_op jit(solution)/shard_map/ppermute | solution.py:539
  32.3 4.1 %collective-permute-done.3.hi_ref = f32[24,16,256]{2,1,0:T(8,128)S(1)} collective-permute-done((f32[24,16,256]{2,1,0:T(8,128)S(1)}, f32[24,16,256]{2,1,0:T(8,128)S(1)}, u32[]{:S(2)}, u32[]{:S(2)}) %collective-permute-start.3) | collective-permute-done | bytes 393248 | tf_op jit(solution)/shard_map/ppermute | solution.py:540
  36.4 2.9 %shard_map.62.c_ref = f32[6,4,8,128]{3,2,1,0:T(8,128)S(1)} custom-call(s32[3]{0:T(128)S(1)} %pad_add_fusion.place_ref, f32[4,8,16,256]{3,2,1,0:T(8,128)S(1)} %get-tuple-element.20.own_ref, f32[24,16,256]{2,1,0:T(8,128)S(1)} %collective-permute-done.2.lo_ref, f32[24,16,256]{2,1,0:T(8,128)S(1)} %collective-permute-done.3.hi_ref), custom_call_target="tpu_custom_call" | custom-call | tf_op jit(solution)/shard_map/pallas_call | solution.py:497
  39.3 8.6 %collective-permute-start.5 = (f32[6,4,8,128]{3,2,1,0:T(8,128)S(1)}, f32[6,4,8,128]{3,2,1,0:T(8,128)S(1)}, u32[]{:S(2)}, u32[]{:S(2)}) collective-permute-start(f32[6,4,8,128]{3,2,1,0:T(8,128)S(1)} %shard_map.62.c_ref), channel_id=1, source_target_pairs={{0,240},{16,0},{32,16},{48,32},{64,48},{80,64},{96,80},{112,96},{1... | collective-permute-start | bytes 294920 | tf_op jit(solution)/shard_map/ppermute | solution.py:522
  47.9 1.9 %collective-permute-start.4 = (f32[6,4,8,128]{3,2,1,0:T(8,128)S(1)}, f32[6,4,8,128]{3,2,1,0:T(8,128)S(1)}, u32[]{:S(2)}, u32[]{:S(2)}) collective-permute-start(f32[6,4,8,128]{3,2,1,0:T(8,128)S(1)} %shard_map.62.c_ref), channel_id=1, source_target_pairs={{0,16},{16,32},{32,48},{48,64},{64,80},{80,96},{96,112},{112,128},... | collective-permute-start | bytes 294920 | tf_op jit(solution)/shard_map/ppermute | solution.py:521
  49.8 3.0 %shard_map.61 = (f32[3,24,16,256]{3,2,1,0:T(8,128)S(1)}, f32[3,24,16,256]{3,2,1,0:T(8,128)S(1)}, f32[24,16,256]{2,1,0:T(8,128)S(1)}, f32[3,24,16,256]{3,2,1,0:T(...) custom-call(s32[3]{0:T(128)S(1)} %pad_add_fusion.place_ref, ...), custom_call_target="tpu_custom_call" | custom-call | flops 20000000 | tf_op jit(solution)/shard_map/pallas_call | solution.py:497
  52.8 0.0 collective-permute-done.5.hi_ref
  52.8 1.6 %collective-permute-done.4.lo_ref = f32[6,4,8,128]{3,2,1,0:T(8,128)S(1)} collective-permute-done((f32[6,4,8,128]{3,2,1,0:T(8,128)S(1)}, f32[6,4,8,128]{3,2,1,0:T(8,128)S(1)}, u32[]{:S(2)}, u32[]{:S(2)}) %collective-permute-start.4) | collective-permute-done | bytes 98336 | tf_op jit(solution)/shard_map/ppermute | solution.py:521
  54.5 0.6 shard_map.63
  55.1 15.5 %all_to_all.20.mixed_ref = f32[4,2,6,4,8,128]{5,4,3,2,1,0:T(8,128)S(1)} all-to-all(f32[4,2,6,4,8,128]{5,4,3,2,1,0:T(8,128)S(1)} %shard_map.63), channel_id=1, replica_groups=mesh['real'=2,'zh'=4,'zl'=4,'xc'=4,'yl'=2,'core'=2] {'xc'}, dimensions={0} | all-to-all | bytes 1572864 | tf_op jit(solution)/shard_map/all_to_all | solution.py:524
  70.6 8.0 %shard_map.64 = (f32[6,3,36,8,128]{4,3,2,1,0:T(8,128)S(1)}, f32[6,3,18,8,128]{4,3,2,1,0:T(8,128)S(1)}, f32[6,3,9,8,128]{4,3,2,1,0:T(8,128)S(1)}, f32[3,24,16,256...) custom-call(s32[3]{0:T(128)S(1)} %pad_add_fusion.place_ref, ...), custom_call_target="tpu_custom_call" | custom-call | tf_op jit(solution)/shard_map/pallas_call | solution.py:497
  78.6 3.0 %collective-permute-start.7 = (f32[3,4,8,128]{3,2,1,0:T(8,128)S(1)}, f32[3,4,8,128]{3,2,1,0:T(8,128)S(1)}, u32[]{:S(2)}, u32[]{:S(2)}) collective-permute-start(f32[3,4,8,128]{3,2,1,0:T(8,128)S(1)} %get-tuple-element.35.c_ref), channel_id=1, source_target_pairs={{0,240},{16,0},{32,16},{48,32},{64,48},{80,64},{96,80},{112,96},{1... | collective-permute-start | bytes 147464 | tf_op jit(solution)/shard_map/ppermute | solution.py:522
  81.6 2.3 %collective-permute-start.6 = (f32[3,4,8,128]{3,2,1,0:T(8,128)S(1)}, f32[3,4,8,128]{3,2,1,0:T(8,128)S(1)}, u32[]{:S(2)}, u32[]{:S(2)}) collective-permute-start(f32[3,4,8,128]{3,2,1,0:T(8,128)S(1)} %get-tuple-element.35.c_ref), channel_id=1, source_target_pairs={{0,16},{16,32},{32,48},{48,64},{64,80},{80,96},{96,112},{112,128},... | collective-permute-start | bytes 147464 | tf_op jit(solution)/shard_map/ppermute | solution.py:521
  83.9 0.0 collective-permute-done.7.hi_ref
  83.9 3.7 %collective-permute-done.6.lo_ref = f32[3,4,8,128]{3,2,1,0:T(8,128)S(1)} collective-permute-done((f32[3,4,8,128]{3,2,1,0:T(8,128)S(1)}, f32[3,4,8,128]{3,2,1,0:T(8,128)S(1)}, u32[]{:S(2)}, u32[]{:S(2)}) %collective-permute-start.6) | collective-permute-done | bytes 49184 | tf_op jit(solution)/shard_map/ppermute | solution.py:521
  87.7 0.6 shard_map.65
  88.2 8.6 %all_to_all.21.mixed_ref = f32[4,2,3,4,8,128]{5,4,3,2,1,0:T(8,128)S(1)} all-to-all(f32[4,2,3,4,8,128]{5,4,3,2,1,0:T(8,128)S(1)} %shard_map.65), channel_id=1, replica_groups=mesh['real'=2,'zh'=4,'zl'=4,'xc'=4,'yl'=2,'core'=2] {'xc'}, dimensions={0} | all-to-all | bytes 786432 | tf_op jit(solution)/shard_map/all_to_all | solution.py:524
  96.9 5.4 %shard_map.66 = (f32[3,24,16,256]{3,2,1,0:T(8,128)S(1)}, f32[16,1,128]{2,1,0:T(1,128)S(1)}) custom-call(s32[3]{0:T(128)S(1)} %pad_add_fusion.place_ref, f32[3,24,16,256]{3,2,1,0:T(8,128)S(1)} %get-tuple-element.24.e_ref, f32[24,16,256]{2,1,0:T(8,128)S(1)} %get-tuple-element.25.refs_0_.load_ref, f32[3,24,16,256]{3,2,1,0:T(8,128)S(1)} %get-tuple-element.26.cx_ref, ...), custom_call_target="tpu_custom_call" | custom-call | tf_op jit(solution)/shard_map/pallas_call | solution.py:497
  102.3 11.6 %all_to_all.22.in_ref = f32[16,1,128]{2,1,0:T(1,128)S(1)} all-to-all(f32[16,1,128]{2,1,0:T(1,128)S(1)} %get-tuple-element.37), channel_id=1, replica_groups=mesh['real'=2,'zh'=4,'zl'=4,'xc'=4,'yl'=2,'core'=2] {'xc','yl','core'}, dimensions={0} | all-to-all | bytes 16384 | tf_op jit(solution)/shard_map/all_to_all | solution.py:567
  113.9 20.8 %all_to_all.23.dots_ref = f32[16,1,128]{2,1,0:T(1,128)S(1)} all-to-all(f32[16,1,128]{2,1,0:T(1,128)S(1)} %shard_map.67), channel_id=1, replica_groups=mesh['real'=2,'zh'=4,'zl'=4,'xc'=4,'yl'=2,'core'=2] {'zh','zl'}, dimensions={0} | all-to-all | bytes 16384 | tf_op jit(solution)/shard_map/all_to_all | solution.py:569
  134.7 2.1 %shard_map.68 = (f32[8,8,128]{2,1,0:T(8,128)}, f32[3]{0:T(128)}) custom-call(s32[3]{0:T(128)S(1)} %pad_add_fusion.place_ref, f32[3,24,16,256]{3,2,1,0:T(8,128)S(1)} %get-tuple-element.23.f_ref, f32[3,24,16,256]{3,2,1,0:T(8,128)S(1)} %get-tuple-element.30.z0_ref, f32[3,24,16,256]{3,2,1,0:T(8,128)S(1)} %get-tuple-element.36.w_ref, ...), custom_call_target="tpu_custom_call" | custom-call | tf_op jit(solution)/shard_map/pallas_call | solution.py:497
  (1 shorter events, 0.0 us)
Async XLA Ops:
  9.1 11.0 %collective-permute-start.1 = (f32[2,4,8,8,128]{4,3,2,1,0:T(8,128)S(1)}, f32[2,4,8,8,128]{4,3,2,1,0:T(8,128)S(1)}, u32[]{:S(2)}, u32[]{:S(2)}) collective-permute-start(f32[2,4,8,8,128]{4,3,2,1,0:T(8,128)S(1)} %bitcast.4), channel_id=1, source_target_pairs={{1,0},{2,1},{3,2},{5,4},{6,5},{7,6},{9,8},{10,9},{11,10},{13,12},{... | collective-permute-start | bytes 786440 | tf_op jit(solution)/shard_map/ppermute | solution.py:537
  18.3 5.2 %collective-permute-start = (f32[2,4,8,8,128]{4,3,2,1,0:T(8,128)S(1)}, f32[2,4,8,8,128]{4,3,2,1,0:T(8,128)S(1)}, u32[]{:S(2)}, u32[]{:S(2)}) collective-permute-start(f32[2,4,8,8,128]{4,3,2,1,0:T(8,128)S(1)} %bitcast.5), channel_id=1, source_target_pairs={{0,1},{1,2},{2,3},{4,5},{5,6},{6,7},{8,9},{9,10},{10,11},{12,13},{... | collective-permute-start | bytes 786440 | tf_op jit(solution)/shard_map/ppermute | solution.py:536
  23.6 8.7 %collective-permute-start.2 = (f32[24,16,256]{2,1,0:T(8,128)S(1)}, f32[24,16,256]{2,1,0:T(8,128)S(1)}, u32[]{:S(2)}, u32[]{:S(2)}) collective-permute-start(f32[24,16,256]{2,1,0:T(8,128)S(1)} %get-tuple-element.21), channel_id=1, source_target_pairs={{0,4},{4,8},{8,12},{12,16},{16,20},{20,24},{24,28},{28,32},{32,36}... | collective-permute-start | bytes 1179656 | tf_op jit(solution)/shard_map/ppermute | solution.py:539
  24.9 11.5 %collective-permute-start.3 = (f32[24,16,256]{2,1,0:T(8,128)S(1)}, f32[24,16,256]{2,1,0:T(8,128)S(1)}, u32[]{:S(2)}, u32[]{:S(2)}) collective-permute-start(f32[24,16,256]{2,1,0:T(8,128)S(1)} %get-tuple-element.22), channel_id=1, source_target_pairs={{4,0},{8,4},{12,8},{16,12},{20,16},{24,20},{28,24},{32,28},{36,32}... | collective-permute-start | bytes 1179656 | tf_op jit(solution)/shard_map/ppermute | solution.py:540
  39.3 13.5 %collective-permute-start.5 = (f32[6,4,8,128]{3,2,1,0:T(8,128)S(1)}, f32[6,4,8,128]{3,2,1,0:T(8,128)S(1)}, u32[]{:S(2)}, u32[]{:S(2)}) collective-permute-start(f32[6,4,8,128]{3,2,1,0:T(8,128)S(1)} %shard_map.62.c_ref), channel_id=1, source_target_pairs={{0,240},{16,0},{32,16},{48,32},{64,48},{80,64},{96,80},{112,96},{1... | collective-permute-start | bytes 294920 | tf_op jit(solution)/shard_map/ppermute | solution.py:522
  47.9 6.6 %collective-permute-start.4 = (f32[6,4,8,128]{3,2,1,0:T(8,128)S(1)}, f32[6,4,8,128]{3,2,1,0:T(8,128)S(1)}, u32[]{:S(2)}, u32[]{:S(2)}) collective-permute-start(f32[6,4,8,128]{3,2,1,0:T(8,128)S(1)} %shard_map.62.c_ref), channel_id=1, source_target_pairs={{0,16},{16,32},{32,48},{48,64},{64,80},{80,96},{96,112},{112,128},... | collective-permute-start | bytes 294920 | tf_op jit(solution)/shard_map/ppermute | solution.py:521
  78.6 5.3 %collective-permute-start.7 = (f32[3,4,8,128]{3,2,1,0:T(8,128)S(1)}, f32[3,4,8,128]{3,2,1,0:T(8,128)S(1)}, u32[]{:S(2)}, u32[]{:S(2)}) collective-permute-start(f32[3,4,8,128]{3,2,1,0:T(8,128)S(1)} %get-tuple-element.35.c_ref), channel_id=1, source_target_pairs={{0,240},{16,0},{32,16},{48,32},{64,48},{80,64},{96,80},{112,96},{1... | collective-permute-start | bytes 147464 | tf_op jit(solution)/shard_map/ppermute | solution.py:522
  81.6 6.0 %collective-permute-start.6 = (f32[3,4,8,128]{3,2,1,0:T(8,128)S(1)}, f32[3,4,8,128]{3,2,1,0:T(8,128)S(1)}, u32[]{:S(2)}, u32[]{:S(2)}) collective-permute-start(f32[3,4,8,128]{3,2,1,0:T(8,128)S(1)} %get-tuple-element.35.c_ref), channel_id=1, source_target_pairs={{0,16},{16,32},{32,48},{48,64},{64,80},{80,96},{96,112},{112,128},... | collective-permute-start | bytes 147464 | tf_op jit(solution)/shard_map/ppermute | solution.py:521

commit v4 on v3

v4 whole, which is shorter than its diff:
```python
import jax
import jax.numpy as jnp
from jax import lax
from jax.experimental import pallas as pl
from jax.experimental.pallas import tpu as pltpu
from jax.sharding import Mesh
from jax.sharding import PartitionSpec as P

EMIN = 0.01
BETA = 8.0
OMEGA = 0.6
ETAS = (0.7, 0.5, 0.3)
NBX = 64
VMEM_LIMIT = 16 * 1024 * 1024
F32 = jnp.float32
HI = lax.Precision.HIGHEST


GROUP = 4


def loop(first, last, step, group=None):
    group = group or GROUP
    turns = (last - first) // group

    def turn(t, _):
        for j in range(group):
            step(first + t * group + j)
        return 0

    lax.fori_loop(0, turns, turn, 0)
    for i in range(first + turns * group, last):
        step(i)


def shaped(*dims):
    return jax.ShapeDtypeStruct(dims, F32)


def rolled(v, amount, axis):
    return pltpu.roll(v, amount % v.shape[axis], axis)


def iota(shape, axis):
    return lax.broadcasted_iota(jnp.int32, shape, axis)


def pool_matrix():
    return (iota((256, 128), 0) // 2 == iota((256, 128), 1)).astype(F32)


def widen_matrix():
    return (iota((128, 256), 1) // 2 == iota((128, 256), 0)).astype(F32)


def y_edges(rows, stride):
    y = iota((rows, 1), 0)
    low = (y >= stride).astype(F32)
    outer = 0.5 * ((y < stride).astype(F32) + (y >= rows - stride).astype(F32))
    return low, outer


def inverse(e, diag):
    return jnp.where(e > 0.0, 1.0 / jnp.where(e > 0.0, diag, 1.0), 0.0)


def prepare(e_ref, level, first, last):
    cx_ref, cy_ref, cyp_ref, cz_ref, czp_ref, diag_ref, inv_ref = level
    low, outer = y_edges(16, 1)

    def step(i):
        for r in range(3):
            e = e_ref[r, i]
            h = 0.5 * e
            cx, cxp = h + 0.5 * e_ref[r, i - 1], h + 0.5 * e_ref[r, i + 1]
            cy, cz = low * (h + rolled(h, 1, 0)), h + rolled(h, 1, 1)
            cyp, czp = rolled(cy, -1, 0), rolled(cz, -1, 1)
            diag = (cx + cxp) + (cy + cyp) + (cz + czp) + outer * e
            for ref, v in zip(level, (cx, cy, cyp, cz, czp, diag, inverse(e, diag))):
                ref[r, i] = v

    loop(first, last, step)
    for r in range(3):
        cx_ref[r, last] = 0.5 * (e_ref[r, last] + e_ref[r, last - 1])


def pull(u_ref, i, r, level):
    cx_ref, cy_ref, cyp_ref, cz_ref, czp_ref = level[:5]
    u = u_ref[r, i]
    total = cx_ref[r, i] * u_ref[r, i - 1] + cx_ref[r, i + 1] * u_ref[r, i + 1]
    total = total + (cy_ref[r, i] * rolled(u, 1, 0) + cyp_ref[r, i] * rolled(u, -1, 0))
    return total + (cz_ref[r, i] * rolled(u, 1, 1) + czp_ref[r, i] * rolled(u, -1, 1))


KEEP = 1.0 - OMEGA


def pool_own(src_of, many, big_ref, half_ref, scale):
    for f in range(many):
        for k in range(4):
            at = (f * 4 + k) * 16
            big_ref[at : at + 16, :] = (0.125 * scale) * (src_of(f, 8 + 2 * k) + src_of(f, 9 + 2 * k))
    rows = many * 64
    half_ref[0:rows, :] = jnp.dot(big_ref[0:rows, :], pool_matrix(), precision=HI, preferred_element_type=F32)
    return half_ref[pl.ds(0, rows // 2, stride=2), :] + half_ref[pl.ds(1, rows // 2, stride=2), :]


def stack_level(e, stride):
    low, outer = y_edges(8, stride)
    h = 0.5 * e
    mid = h[1:-1]
    cx, cxp = mid + h[:-2], mid + h[2:]
    cy, cz = low * (mid + rolled(mid, stride, 1)), mid + rolled(mid, stride, 2)
    cyp, czp = rolled(cy, -stride, 1), rolled(cz, -stride, 2)
    diag = (cx + cxp) + (cy + cyp) + (cz + czp) + outer * e[1:-1]
    return cx, cxp, cy, cyp, cz, czp, inverse(e[1:-1], diag)


def stack_pull(level, u, stride, first, last):
    cx, cxp, cy, cyp, cz, czp = (v[first:last] for v in level[:6])
    mid = u[1:-1]
    total = cx * u[:-2] + cxp * u[2:]
    total = total + (cy * rolled(mid, stride, 1) + cyp * rolled(mid, -stride, 1))
    return total + (cz * rolled(mid, stride, 2) + czp * rolled(mid, -stride, 2))


def stack_pool(v, stride):
    n = v.shape[0] // 2
    v = v.reshape(n, 2, 8, 128)
    v = v[:, 0] + v[:, 1]
    y = iota((1, 8, 1), 1)
    v = v + jnp.where((y // stride) % 2 == 0, rolled(v, -stride, 1), rolled(v, stride, 1))
    z = iota((1, 1, 128), 2)
    v = v + jnp.where((z // stride) % 2 == 0, rolled(v, -stride, 2), rolled(v, stride, 2))
    return 0.125 * v


def twice(v):
    n = v.shape[0]
    return jnp.broadcast_to(v[:, None], (n, 2, 8, 128)).reshape(2 * n, 8, 128)


STRIDES = (1, 2, 4)


def set_levels(e1_ref, level_refs):
    for r in range(3):
        e = e1_ref[r]
        for ref, stride in zip(level_refs, STRIDES):
            for q, v in enumerate(stack_level(e, stride)):
                ref[q, r, 1 : 1 + v.shape[0]] = v
            e = 0.25 * stack_pool(e, stride) if stride < 4 else e


def coarse(levels, rhs1, first, last):
    one, two, three = levels
    x1 = OMEGA * rhs1[1:35] * one[6][1:35]
    rhs2 = stack_pool(KEEP * rhs1[2:34] + stack_pull(one, x1, 1, 2, 34), 1)
    x2 = OMEGA * rhs2 * two[6][1:17]
    rhs3 = stack_pool(KEEP * rhs2[1:15] + stack_pull(two, x2, 2, 2, 16), 2)
    x3 = OMEGA * rhs3 * three[6][1:8]
    x3 = KEEP * x3[1:6] + OMEGA * three[6][2:7] * (rhs3[1:6] + stack_pull(three, x3, 4, 2, 7))
    x2 = x2[3:13] + twice(x3)
    x2 = KEEP * x2[1:9] + OMEGA * two[6][5:13] * (rhs2[4:12] + stack_pull(two, x2, 2, 5, 13))
    x1 = x1[9:25] + twice(x2)
    x1, at = x1[first - 11 : last - 9], slice(first, last)
    return KEEP * x1[1:-1] + OMEGA * one[6][at] * (rhs1[at] + stack_pull(one, x1, 1, first, last))


def coarse_all(level_refs, rhs1_ref, out_ref, first, last):
    for r in range(3):
        levels = [[ref[q, r] for q in range(7)] for ref in level_refs]
        out_ref[r] = coarse(levels, rhs1_ref[r], first, last)


def widen_into(e1_ref, count, wide_ref):
    rows = 3 * count * 8
    src = jnp.concatenate([e1_ref[r, :count].reshape(count * 8, 128) for r in range(3)], 0)
    wide = jnp.dot(src, widen_matrix(), precision=HI, preferred_element_type=F32)
    for h in range(2):
        part = wide[:, 128 * h : 128 * h + 128]
        wide_ref[h, pl.ds(0, rows, stride=2), :] = part
        wide_ref[h, pl.ds(1, rows, stride=2), :] = part


def widened(wide_ref, r, k, count):
    at = pl.multiple_of((r * count + k) * 16, 16)
    return jnp.concatenate([wide_ref[0, pl.ds(at, 16), :], wide_ref[1, pl.ds(at, 16), :]], 1)


REACH = (7, 6, 6, 5)
OFFS = (0, 7, 13, 19)


def pack_kernel(d_ref, v_ref, s_ref, load_ref, out_ref, v_in, s_in, sems):
    pairs = ((d_ref, out_ref.at[0]), (v_ref, v_in), (s_ref, s_in), (load_ref, out_ref.at[3]))
    copies = [pltpu.make_async_copy(src, dst, sems.at[q]) for q, (src, dst) in enumerate(pairs)]
    for copy in copies:
        copy.start()
    copies[1].wait()
    out_ref[1] = v_in[...].astype(F32)
    copies[2].wait()
    out_ref[2] = s_in[...].astype(F32)
    copies[0].wait()
    copies[3].wait()


def select_kernel(place_ref, c_ref, a_ref, b_ref, own_ref, up_ref, down_ref):
    right = (iota((8, 128), 1) < 64) == (place_ref[1] % 2 == 0)
    for f in range(4):
        for i in range(8):
            for h in range(2):
                halo = jnp.where(right, a_ref[h, f, i], b_ref[h, f, i])
                piece = jnp.concatenate([c_ref[h, f, i], halo], 1)
                own_ref[f, i, 8 * h : 8 * h + 8, :] = piece
                if i >= 8 - REACH[f]:
                    up_ref[OFFS[f] + i - (8 - REACH[f]), 8 * h : 8 * h + 8, :] = piece
                if i < REACH[f]:
                    down_ref[OFFS[f] + i, 8 * h : 8 * h + 8, :] = piece


def spread_out(own_ref, lo_ref, hi_ref, refs):
    for f, (ref, n) in enumerate(zip(refs, REACH)):
        ref[8 - n : 8] = lo_ref[OFFS[f] : OFFS[f] + n]
        ref[8:16] = own_ref[f]
        ref[16 : 16 + n] = hi_ref[OFFS[f] : OFFS[f] + n]


def stiffness(place_ref, d_ref, v_ref, s_ref, e_ref, f_ref, first, last):
    block, gy = place_ref[0], place_ref[1]
    lane = iota((1, 256), 1)
    z = gy * 128 + jnp.where(lane < 192, lane, lane - 256)
    z_in = ((z >= 0) & (z < 512)).astype(F32)
    z_count = ((z >= 1) & (z < 513)).astype(F32) + ((z >= -1) & (z < 511)).astype(F32)
    y = iota((16, 1), 0)
    low, high = (y >= 1).astype(F32), (y < 15).astype(F32)
    yz_count = (low + high) + z_count
    shifts = []
    for eta in ETAS:
        t0 = jnp.tanh(jnp.full((1, 1), BETA * eta, F32))
        shifts.append((t0, 1.0 / (t0 + jnp.tanh(jnp.full((1, 1), BETA * (1.0 - eta), F32)))))

    def step(i):
        x = 8 * block + i - 8
        inside = lambda at: ((at >= 0) & (at < 8 * NBX)).astype(F32)
        d = d_ref[i]
        total = 2.0 * d + d_ref[i + 1] + d_ref[i - 1]
        total = total + low * rolled(d, 1, 0) + high * rolled(d, -1, 0) + rolled(d, 1, 1) + rolled(d, -1, 1)
        weight = 1.0 / (yz_count + (2.0 + inside(x - 1) + inside(x + 1)))
        here = z_in * inside(x)
        filtered = total * weight
        void, solid = v_ref[i], s_ref[i]
        open_ = 1.0 - void
        scale = here * (open_ * (1.0 - solid)) * weight
        for r, eta in enumerate(ETAS):
            t0, den = shifts[r]
            t = jnp.tanh(BETA * (filtered - eta))
            projected = (t0 + t) * den
            physical = open_ * (solid + (1.0 - solid) * projected)
            square = physical * physical
            e_ref[r, i] = here * (EMIN + (1.0 - EMIN) * (square * physical))
            if f_ref is not None:
                slope = BETA * (1.0 - t * t) * den
                f_ref[r, i] = (3.0 * (1.0 - EMIN)) * square * scale * slope

    loop(first, last, step)


def first_kernel(
    place_ref, own_ref, lo_ref, hi_ref, g_ref,
    d_ref, v_ref, s_ref, load_ref, e_ref, x_ref, rest_ref, big_ref, half_ref, *level,
):
    spread_out(own_ref, lo_ref, hi_ref, (d_ref, v_ref, s_ref, load_ref))
    stiffness(place_ref, d_ref, v_ref, s_ref, e_ref, None, 6, 18)
    prepare(e_ref, level, 7, 17)

    def start(i):
        for r in range(3):
            x_ref[r, i] = OMEGA * load_ref[i] * level[6][r, i]

    loop(7, 17, start)

    def leftover(i):
        for r in range(3):
            rest_ref[r, i - 8] = KEEP * load_ref[i] + pull(x_ref, i, r, level)

    loop(8, 16, leftover)
    g_ref[0:3] = pool_own(lambda f, i: rest_ref[f, i - 8], 3, big_ref, half_ref, 1.0).reshape(3, 4, 8, 128)
    g_ref[3:6] = pool_own(lambda f, i: e_ref[f, i], 3, big_ref, half_ref, 0.25).reshape(3, 4, 8, 128)


def wide_kernel(
    place_ref, own_ref, lo_ref, hi_ref, f_ref, load_ref, *refs,
):
    level, (d_ref, v_ref, s_ref, e_ref) = refs[:7], refs[7:]
    spread_out(own_ref, lo_ref, hi_ref, (d_ref, v_ref, s_ref, load_ref))
    stiffness(place_ref, d_ref, v_ref, s_ref, e_ref, f_ref, 2, 22)
    prepare(e_ref, level, 3, 21)


def mix_kernel(place_ref, c_ref, even_ref, odd_ref, *refs):
    out_ref = refs[-1]
    mine, even = place_ref[0] % 4, (place_ref[0] // 4) % 2 == 0
    for to in range(4):
        out_ref[to, 0] = c_ref[...]
        out_ref[to, 1] = jnp.where((mine > to) == even, odd_ref[...], even_ref[...])


def window(place_ref, c_ref, even_ref, odd_ref, mixed_ref, first, into_ref):
    block = place_ref[0]
    mine, even = block % 4, (block // 4) % 2 == 0
    for b in range(9):
        at = block - 4 + b
        keep = ((at >= 0) & (at < NBX)).astype(F32)
        source = mine + (b - 4)
        for r in range(3):
            if b == 0:
                piece = jnp.where(even, odd_ref[first + r], even_ref[first + r])
            elif b == 4:
                piece = c_ref[first + r]
            elif b == 8:
                piece = jnp.where(even, even_ref[first + r], odd_ref[first + r])
            else:
                far = ((source < 0) | (source > 3)).astype(jnp.int32)
                piece = mixed_ref[(source + 4) % 4, far, first + r]
            into_ref[r, 4 * b : 4 * b + 4] = keep * piece


def second_kernel(place_ref, load_ref, *refs):
    level, (c_ref, even_ref, odd_ref, mixed_ref) = refs[:7], refs[7:11]
    one_ref, two_ref, three_ref, z0_ref, q0_ref, g_ref = refs[11:17]
    e1_ref, x_ref, y_ref, rhs_ref, out1_ref, wide_ref, big_ref, half_ref = refs[17:]
    diag_ref, inv_ref = level[5:]
    got = (place_ref, c_ref, even_ref, odd_ref, mixed_ref)
    window(*got, 3, e1_ref)
    window(*got, 0, rhs_ref)
    levels = (one_ref, two_ref, three_ref)
    set_levels(e1_ref, levels)
    coarse_all(levels, rhs_ref, out1_ref, 13, 23)
    widen_into(out1_ref, 10, wide_ref)

    def start(i):
        for r in range(3):
            x_ref[r, i] = OMEGA * load_ref[i] * inv_ref[r, i] + widened(wide_ref, r, (i - 2) // 2, 10)

    loop(3, 21, start)

    def smooth(i):
        for r in range(3):
            near = load_ref[i] + pull(x_ref, i, r, level)
            z0_ref[r, i] = KEEP * x_ref[r, i] + OMEGA * near * inv_ref[r, i]

    loop(4, 20, smooth)

    def apply(i):
        for r in range(3):
            image = diag_ref[r, i] * z0_ref[r, i] - pull(z0_ref, i, r, level)
            q0_ref[r, i] = image
            y_ref[r, i] = OMEGA * image * inv_ref[r, i]

    loop(5, 19, apply)

    def leftover(i):
        for r in range(3):
            x_ref[r, i] = KEEP * q0_ref[r, i] + pull(y_ref, i, r, level)

    loop(8, 16, leftover)
    g_ref[...] = pool_own(lambda f, i: x_ref[f, i], 3, big_ref, half_ref, 1.0).reshape(3, 4, 8, 128)


def third_kernel(place_ref, load_ref, *refs):
    level, (one_ref, two_ref, three_ref, z0_ref, q0_ref, c_ref, even_ref, odd_ref, mixed_ref) = refs[:7], refs[7:16]
    w_ref, dots_ref, x_ref, rhs_ref, out1_ref, wide_ref = refs[16:]
    diag_ref, inv_ref = level[5:]
    window(place_ref, c_ref, even_ref, odd_ref, mixed_ref, 0, rhs_ref)
    coarse_all((one_ref, two_ref, three_ref), rhs_ref, out1_ref, 14, 22)
    widen_into(out1_ref, 8, wide_ref)

    def start(i):
        for r in range(3):
            x_ref[r, i] = OMEGA * q0_ref[r, i] * inv_ref[r, i] + widened(wide_ref, r, (i - 4) // 2, 8)

    loop(5, 19, start)

    def smooth(i):
        for r in range(3):
            near = q0_ref[r, i] + pull(x_ref, i, r, level)
            w_ref[r, i] = KEEP * x_ref[r, i] + OMEGA * near * inv_ref[r, i]

    loop(6, 18, smooth)

    def add(t, sums):
        sums = list(sums)
        for i in (8 + 2 * t, 9 + 2 * t):
            for r in range(3):
                image = (diag_ref[r, i] * w_ref[r, i] - pull(w_ref, i, r, level))[:, :128]
                b, z0, q0, w = load_ref[i, :, :128], z0_ref[r, i, :, :128], q0_ref[r, i, :, :128], w_ref[r, i, :, :128]
                for q, term in enumerate((b * z0, z0 * q0, b * w, q0 * w, w * image)):
                    sums[r * 5 + q] = sums[r * 5 + q] + (term[:8] + term[8:])
        return tuple(sums)

    sums = lax.fori_loop(0, 4, add, tuple(jnp.zeros((8, 128), F32) for _ in range(15)))
    lane = iota((1, 128), 1)
    row = jnp.zeros((1, 128), F32)
    for q, v in enumerate(sums):
        row = row + jnp.where(lane == q, jnp.sum(jnp.sum(v, 0, keepdims=True), 1, keepdims=True), 0.0)
    dots_ref[...] = jnp.broadcast_to(row[None], (16, 1, 128))


def sum_kernel(in_ref, out_ref):
    out_ref[...] = jnp.broadcast_to(jnp.sum(in_ref[...], 0, keepdims=True), (16, 1, 128))


def last_kernel(place_ref, f_ref, z0_ref, w_ref, dots_ref, sens_ref, comp_ref, u_ref, comb_ref):
    real = place_ref[2]
    totals = jnp.sum(dots_ref[...], 0)
    lane = iota((1, 128), 1)
    pick = lambda q: jnp.sum(jnp.where(lane == q, totals, 0.0), 1, keepdims=True)
    factors = []
    for r in range(3):
        bz, zq, bw, qw, wa = (pick(r * 5 + q) for q in range(5))
        a0 = bz / zq
        rz1 = bz - a0 * bw - a0 * zq + (a0 * a0) * qw
        grow = 1.0 + rz1 / bz
        a1 = rz1 / ((grow * grow) * zq - 2.0 * (a0 * grow) * qw + (a0 * a0) * wa)
        c0, c1 = a0 + a1 * grow, -(a1 * a0)
        factors.append((c0, c1))
        comp_ref[r] = jnp.sum(c0 * bz + c1 * bw)
    y = iota((16, 1), 0)
    low, high = (y >= 1).astype(F32), (y < 15).astype(F32)

    def state(i):
        for r in range(3):
            u_ref[r, i] = factors[r][0] * z0_ref[r, i] + factors[r][1] * w_ref[r, i]

    loop(6, 18, state)

    def energy(i):
        total = jnp.zeros((16, 256), F32)
        for r in range(3):
            u = u_ref[r, i]
            gaps = (
                u - u_ref[r, i - 1],
                u - u_ref[r, i + 1],
                u - low * rolled(u, 1, 0),
                u - high * rolled(u, -1, 0),
                u - rolled(u, 1, 1),
                u - rolled(u, -1, 1),
            )
            square = gaps[0] * gaps[0]
            for gap in gaps[1:]:
                square = square + gap * gap
            total = total - (0.5 * square) * f_ref[r, i]
        comb_ref[i] = total

    loop(7, 17, energy)

    def spread(i):
        c = comb_ref[i]
        total = 2.0 * c + comb_ref[i + 1] + comb_ref[i - 1]
        total = total + low * rolled(c, 1, 0) + high * rolled(c, -1, 0) + rolled(c, 1, 1) + rolled(c, -1, 1)
        sens_ref[i - 8] = jnp.where(real == 0, total[:8, :128], total[8:, :128])

    loop(8, 16, spread)


def call(body, outs, scratch, *args, place=False, flops=0, out_specs=None):
    if place:
        inner = body

        def body(*refs):
            return inner((lax.axis_index(X_AXES), lax.axis_index(Y_AXES), lax.axis_index("real")), *refs)

    return pl.pallas_call(
        body,
        out_shape=outs,
        in_specs=[pl.BlockSpec(memory_space=pltpu.VMEM)] * len(args),
        **({} if out_specs is None else {"out_specs": out_specs}),
        scratch_shapes=[pltpu.VMEM(dims, F32) for dims in scratch],
        compiler_params=pltpu.CompilerParams(vmem_limit_bytes=VMEM_LIMIT),
        cost_estimate=pl.CostEstimate(flops=flops, bytes_accessed=0, transcendentals=0),
    )(*args)


Z_AXES = ("zh", "zl")
X_AXES = ("zh", "zl", "xc")
Y_AXES = ("yl", "core")
FIELD = (3, 24, 16, 256)
LEVEL1 = (3, 36, 8, 128)
SLICES = (24, 16, 256)


def swap(to_even, to_odd, axes, count):
    got = []
    for first, v in ((0, to_even), (1, to_odd)):
        pairs = [(i, i + 1) for i in range(first, count - 1, 2)]
        got.append(lax.ppermute(v, axes, pairs + [(j, i) for i, j in pairs]))
    return got


def fetch(own, *after):
    even, odd = swap(own, own, Z_AXES, 16)
    mixed = call(mix_kernel, shaped(4, 2, *own.shape), [], own, even, odd, *after, place=True)
    return own, even, odd, lax.all_to_all(mixed, "xc", 0, 0)


def body(design, load, void_mask, solid_mask):
    own = pl.pallas_call(
        pack_kernel,
        out_shape=shaped(4, 8, 8, 128),
        in_specs=[pl.BlockSpec(memory_space=pl.ANY)] * 4,
        scratch_shapes=[pltpu.VMEM((8, 8, 128), jnp.int32)] * 2 + [pltpu.SemaphoreType.DMA((4,))],
    )(design, void_mask, solid_mask, load)
    both = lax.all_gather(own, "real")
    outs = (shaped(4, 8, 16, 256), shaped(*SLICES), shaped(*SLICES))
    mine, up, down = call(select_kernel, outs, [], both, *swap(both, both, Y_AXES, 4), place=True)
    lo = lax.ppermute(up, X_AXES, [(i, i + 1) for i in range(NBX - 1)])
    hi = lax.ppermute(down, X_AXES, [(i + 1, i) for i in range(NBX - 1)])
    g = call(
        first_kernel,
        shaped(6, 4, 8, 128),
        [SLICES] * 4 + [FIELD] * 2 + [(3, 8, 16, 256), (192, 256), (192, 128)] + [FIELD] * 7,
        mine, lo, hi, place=True,
    )
    f, *level0 = call(
        wide_kernel,
        (shaped(*FIELD), shaped(*SLICES)) + (shaped(*FIELD),) * 7,
        [SLICES] * 3 + [FIELD],
        mine, lo, hi, place=True, flops=2 * 10**7,
    )
    levels = tuple(shaped(7, 3, n, 8, 128) for n in (36, 18, 9))
    *levels, z0, q0, g2 = call(
        second_kernel,
        levels + (shaped(*FIELD), shaped(*FIELD), shaped(3, 4, 8, 128)),
        [LEVEL1, FIELD, FIELD, LEVEL1, (3, 10, 8, 128), (2, 480, 128), (192, 256), (192, 128)],
        *level0, *fetch(g, level0[0]), place=True,
    )
    w, dots = call(
        third_kernel,
        (shaped(*FIELD), shaped(16, 1, 128)),
        [FIELD, LEVEL1, (3, 8, 8, 128), (2, 384, 128)],
        *level0, *levels, z0, q0, *fetch(g2), place=True,
    )
    dots = lax.all_to_all(dots, ("xc", "yl", "core"), 0, 0, tiled=True)
    dots = call(sum_kernel, shaped(16, 1, 128), [], dots)
    dots = lax.all_to_all(dots, ("zh", "zl"), 0, 0, tiled=True)
    return call(
        last_kernel,
        (shaped(8, 8, 128), shaped(3)),
        [FIELD, SLICES],
        f, z0, w, dots, place=True,
        out_specs=(pl.BlockSpec(memory_space=pltpu.VMEM), pl.BlockSpec(memory_space=pltpu.SMEM)),
    )


def solution(mesh):
    split = Mesh(mesh.devices.reshape(2, 4, 4, 4, 2, 2), ("real", "zh", "zl", "xc", "yl", "core"))
    spec = P(X_AXES, "real", Y_AXES)
    return jax.shard_map(body, mesh=split, in_specs=(spec,) * 4, out_specs=(spec, P()), check_vma=False)
```

time: 138 us -> 127 us (0.920)
  Pallas kernels: 24.2 us -> 15.2 us
  waiting for transfers between devices: 18.8 us -> 13.7 us
  blocking collectives: 63.6 us -> 68.5 us
    pallas_call x9, Pallas kernels: 22.7 us -> 13.8 us  [call(): pl.pallas_call(body, out_shape=outs, in_specs=[pl.BlockSpec(memory_space=...]
    ppermute x8, waiting for transfers between devices: 18.8 us -> 13.7 us  [the longest x1 7.24 us: body(): lo = lax.ppermute(up, X_AXES, [(i, i + 1) for i in range(NBX - 1)])]
    all_to_all x1, blocking collectives: 20.8 us -> 23.5 us  [body(): dots = lax.all_to_all(dots, ('zh', 'zl'), 0, 0, tiled=True)]
  transfers between devices with their start and end apart: 8 -> 8, of which waited for: 5 -> 4; matrix products, arithmetic and copies ran while one was open for 0% -> 0% of each run, Pallas kernels for 2% -> 2%
where the time goes in v4:
time: 127 us
  blocking collectives  68.5 us (54%)
  starting transfers between devices  28.5 us (22%)
  Pallas kernels  15.2 us (12%)
  waiting for transfers between devices  13.7 us (11%)
    ppermute x6, starting transfers between devices, swap(): got.append(lax.ppermute(v, axes, pairs + [(j, i) for i, j in pairs]))  25.7 us
    all_to_all x2, blocking collectives, fetch(): return (own, even, odd, lax.all_to_all(mixed, 'xc', 0, 0))  25.2 us
    all_to_all x1, blocking collectives, body(): dots = lax.all_to_all(dots, ('zh', 'zl'), 0, 0, tiled=True)  23.5 us
    pallas_call x9, Pallas kernels, call(): pl.pallas_call(body, out_shape=outs, in_specs=[pl.BlockSpec(memory_space=...  13.8 us
    all_to_all x1, blocking collectives, body(): dots = lax.all_to_all(dots, ('xc', 'yl', 'core'), 0, 0, tiled=True)  12.8 us
    ppermute x1, waiting for transfers between devices, body(): lo = lax.ppermute(up, X_AXES, [(i, i + 1) for i in range(NBX - 1)])  7.24 us
    all_gather x1, blocking collectives, body(): both = lax.all_gather(own, 'real')  7.03 us
    ppermute x1, waiting for transfers between devices, body(): hi = lax.ppermute(down, X_AXES, [(i + 1, i) for i in range(NBX - 1)])  3.82 us
  transfers between devices with their start and end apart: 8, of which 4 were waited for; matrix products, arithmetic and copies ran while one was open for 0% of the time, Pallas kernels for 2%

profile of v4, /device:TPU:1, one launch (start us, length us, event | category | flops | bytes accessed | tf_op | source)
XLA Modules:
  0.0 126.6 jit_solution(5249200212510019295)
XLA Ops:
  0.6 1.5 %shard_map.59 = f32[4,8,8,128]{3,2,1,0:T(8,128)} custom-call(f32[8,8,128]{2,1,0:T(8,128)} %d_ref.1, s32[8,8,128]{2,1,0:T(8,128)} %v_ref.1, s32[8,8,128]{2,1,0:T(8,128)} %s_ref.1, f32[8,8,128]{2,1,0:T(8,128)} %load_ref.1), custom_call_target="tpu_custom_call" | custom-call | tf_op jit(solution)/shard_map/pallas_call | solution.py:508
  2.1 7.0 %all-gather = f32[8,8,8,128]{3,2,1,0:T(8,128)S(1)} all-gather(f32[4,8,8,128]{3,2,1,0:T(8,128)} %shard_map.59), channel_id=2, replica_groups=mesh['real'=2,'zh'=4,'zl'=4,'xc'=4,'yl'=2,'core'=2] {'real'}, dimensions={0}, use_global_device_ids=true | all-gather | bytes 393216 | tf_op jit(solution)/shard_map/all_gather | solution.py:514
  9.1 5.2 %collective-permute-start.1 = (f32[2,4,8,8,128]{4,3,2,1,0:T(8,128)S(1)}, f32[2,4,8,8,128]{4,3,2,1,0:T(8,128)S(1)}, u32[]{:S(2)}, u32[]{:S(2)}) collective-permute-start(f32[2,4,8,8,128]{4,3,2,1,0:T(8,128)S(1)} %bitcast.1), channel_id=1, source_target_pairs={{1,2},{2,1},{5,6},{6,5},{9,10},{10,9},{13,14},{14,13},{17,18},{18,... | collective-permute-start | bytes 786440 | tf_op jit(solution)/shard_map/ppermute | solution.py:497
  14.3 4.6 %collective-permute-start = (f32[2,4,8,8,128]{4,3,2,1,0:T(8,128)S(1)}, f32[2,4,8,8,128]{4,3,2,1,0:T(8,128)S(1)}, u32[]{:S(2)}, u32[]{:S(2)}) collective-permute-start(f32[2,4,8,8,128]{4,3,2,1,0:T(8,128)S(1)} %bitcast.2), channel_id=1, source_target_pairs={{0,1},{2,3},{1,0},{3,2},{4,5},{6,7},{5,4},{7,6},{8,9},{10,11},{9,8... | collective-permute-start | bytes 786440 | tf_op jit(solution)/shard_map/ppermute | solution.py:497
  18.9 0.0 collective-permute-done.1.refs_2_
  19.0 1.1 collective-permute-done.refs_1_
  20.1 0.1 shard_map.60
  20.2 1.4 %collective-permute-start.2 = (f32[24,16,256]{2,1,0:T(8,128)S(1)}, f32[24,16,256]{2,1,0:T(8,128)S(1)}, u32[]{:S(2)}, u32[]{:S(2)}) collective-permute-start(f32[24,16,256]{2,1,0:T(8,128)S(1)} %get-tuple-element.23), channel_id=1, source_target_pairs={{0,4},{4,8},{8,12},{12,16},{16,20},{20,24},{24,28},{28,32},{32,36}... | collective-permute-start | bytes 1179656 | tf_op jit(solution)/shard_map/ppermute | solution.py:517
  21.6 1.3 %collective-permute-start.3 = (f32[24,16,256]{2,1,0:T(8,128)S(1)}, f32[24,16,256]{2,1,0:T(8,128)S(1)}, u32[]{:S(2)}, u32[]{:S(2)}) collective-permute-start(f32[24,16,256]{2,1,0:T(8,128)S(1)} %get-tuple-element.24), channel_id=1, source_target_pairs={{4,0},{8,4},{12,8},{16,12},{20,16},{24,20},{28,24},{32,28},{36,32}... | collective-permute-start | bytes 1179656 | tf_op jit(solution)/shard_map/ppermute | solution.py:518
  22.9 7.2 %collective-permute-done.2.refs_1_ = f32[24,16,256]{2,1,0:T(8,128)S(1)} collective-permute-done((f32[24,16,256]{2,1,0:T(8,128)S(1)}, f32[24,16,256]{2,1,0:T(8,128)S(1)}, u32[]{:S(2)}, u32[]{:S(2)}) %collective-permute-start.2) | collective-permute-done | bytes 393248 | tf_op jit(solution)/shard_map/ppermute | solution.py:517
  30.2 3.8 %collective-permute-done.3.refs_2_ = f32[24,16,256]{2,1,0:T(8,128)S(1)} collective-permute-done((f32[24,16,256]{2,1,0:T(8,128)S(1)}, f32[24,16,256]{2,1,0:T(8,128)S(1)}, u32[]{:S(2)}, u32[]{:S(2)}) %collective-permute-start.3) | collective-permute-done | bytes 393248 | tf_op jit(solution)/shard_map/ppermute | solution.py:518
  34.0 2.2 %shard_map.62.refs_0_.refs_8_ = f32[6,4,8,128]{3,2,1,0:T(8,128)S(1)} custom-call(f32[4,8,16,256]{3,2,1,0:T(8,128)S(1)} %get-tuple-element.22.refs_0_, f32[24,16,256]{2,1,0:T(8,128)S(1)} %collective-permute-done.2.refs_1_, f32[24,16,256]{2,1,0:T(8,128)S(1)} %collective-permute-done.3.refs_2_), custom_call_target="tpu_custom_call" | custom-call | tf_op jit(solution)/shard_map/pallas_call | solution.py:474
  36.2 0.7 collective-permute-start.5
  36.9 7.0 %collective-permute-start.4 = (f32[6,4,8,128]{3,2,1,0:T(8,128)S(1)}, f32[6,4,8,128]{3,2,1,0:T(8,128)S(1)}, u32[]{:S(2)}, u32[]{:S(2)}) collective-permute-start(f32[6,4,8,128]{3,2,1,0:T(8,128)S(1)} %shard_map.62.refs_0_.refs_8_), channel_id=1, source_target_pairs={{0,16},{32,48},{64,80},{96,112},{128,144},{160,176},{192,208},{224... | collective-permute-start | bytes 294920 | tf_op jit(solution)/shard_map/ppermute | solution.py:497
  43.9 2.4 %shard_map.61 = (f32[3,24,16,256]{3,2,1,0:T(8,128)S(1)}, f32[24,16,256]{2,1,0:T(8,128)S(1)}, f32[3,24,16,256]{3,2,1,0:T(8,128)S(1)}, f32[3,24,16,256]{3,2,1,0:T(...) custom-call(f32[4,8,16,256]{3,2,1,0:T(8,128)S(1)} %get-tuple-element, ...), custom_call_target="tpu_custom_call" | custom-call | flops 20000000 | tf_op jit(solution)/shard_map/pallas_call | solution.py:474
  46.3 0.0 collective-permute-done.5.refs_2_.refs_10_
  46.3 0.0 collective-permute-done.4.refs_1_.refs_9_
  46.3 0.1 shard_map.63
  46.4 16.5 %all_to_all.20.refs_11_ = f32[4,2,6,4,8,128]{5,4,3,2,1,0:T(8,128)S(1)} all-to-all(f32[4,2,6,4,8,128]{5,4,3,2,1,0:T(8,128)S(1)} %shard_map.63), channel_id=1, replica_groups=mesh['real'=2,'zh'=4,'zl'=4,'xc'=4,'yl'=2,'core'=2] {'xc'}, dimensions={0} | all-to-all | bytes 1572864 | tf_op jit(solution)/shard_map/all_to_all | solution.py:504
  62.9 4.9 %shard_map.64 = (f32[7,3,36,8,128]{4,3,2,1,0:T(8,128)S(1)}, f32[7,3,18,8,128]{4,3,2,1,0:T(8,128)S(1)}, f32[7,3,9,8,128]{4,3,2,1,0:T(8,128)S(1)}, f32[3,24,16,256...) custom-call(f32[24,16,256]{2,1,0:T(8,128)S(1)} %get-tuple-element.26.refs_3_.refs_0_, ...), custom_call_target="tpu_custom_call" | custom-call | tf_op jit(solution)/shard_map/pallas_call | solution.py:474
  67.8 0.7 collective-permute-start.7
  68.5 7.6 %collective-permute-start.6 = (f32[3,4,8,128]{3,2,1,0:T(8,128)S(1)}, f32[3,4,8,128]{3,2,1,0:T(8,128)S(1)}, u32[]{:S(2)}, u32[]{:S(2)}) collective-permute-start(f32[3,4,8,128]{3,2,1,0:T(8,128)S(1)} %get-tuple-element.39.refs_0_.refs_13_), channel_id=1, source_target_pairs={{0,16},{32,48},{64,80},{96,112},{128,144},{160,176},{192,208},{224... | collective-permute-start | bytes 147464 | tf_op jit(solution)/shard_map/ppermute | solution.py:497
  76.1 0.0 collective-permute-done.7.refs_2_.refs_15_
  76.2 1.5 %collective-permute-done.6.refs_1_.refs_14_ = f32[3,4,8,128]{3,2,1,0:T(8,128)S(1)} collective-permute-done((f32[3,4,8,128]{3,2,1,0:T(8,128)S(1)}, f32[3,4,8,128]{3,2,1,0:T(8,128)S(1)}, u32[]{:S(2)}, u32[]{:S(2)}) %collective-permute-start.6) | collective-permute-done | bytes 49184 | tf_op jit(solution)/shard_map/ppermute | solution.py:497
  77.7 8.6 %all_to_all.21.refs_16_ = f32[4,2,3,4,8,128]{5,4,3,2,1,0:T(8,128)S(1)} all-to-all(f32[4,2,3,4,8,128]{5,4,3,2,1,0:T(8,128)S(1)} %shard_map.65), channel_id=1, replica_groups=mesh['real'=2,'zh'=4,'zl'=4,'xc'=4,'yl'=2,'core'=2] {'xc'}, dimensions={0} | all-to-all | bytes 786432 | tf_op jit(solution)/shard_map/all_to_all | solution.py:504
  86.3 2.4 %shard_map.66 = (f32[3,24,16,256]{3,2,1,0:T(8,128)S(1)}, f32[16,1,128]{2,1,0:T(1,128)S(1)}) custom-call(f32[24,16,256]{2,1,0:T(8,128)S(1)} %get-tuple-element.26.refs_3_.refs_0_, f32[3,24,16,256]{3,2,1,0:T(8,128)S(1)} %get-tuple-element.27.refs_1_, f32[3,24,16,256]{3,2,1,0:T(8,128)S(1)} %get-tuple-element.28.refs_2_, ...), custom_call_target="tpu_custom_call" | custom-call | tf_op jit(solution)/shard_map/pallas_call | solution.py:474
  88.7 12.8 %all_to_all.22.in_ref = f32[16,1,128]{2,1,0:T(1,128)S(1)} all-to-all(f32[16,1,128]{2,1,0:T(1,128)S(1)} %get-tuple-element.41), channel_id=1, replica_groups=mesh['real'=2,'zh'=4,'zl'=4,'xc'=4,'yl'=2,'core'=2] {'xc','yl','core'}, dimensions={0} | all-to-all | bytes 16384 | tf_op jit(solution)/shard_map/all_to_all | solution.py:544
  101.5 23.5 %all_to_all.23.refs_3_ = f32[16,1,128]{2,1,0:T(1,128)S(1)} all-to-all(f32[16,1,128]{2,1,0:T(1,128)S(1)} %shard_map.67), channel_id=1, replica_groups=mesh['real'=2,'zh'=4,'zl'=4,'xc'=4,'yl'=2,'core'=2] {'zh','zl'}, dimensions={0} | all-to-all | bytes 16384 | tf_op jit(solution)/shard_map/all_to_all | solution.py:546
  125.1 1.5 %shard_map.68 = (f32[8,8,128]{2,1,0:T(8,128)}, f32[3]{0:T(128)}) custom-call(f32[3,24,16,256]{3,2,1,0:T(8,128)S(1)} %get-tuple-element.25.refs_0_, f32[3,24,16,256]{3,2,1,0:T(8,128)S(1)} %get-tuple-element.34.refs_11_.refs_1_, f32[3,24,16,256]{3,2,1,0:T(8,128)S(1)} %get-tuple-element.40.refs_2_, f32[16,1,128]{2,1,0:T(1,128)S(1)} %all_to_all.23.refs_3_), custom_call_target="tpu_custom_call" | custom-call | tf_op jit(solution)/shard_map/pallas_call | solution.py:474
  (2 shorter events, 0.1 us)
Async XLA Ops:
  9.1 9.8 %collective-permute-start.1 = (f32[2,4,8,8,128]{4,3,2,1,0:T(8,128)S(1)}, f32[2,4,8,8,128]{4,3,2,1,0:T(8,128)S(1)}, u32[]{:S(2)}, u32[]{:S(2)}) collective-permute-start(f32[2,4,8,8,128]{4,3,2,1,0:T(8,128)S(1)} %bitcast.1), channel_id=1, source_target_pairs={{1,2},{2,1},{5,6},{6,5},{9,10},{10,9},{13,14},{14,13},{17,18},{18,... | collective-permute-start | bytes 786440 | tf_op jit(solution)/shard_map/ppermute | solution.py:497
  14.3 5.7 %collective-permute-start = (f32[2,4,8,8,128]{4,3,2,1,0:T(8,128)S(1)}, f32[2,4,8,8,128]{4,3,2,1,0:T(8,128)S(1)}, u32[]{:S(2)}, u32[]{:S(2)}) collective-permute-start(f32[2,4,8,8,128]{4,3,2,1,0:T(8,128)S(1)} %bitcast.2), channel_id=1, source_target_pairs={{0,1},{2,3},{1,0},{3,2},{4,5},{6,7},{5,4},{7,6},{8,9},{10,11},{9,8... | collective-permute-start | bytes 786440 | tf_op jit(solution)/shard_map/ppermute | solution.py:497
  20.2 10.0 %collective-permute-start.2 = (f32[24,16,256]{2,1,0:T(8,128)S(1)}, f32[24,16,256]{2,1,0:T(8,128)S(1)}, u32[]{:S(2)}, u32[]{:S(2)}) collective-permute-start(f32[24,16,256]{2,1,0:T(8,128)S(1)} %get-tuple-element.23), channel_id=1, source_target_pairs={{0,4},{4,8},{8,12},{12,16},{16,20},{20,24},{24,28},{28,32},{32,36}... | collective-permute-start | bytes 1179656 | tf_op jit(solution)/shard_map/ppermute | solution.py:517
  21.6 12.4 %collective-permute-start.3 = (f32[24,16,256]{2,1,0:T(8,128)S(1)}, f32[24,16,256]{2,1,0:T(8,128)S(1)}, u32[]{:S(2)}, u32[]{:S(2)}) collective-permute-start(f32[24,16,256]{2,1,0:T(8,128)S(1)} %get-tuple-element.24), channel_id=1, source_target_pairs={{4,0},{8,4},{12,8},{16,12},{20,16},{24,20},{28,24},{32,28},{36,32}... | collective-permute-start | bytes 1179656 | tf_op jit(solution)/shard_map/ppermute | solution.py:518
  36.2 10.1 %collective-permute-start.5 = (f32[6,4,8,128]{3,2,1,0:T(8,128)S(1)}, f32[6,4,8,128]{3,2,1,0:T(8,128)S(1)}, u32[]{:S(2)}, u32[]{:S(2)}) collective-permute-start(f32[6,4,8,128]{3,2,1,0:T(8,128)S(1)} %shard_map.62.refs_0_.refs_8_), channel_id=1, source_target_pairs={{16,32},{48,64},{80,96},{112,128},{144,160},{176,192},{208,224},{3... | collective-permute-start | bytes 294920 | tf_op jit(solution)/shard_map/ppermute | solution.py:497
  36.9 9.4 %collective-permute-start.4 = (f32[6,4,8,128]{3,2,1,0:T(8,128)S(1)}, f32[6,4,8,128]{3,2,1,0:T(8,128)S(1)}, u32[]{:S(2)}, u32[]{:S(2)}) collective-permute-start(f32[6,4,8,128]{3,2,1,0:T(8,128)S(1)} %shard_map.62.refs_0_.refs_8_), channel_id=1, source_target_pairs={{0,16},{32,48},{64,80},{96,112},{128,144},{160,176},{192,208},{224... | collective-permute-start | bytes 294920 | tf_op jit(solution)/shard_map/ppermute | solution.py:497
  67.8 8.3 %collective-permute-start.7 = (f32[3,4,8,128]{3,2,1,0:T(8,128)S(1)}, f32[3,4,8,128]{3,2,1,0:T(8,128)S(1)}, u32[]{:S(2)}, u32[]{:S(2)}) collective-permute-start(f32[3,4,8,128]{3,2,1,0:T(8,128)S(1)} %get-tuple-element.39.refs_0_.refs_13_), channel_id=1, source_target_pairs={{16,32},{48,64},{80,96},{112,128},{144,160},{176,192},{208,224},{3... | collective-permute-start | bytes 147464 | tf_op jit(solution)/shard_map/ppermute | solution.py:497
  68.5 9.1 %collective-permute-start.6 = (f32[3,4,8,128]{3,2,1,0:T(8,128)S(1)}, f32[3,4,8,128]{3,2,1,0:T(8,128)S(1)}, u32[]{:S(2)}, u32[]{:S(2)}) collective-permute-start(f32[3,4,8,128]{3,2,1,0:T(8,128)S(1)} %get-tuple-element.39.refs_0_.refs_13_), channel_id=1, source_target_pairs={{0,16},{32,48},{64,80},{96,112},{128,144},{160,176},{192,208},{224... | collective-permute-start | bytes 147464 | tf_op jit(solution)/shard_map/ppermute | solution.py:497

commit v5 on v4

--- a/solution.py
+++ b/solution.py
@@ -16,7 +16,7 @@
 HI = lax.Precision.HIGHEST
 
 
-GROUP = 4
+GROUP = 8
 
 
 def loop(first, last, step, group=None):
@@ -64,7 +64,7 @@
     return jnp.where(e > 0.0, 1.0 / jnp.where(e > 0.0, diag, 1.0), 0.0)
 
 
-def prepare(e_ref, level, first, last):
+def prepare(e_ref, level, first, last, group=None):
     cx_ref, cy_ref, cyp_ref, cz_ref, czp_ref, diag_ref, inv_ref = level
     low, outer = y_edges(16, 1)
 
@@ -79,7 +79,7 @@
             for ref, v in zip(level, (cx, cy, cyp, cz, czp, diag, inverse(e, diag))):
                 ref[r, i] = v
 
-    loop(first, last, step)
+    loop(first, last, step, group)
     for r in range(3):
         cx_ref[r, last] = 0.5 * (e_ref[r, last] + e_ref[r, last - 1])
 
@@ -95,14 +95,16 @@
 KEEP = 1.0 - OMEGA
 
 
-def pool_own(src_of, many, big_ref, half_ref, scale):
+def pool_own(src_of, many, big_ref):
     for f in range(many):
         for k in range(4):
             at = (f * 4 + k) * 16
-            big_ref[at : at + 16, :] = (0.125 * scale) * (src_of(f, 8 + 2 * k) + src_of(f, 9 + 2 * k))
-    rows = many * 64
-    half_ref[0:rows, :] = jnp.dot(big_ref[0:rows, :], pool_matrix(), precision=HI, preferred_element_type=F32)
-    return half_ref[pl.ds(0, rows // 2, stride=2), :] + half_ref[pl.ds(1, rows // 2, stride=2), :]
+            pair = src_of(f, 8 + 2 * k) + src_of(f, 9 + 2 * k)
+            for h in range(2):
+                big_ref[h, at : at + 16, :] = 0.125 * pair[:, 128 * h : 128 * h + 128]
+    rows = many * 32
+    halves = [big_ref[h, pl.ds(0, rows, stride=2), :] + big_ref[h, pl.ds(1, rows, stride=2), :] for h in range(2)]
+    return jnp.dot(jnp.concatenate(halves, 1), pool_matrix(), precision=HI, preferred_element_type=F32)
 
 
 def stack_level(e, stride):
@@ -143,9 +145,9 @@
 STRIDES = (1, 2, 4)
 
 
-def set_levels(e1_ref, level_refs):
+def set_levels(e1, level_refs):
     for r in range(3):
-        e = e1_ref[r]
+        e = e1[r]
         for ref, stride in zip(level_refs, STRIDES):
             for q, v in enumerate(stack_level(e, stride)):
                 ref[q, r, 1 : 1 + v.shape[0]] = v
@@ -167,10 +169,10 @@
     return KEEP * x1[1:-1] + OMEGA * one[6][at] * (rhs1[at] + stack_pull(one, x1, 1, first, last))
 
 
-def coarse_all(level_refs, rhs1_ref, out_ref, first, last):
+def coarse_all(level_refs, rhs1, out_ref, first, last):
     for r in range(3):
         levels = [[ref[q, r] for q in range(7)] for ref in level_refs]
-        out_ref[r] = coarse(levels, rhs1_ref[r], first, last)
+        out_ref[r] = coarse(levels, rhs1[r], first, last)
 
 
 def widen_into(e1_ref, count, wide_ref):
@@ -226,7 +228,7 @@
         ref[16 : 16 + n] = hi_ref[OFFS[f] : OFFS[f] + n]
 
 
-def stiffness(place_ref, d_ref, v_ref, s_ref, e_ref, f_ref, first, last):
+def stiffness(place_ref, d_ref, v_ref, s_ref, e_ref, f_ref, first, last, group=None):
     block, gy = place_ref[0], place_ref[1]
     lane = iota((1, 256), 1)
     z = gy * 128 + jnp.where(lane < 192, lane, lane - 256)
@@ -263,20 +265,30 @@
                 slope = BETA * (1.0 - t * t) * den
                 f_ref[r, i] = (3.0 * (1.0 - EMIN)) * square * scale * slope
 
-    loop(first, last, step)
-
-
-def first_kernel(
-    place_ref, own_ref, lo_ref, hi_ref, g_ref,
-    d_ref, v_ref, s_ref, load_ref, e_ref, x_ref, rest_ref, big_ref, half_ref, *level,
-):
+    loop(first, last, step, group)
+
+
+def inner_kernel(place_ref, own_ref, load_ref, f_ref, e_ref, *refs):
+    level, (d_ref, v_ref, s_ref) = refs[:7], refs[7:]
+    for f, ref in enumerate((d_ref, v_ref, s_ref, load_ref)):
+        ref[8:16] = own_ref[f]
+    stiffness(place_ref, d_ref, v_ref, s_ref, e_ref, f_ref, 9, 15, 3)
+    prepare(e_ref, level, 10, 14)
+
+
+def first_kernel(place_ref, own_ref, lo_ref, hi_ref, *refs):
+    g_ref, load_ref, f_ref, e_ref = refs[10:14]
+    level, (d_ref, v_ref, s_ref, x_ref, rest_ref, big_ref) = refs[14:21], refs[21:]
+    inv_ref = level[6]
     spread_out(own_ref, lo_ref, hi_ref, (d_ref, v_ref, s_ref, load_ref))
-    stiffness(place_ref, d_ref, v_ref, s_ref, e_ref, None, 6, 18)
-    prepare(e_ref, level, 7, 17)
+    for first in (6, 15):
+        stiffness(place_ref, d_ref, v_ref, s_ref, e_ref, f_ref, first, first + 3, 3)
+    for first in (7, 14):
+        prepare(e_ref, level, first, first + 3, 3)
 
     def start(i):
         for r in range(3):
-            x_ref[r, i] = OMEGA * load_ref[i] * level[6][r, i]
+            x_ref[r, i] = OMEGA * load_ref[i] * inv_ref[r, i]
 
     loop(7, 17, start)
 
@@ -285,17 +297,18 @@
             rest_ref[r, i - 8] = KEEP * load_ref[i] + pull(x_ref, i, r, level)
 
     loop(8, 16, leftover)
-    g_ref[0:3] = pool_own(lambda f, i: rest_ref[f, i - 8], 3, big_ref, half_ref, 1.0).reshape(3, 4, 8, 128)
-    g_ref[3:6] = pool_own(lambda f, i: e_ref[f, i], 3, big_ref, half_ref, 0.25).reshape(3, 4, 8, 128)
-
-
-def wide_kernel(
-    place_ref, own_ref, lo_ref, hi_ref, f_ref, load_ref, *refs,
-):
-    level, (d_ref, v_ref, s_ref, e_ref) = refs[:7], refs[7:]
+    source = lambda f, i: rest_ref[f, i - 8] if f < 3 else 0.25 * e_ref[f - 3, i]
+    g_ref[...] = pool_own(source, 6, big_ref).reshape(6, 4, 8, 128)
+
+
+def wide_kernel(place_ref, own_ref, lo_ref, hi_ref, *refs):
+    load_ref, f_ref, e_ref = refs[10:13]
+    level, (d_ref, v_ref, s_ref) = refs[13:20], refs[20:]
     spread_out(own_ref, lo_ref, hi_ref, (d_ref, v_ref, s_ref, load_ref))
-    stiffness(place_ref, d_ref, v_ref, s_ref, e_ref, f_ref, 2, 22)
-    prepare(e_ref, level, 3, 21)
+    for first in (2, 18):
+        stiffness(place_ref, d_ref, v_ref, s_ref, e_ref, None, first, first + 4)
+    for first in (3, 17):
+        prepare(e_ref, level, first, first + 4)
 
 
 def mix_kernel(place_ref, c_ref, even_ref, odd_ref, *refs):
@@ -306,37 +319,33 @@
         out_ref[to, 1] = jnp.where((mine > to) == even, odd_ref[...], even_ref[...])
 
 
-def window(place_ref, c_ref, even_ref, odd_ref, mixed_ref, first, into_ref):
-    block = place_ref[0]
-    mine, even = block % 4, (block // 4) % 2 == 0
+def window(place_ref, c_ref, even_ref, odd_ref, mixed_ref, field):
+    mine, even = place_ref[0] % 4, (place_ref[0] // 4) % 2 == 0
+    pieces = []
     for b in range(9):
-        at = block - 4 + b
-        keep = ((at >= 0) & (at < NBX)).astype(F32)
         source = mine + (b - 4)
-        for r in range(3):
-            if b == 0:
-                piece = jnp.where(even, odd_ref[first + r], even_ref[first + r])
-            elif b == 4:
-                piece = c_ref[first + r]
-            elif b == 8:
-                piece = jnp.where(even, even_ref[first + r], odd_ref[first + r])
-            else:
-                far = ((source < 0) | (source > 3)).astype(jnp.int32)
-                piece = mixed_ref[(source + 4) % 4, far, first + r]
-            into_ref[r, 4 * b : 4 * b + 4] = keep * piece
+        if b == 0:
+            piece = jnp.where(even, odd_ref[field], even_ref[field])
+        elif b == 4:
+            piece = c_ref[field]
+        elif b == 8:
+            piece = jnp.where(even, even_ref[field], odd_ref[field])
+        else:
+            far = ((source < 0) | (source > 3)).astype(jnp.int32)
+            piece = mixed_ref[(source + 4) % 4, far, field]
+        pieces.append(piece)
+    return jnp.concatenate(pieces, 0)
 
 
 def second_kernel(place_ref, load_ref, *refs):
     level, (c_ref, even_ref, odd_ref, mixed_ref) = refs[:7], refs[7:11]
     one_ref, two_ref, three_ref, z0_ref, q0_ref, g_ref = refs[11:17]
-    e1_ref, x_ref, y_ref, rhs_ref, out1_ref, wide_ref, big_ref, half_ref = refs[17:]
+    x_ref, y_ref, out1_ref, wide_ref, big_ref = refs[17:]
     diag_ref, inv_ref = level[5:]
     got = (place_ref, c_ref, even_ref, odd_ref, mixed_ref)
-    window(*got, 3, e1_ref)
-    window(*got, 0, rhs_ref)
     levels = (one_ref, two_ref, three_ref)
-    set_levels(e1_ref, levels)
-    coarse_all(levels, rhs_ref, out1_ref, 13, 23)
+    set_levels([window(*got, 3 + r) for r in range(3)], levels)
+    coarse_all(levels, [window(*got, r) for r in range(3)], out1_ref, 13, 23)
     widen_into(out1_ref, 10, wide_ref)
 
     def start(i):
@@ -365,29 +374,29 @@
             x_ref[r, i] = KEEP * q0_ref[r, i] + pull(y_ref, i, r, level)
 
     loop(8, 16, leftover)
-    g_ref[...] = pool_own(lambda f, i: x_ref[f, i], 3, big_ref, half_ref, 1.0).reshape(3, 4, 8, 128)
+    g_ref[...] = pool_own(lambda f, i: x_ref[f, i], 3, big_ref).reshape(3, 4, 8, 128)
 
 
 def third_kernel(place_ref, load_ref, *refs):
     level, (one_ref, two_ref, three_ref, z0_ref, q0_ref, c_ref, even_ref, odd_ref, mixed_ref) = refs[:7], refs[7:16]
-    w_ref, dots_ref, x_ref, rhs_ref, out1_ref, wide_ref = refs[16:]
+    w_ref, dots_ref, x_ref, out1_ref, wide_ref = refs[16:]
     diag_ref, inv_ref = level[5:]
-    window(place_ref, c_ref, even_ref, odd_ref, mixed_ref, 0, rhs_ref)
-    coarse_all((one_ref, two_ref, three_ref), rhs_ref, out1_ref, 14, 22)
+    rhs1 = [window(place_ref, c_ref, even_ref, odd_ref, mixed_ref, r) for r in range(3)]
+    coarse_all((one_ref, two_ref, three_ref), rhs1, out1_ref, 14, 22)
     widen_into(out1_ref, 8, wide_ref)
 
     def start(i):
         for r in range(3):
             x_ref[r, i] = OMEGA * q0_ref[r, i] * inv_ref[r, i] + widened(wide_ref, r, (i - 4) // 2, 8)
 
-    loop(5, 19, start)
+    loop(5, 19, start, 7)
 
     def smooth(i):
         for r in range(3):
             near = q0_ref[r, i] + pull(x_ref, i, r, level)
             w_ref[r, i] = KEEP * x_ref[r, i] + OMEGA * near * inv_ref[r, i]
 
-    loop(6, 18, smooth)
+    loop(6, 18, smooth, 6)
 
     def add(t, sums):
         sums = list(sums)
@@ -464,18 +473,21 @@
     loop(8, 16, spread)
 
 
-def call(body, outs, scratch, *args, place=False, flops=0, out_specs=None):
+def call(body, outs, scratch, *args, place=False, flops=0, out_specs=None, aliases=None):
     if place:
         inner = body
 
         def body(*refs):
             return inner((lax.axis_index(X_AXES), lax.axis_index(Y_AXES), lax.axis_index("real")), *refs)
 
+    if aliases:
+        out_specs = (pl.BlockSpec(memory_space=pltpu.VMEM),) * len(outs)
     return pl.pallas_call(
         body,
         out_shape=outs,
         in_specs=[pl.BlockSpec(memory_space=pltpu.VMEM)] * len(args),
         **({} if out_specs is None else {"out_specs": out_specs}),
+        input_output_aliases=aliases or {},
         scratch_shapes=[pltpu.VMEM(dims, F32) for dims in scratch],
         compiler_params=pltpu.CompilerParams(vmem_limit_bytes=VMEM_LIMIT),
         cost_estimate=pl.CostEstimate(flops=flops, bytes_accessed=0, transcendentals=0),
@@ -486,7 +498,6 @@
 X_AXES = ("zh", "zl", "xc")
 Y_AXES = ("yl", "core")
 FIELD = (3, 24, 16, 256)
-LEVEL1 = (3, 36, 8, 128)
 SLICES = (24, 16, 256)
 
 
@@ -509,6 +520,7 @@
         pack_kernel,
         out_shape=shaped(4, 8, 8, 128),
         in_specs=[pl.BlockSpec(memory_space=pl.ANY)] * 4,
+        out_specs=pl.BlockSpec(memory_space=pltpu.VMEM),
         scratch_shapes=[pltpu.VMEM((8, 8, 128), jnp.int32)] * 2 + [pltpu.SemaphoreType.DMA((4,))],
     )(design, void_mask, solid_mask, load)
     both = lax.all_gather(own, "real")
@@ -516,29 +528,32 @@
     mine, up, down = call(select_kernel, outs, [], both, *swap(both, both, Y_AXES, 4), place=True)
     lo = lax.ppermute(up, X_AXES, [(i, i + 1) for i in range(NBX - 1)])
     hi = lax.ppermute(down, X_AXES, [(i + 1, i) for i in range(NBX - 1)])
-    g = call(
+    fields = (shaped(*SLICES),) + (shaped(*FIELD),) * 9
+    kept = call(inner_kernel, fields, [SLICES] * 3, mine, place=True, flops=10**7)
+    g, *kept = call(
         first_kernel,
-        shaped(6, 4, 8, 128),
-        [SLICES] * 4 + [FIELD] * 2 + [(3, 8, 16, 256), (192, 256), (192, 128)] + [FIELD] * 7,
-        mine, lo, hi, place=True,
+        (shaped(6, 4, 8, 128),) + fields,
+        [SLICES] * 3 + [FIELD, (3, 8, 16, 256), (2, 384, 128)],
+        mine, lo, hi, *kept, place=True, aliases={3 + q: 1 + q for q in range(10)},
     )
-    f, *level0 = call(
+    wide_load, f, _, *level0 = call(
         wide_kernel,
-        (shaped(*FIELD), shaped(*SLICES)) + (shaped(*FIELD),) * 7,
-        [SLICES] * 3 + [FIELD],
-        mine, lo, hi, place=True, flops=2 * 10**7,
+        fields,
+        [SLICES] * 3,
+        mine, lo, hi, *kept, place=True, flops=2 * 10**7, aliases={3 + q: q for q in range(10)},
     )
+    level0 = (wide_load, *level0)
     levels = tuple(shaped(7, 3, n, 8, 128) for n in (36, 18, 9))
     *levels, z0, q0, g2 = call(
         second_kernel,
         levels + (shaped(*FIELD), shaped(*FIELD), shaped(3, 4, 8, 128)),
-        [LEVEL1, FIELD, FIELD, LEVEL1, (3, 10, 8, 128), (2, 480, 128), (192, 256), (192, 128)],
+        [FIELD, FIELD, (3, 10, 8, 128), (2, 480, 128), (2, 192, 128)],
         *level0, *fetch(g, level0[0]), place=True,
     )
     w, dots = call(
         third_kernel,
         (shaped(*FIELD), shaped(16, 1, 128)),
-        [FIELD, LEVEL1, (3, 8, 8, 128), (2, 384, 128)],
+        [FIELD, (3, 8, 8, 128), (2, 384, 128)],
         *level0, *levels, z0, q0, *fetch(g2), place=True,
     )
     dots = lax.all_to_all(dots, ("xc", "yl", "core"), 0, 0, tiled=True)

time: 127 us -> 125 us (0.984)
  Pallas kernels: 15.2 us -> 12.1 us
    pallas_call x9 -> x10, Pallas kernels: 13.8 us -> 10.6 us  [call(): pl.pallas_call(body, out_shape=outs, in_specs=[pl.BlockSpec(memory_space=...]
  transfers between devices with their start and end apart: 8 -> 8, of which waited for: 4 -> 5; matrix products, arithmetic and copies ran while one was open for 0% -> 0% of each run, Pallas kernels for 2% -> 1%
where the time goes in v5:
time: 125 us; the launch traced here: 124 us
  blocking collectives  69 us (55%)
  starting transfers between devices  28.5 us (23%)
  waiting for transfers between devices  14 us (11%)
  Pallas kernels  12.1 us (10%)
    ppermute x6, starting transfers between devices, swap(): got.append(lax.ppermute(v, axes, pairs + [(j, i) for i, j in pairs]))  25.7 us
    all_to_all x2, blocking collectives, fetch(): return (own, even, odd, lax.all_to_all(mixed, 'xc', 0, 0))  24.4 us
    all_to_all x1, blocking collectives, body(): dots = lax.all_to_all(dots, ('zh', 'zl'), 0, 0, tiled=True)  24 us
    all_to_all x1, blocking collectives, body(): dots = lax.all_to_all(dots, ('xc', 'yl', 'core'), 0, 0, tiled=True)  13.5 us
    pallas_call x10, Pallas kernels, call(): pl.pallas_call(body, out_shape=outs, in_specs=[pl.BlockSpec(memory_space=...  10.6 us
    all_gather x1, blocking collectives, body(): both = lax.all_gather(own, 'real')  7.03 us
    ppermute x1, waiting for transfers between devices, body(): lo = lax.ppermute(up, X_AXES, [(i, i + 1) for i in range(NBX - 1)])  6.55 us
    ppermute x1, waiting for transfers between devices, body(): hi = lax.ppermute(down, X_AXES, [(i + 1, i) for i in range(NBX - 1)])  3.82 us
  transfers between devices with their start and end apart: 8, of which 5 were waited for; matrix products, arithmetic and copies ran while one was open for 0% of the time, Pallas kernels for 1%

profile of v5, /device:TPU:1, one launch (start us, length us, event | category | flops | bytes accessed | tf_op | source)
XLA Modules:
  0.0 124.3 jit_solution(17382913800953328386)
XLA Ops:
  0.6 1.5 %shard_map.59 = f32[4,8,8,128]{3,2,1,0:T(8,128)} custom-call(f32[8,8,128]{2,1,0:T(8,128)} %d_ref.1, s32[8,8,128]{2,1,0:T(8,128)} %v_ref.1, s32[8,8,128]{2,1,0:T(8,128)} %s_ref.1, f32[8,8,128]{2,1,0:T(8,128)} %load_ref.1), custom_call_target="tpu_custom_call" | custom-call | tf_op jit(solution)/shard_map/pallas_call | solution.py:519
  2.1 7.0 %all-gather = f32[8,8,8,128]{3,2,1,0:T(8,128)S(1)} all-gather(f32[4,8,8,128]{3,2,1,0:T(8,128)} %shard_map.59), channel_id=2, replica_groups=mesh['real'=2,'zh'=4,'zl'=4,'xc'=4,'yl'=2,'core'=2] {'real'}, dimensions={0}, use_global_device_ids=true | all-gather | bytes 393216 | tf_op jit(solution)/shard_map/all_gather | solution.py:526
  9.2 5.2 %collective-permute-start.1 = (f32[2,4,8,8,128]{4,3,2,1,0:T(8,128)S(1)}, f32[2,4,8,8,128]{4,3,2,1,0:T(8,128)S(1)}, u32[]{:S(2)}, u32[]{:S(2)}) collective-permute-start(f32[2,4,8,8,128]{4,3,2,1,0:T(8,128)S(1)} %bitcast.1), channel_id=1, source_target_pairs={{1,2},{2,1},{5,6},{6,5},{9,10},{10,9},{13,14},{14,13},{17,18},{18,... | collective-permute-start | bytes 786440 | tf_op jit(solution)/shard_map/ppermute | solution.py:508
  14.4 4.6 %collective-permute-start = (f32[2,4,8,8,128]{4,3,2,1,0:T(8,128)S(1)}, f32[2,4,8,8,128]{4,3,2,1,0:T(8,128)S(1)}, u32[]{:S(2)}, u32[]{:S(2)}) collective-permute-start(f32[2,4,8,8,128]{4,3,2,1,0:T(8,128)S(1)} %bitcast.2), channel_id=1, source_target_pairs={{0,1},{2,3},{1,0},{3,2},{4,5},{6,7},{5,4},{7,6},{8,9},{10,11},{9,8... | collective-permute-start | bytes 786440 | tf_op jit(solution)/shard_map/ppermute | solution.py:508
  19.0 0.0 collective-permute-done.1.refs_2_
  19.0 1.1 collective-permute-done.refs_1_
  20.1 0.1 shard_map.60
  20.2 1.4 %collective-permute-start.2 = (f32[24,16,256]{2,1,0:T(8,128)S(1)}, f32[24,16,256]{2,1,0:T(8,128)S(1)}, u32[]{:S(2)}, u32[]{:S(2)}) collective-permute-start(f32[24,16,256]{2,1,0:T(8,128)S(1)} %get-tuple-element.44), channel_id=1, source_target_pairs={{0,4},{4,8},{8,12},{12,16},{16,20},{20,24},{24,28},{28,32},{32,36}... | collective-permute-start | bytes 1179656 | tf_op jit(solution)/shard_map/ppermute | solution.py:529
  21.6 1.3 %collective-permute-start.3 = (f32[24,16,256]{2,1,0:T(8,128)S(1)}, f32[24,16,256]{2,1,0:T(8,128)S(1)}, u32[]{:S(2)}, u32[]{:S(2)}) collective-permute-start(f32[24,16,256]{2,1,0:T(8,128)S(1)} %get-tuple-element.45), channel_id=1, source_target_pairs={{4,0},{8,4},{12,8},{16,12},{20,16},{24,20},{28,24},{32,28},{36,32}... | collective-permute-start | bytes 1179656 | tf_op jit(solution)/shard_map/ppermute | solution.py:530
  22.9 0.7 shard_map.61
  23.6 6.5 %collective-permute-done.2.refs_1_ = f32[24,16,256]{2,1,0:T(8,128)S(1)} collective-permute-done((f32[24,16,256]{2,1,0:T(8,128)S(1)}, f32[24,16,256]{2,1,0:T(8,128)S(1)}, u32[]{:S(2)}, u32[]{:S(2)}) %collective-permute-start.2) | collective-permute-done | bytes 393248 | tf_op jit(solution)/shard_map/ppermute | solution.py:529
  30.2 3.8 %collective-permute-done.3.refs_2_ = f32[24,16,256]{2,1,0:T(8,128)S(1)} collective-permute-done((f32[24,16,256]{2,1,0:T(8,128)S(1)}, f32[24,16,256]{2,1,0:T(8,128)S(1)}, u32[]{:S(2)}, u32[]{:S(2)}) %collective-permute-start.3) | collective-permute-done | bytes 393248 | tf_op jit(solution)/shard_map/ppermute | solution.py:530
  34.0 1.3 %shard_map.62 = (f32[6,4,8,128]{3,2,1,0:T(8,128)S(1)}, f32[24,16,256]{2,1,0:T(8,128)S(1)}, f32[3,24,16,256]{3,2,1,0:T(8,128)S(1)}, f32[3,24,16,256]{3,2,1,0:T(8,...) custom-call(f32[4,8,16,256]{3,2,1,0:T(8,128)S(1)} %get-tuple-element, ...), custom_call_target="tpu_custom_call", output_to_operand_aliasing={{1}: (3, {}), {2}: (4, {}), {3}: (5, {}), {4}: (6, {}), {5}... | custom-call | tf_op jit(solution)/shard_map/pallas_call | solution.py:485
  35.3 0.7 collective-permute-start.5
  36.0 7.0 %collective-permute-start.4 = (f32[6,4,8,128]{3,2,1,0:T(8,128)S(1)}, f32[6,4,8,128]{3,2,1,0:T(8,128)S(1)}, u32[]{:S(2)}, u32[]{:S(2)}) collective-permute-start(f32[6,4,8,128]{3,2,1,0:T(8,128)S(1)} %get-tuple-element.75.refs_0_.refs_8_), channel_id=1, source_target_pairs={{0,16},{32,48},{64,80},{96,112},{128,144},{160,176},{192,208},{224... | collective-permute-start | bytes 294920 | tf_op jit(solution)/shard_map/ppermute | solution.py:508
  43.0 0.9 shard_map.63
  43.9 0.0 collective-permute-done.5.refs_2_.refs_10_
  43.9 1.0 collective-permute-done.4.refs_1_.refs_9_
  44.9 0.1 shard_map.64
  45.0 15.8 %all_to_all.20.refs_11_ = f32[4,2,6,4,8,128]{5,4,3,2,1,0:T(8,128)S(1)} all-to-all(f32[4,2,6,4,8,128]{5,4,3,2,1,0:T(8,128)S(1)} %shard_map.64), channel_id=1, replica_groups=mesh['real'=2,'zh'=4,'zl'=4,'xc'=4,'yl'=2,'core'=2] {'xc'}, dimensions={0} | all-to-all | bytes 1572864 | tf_op jit(solution)/shard_map/all_to_all | solution.py:515
  60.8 4.0 %shard_map.65 = (f32[7,3,36,8,128]{4,3,2,1,0:T(8,128)S(1)}, f32[7,3,18,8,128]{4,3,2,1,0:T(8,128)S(1)}, f32[7,3,9,8,128]{4,3,2,1,0:T(8,128)S(1)}, f32[3,24,16,256...) custom-call(f32[24,16,256]{2,1,0:T(8,128)S(1)} %get-tuple-element.67.refs_3_.refs_0_, ...), custom_call_target="tpu_custom_call" | custom-call | tf_op jit(solution)/shard_map/pallas_call | solution.py:485
  64.8 0.7 collective-permute-start.7
  65.5 7.6 %collective-permute-start.6 = (f32[3,4,8,128]{3,2,1,0:T(8,128)S(1)}, f32[3,4,8,128]{3,2,1,0:T(8,128)S(1)}, u32[]{:S(2)}, u32[]{:S(2)}) collective-permute-start(f32[3,4,8,128]{3,2,1,0:T(8,128)S(1)} %get-tuple-element.81.refs_0_.refs_13_), channel_id=1, source_target_pairs={{0,16},{32,48},{64,80},{96,112},{128,144},{160,176},{192,208},{224... | collective-permute-start | bytes 147464 | tf_op jit(solution)/shard_map/ppermute | solution.py:508
  73.1 0.0 collective-permute-done.7.refs_2_.refs_15_
  73.1 1.5 %collective-permute-done.6.refs_1_.refs_14_ = f32[3,4,8,128]{3,2,1,0:T(8,128)S(1)} collective-permute-done((f32[3,4,8,128]{3,2,1,0:T(8,128)S(1)}, f32[3,4,8,128]{3,2,1,0:T(8,128)S(1)}, u32[]{:S(2)}, u32[]{:S(2)}) %collective-permute-start.6) | collective-permute-done | bytes 49184 | tf_op jit(solution)/shard_map/ppermute | solution.py:508
  74.6 8.6 %all_to_all.21.refs_16_ = f32[4,2,3,4,8,128]{5,4,3,2,1,0:T(8,128)S(1)} all-to-all(f32[4,2,3,4,8,128]{5,4,3,2,1,0:T(8,128)S(1)} %shard_map.66), channel_id=1, replica_groups=mesh['real'=2,'zh'=4,'zl'=4,'xc'=4,'yl'=2,'core'=2] {'xc'}, dimensions={0} | all-to-all | bytes 786432 | tf_op jit(solution)/shard_map/all_to_all | solution.py:515
  83.3 2.2 %shard_map.67 = (f32[3,24,16,256]{3,2,1,0:T(8,128)S(1)}, f32[16,1,128]{2,1,0:T(1,128)S(1)}) custom-call(f32[24,16,256]{2,1,0:T(8,128)S(1)} %get-tuple-element.67.refs_3_.refs_0_, f32[3,24,16,256]{3,2,1,0:T(8,128)S(1)} %get-tuple-element.68.refs_1_, f32[3,24,16,256]{3,2,1,0:T(8,128)S(1)} %get-tuple-element.69.refs_2_, ...), custom_call_target="tpu_custom_call" | custom-call | tf_op jit(solution)/shard_map/pallas_call | solution.py:485
  85.5 13.5 %all_to_all.22.in_ref = f32[16,1,128]{2,1,0:T(1,128)S(1)} all-to-all(f32[16,1,128]{2,1,0:T(1,128)S(1)} %get-tuple-element.83), channel_id=1, replica_groups=mesh['real'=2,'zh'=4,'zl'=4,'xc'=4,'yl'=2,'core'=2] {'xc','yl','core'}, dimensions={0} | all-to-all | bytes 16384 | tf_op jit(solution)/shard_map/all_to_all | solution.py:559
  99.0 24.0 %all_to_all.23.refs_3_ = f32[16,1,128]{2,1,0:T(1,128)S(1)} all-to-all(f32[16,1,128]{2,1,0:T(1,128)S(1)} %shard_map.68), channel_id=1, replica_groups=mesh['real'=2,'zh'=4,'zl'=4,'xc'=4,'yl'=2,'core'=2] {'zh','zl'}, dimensions={0} | all-to-all | bytes 16384 | tf_op jit(solution)/shard_map/all_to_all | solution.py:561
  123.0 1.3 %shard_map.69 = (f32[8,8,128]{2,1,0:T(8,128)}, f32[3]{0:T(128)}) custom-call(f32[3,24,16,256]{3,2,1,0:T(8,128)S(1)} %get-tuple-element.66.refs_0_, f32[3,24,16,256]{3,2,1,0:T(8,128)S(1)} %get-tuple-element.76.refs_11_.refs_1_, f32[3,24,16,256]{3,2,1,0:T(8,128)S(1)} %get-tuple-element.82.refs_2_, f32[16,1,128]{2,1,0:T(1,128)S(1)} %all_to_all.23.refs_3_), custom_call_target="tpu_custom_call" | custom-call | tf_op jit(solution)/shard_map/pallas_call | solution.py:485
  (2 shorter events, 0.1 us)
Async XLA Ops:
  9.2 9.8 %collective-permute-start.1 = (f32[2,4,8,8,128]{4,3,2,1,0:T(8,128)S(1)}, f32[2,4,8,8,128]{4,3,2,1,0:T(8,128)S(1)}, u32[]{:S(2)}, u32[]{:S(2)}) collective-permute-start(f32[2,4,8,8,128]{4,3,2,1,0:T(8,128)S(1)} %bitcast.1), channel_id=1, source_target_pairs={{1,2},{2,1},{5,6},{6,5},{9,10},{10,9},{13,14},{14,13},{17,18},{18,... | collective-permute-start | bytes 786440 | tf_op jit(solution)/shard_map/ppermute | solution.py:508
  14.4 5.7 %collective-permute-start = (f32[2,4,8,8,128]{4,3,2,1,0:T(8,128)S(1)}, f32[2,4,8,8,128]{4,3,2,1,0:T(8,128)S(1)}, u32[]{:S(2)}, u32[]{:S(2)}) collective-permute-start(f32[2,4,8,8,128]{4,3,2,1,0:T(8,128)S(1)} %bitcast.2), channel_id=1, source_target_pairs={{0,1},{2,3},{1,0},{3,2},{4,5},{6,7},{5,4},{7,6},{8,9},{10,11},{9,8... | collective-permute-start | bytes 786440 | tf_op jit(solution)/shard_map/ppermute | solution.py:508
  20.2 10.0 %collective-permute-start.2 = (f32[24,16,256]{2,1,0:T(8,128)S(1)}, f32[24,16,256]{2,1,0:T(8,128)S(1)}, u32[]{:S(2)}, u32[]{:S(2)}) collective-permute-start(f32[24,16,256]{2,1,0:T(8,128)S(1)} %get-tuple-element.44), channel_id=1, source_target_pairs={{0,4},{4,8},{8,12},{12,16},{16,20},{20,24},{24,28},{28,32},{32,36}... | collective-permute-start | bytes 1179656 | tf_op jit(solution)/shard_map/ppermute | solution.py:529
  21.6 12.4 %collective-permute-start.3 = (f32[24,16,256]{2,1,0:T(8,128)S(1)}, f32[24,16,256]{2,1,0:T(8,128)S(1)}, u32[]{:S(2)}, u32[]{:S(2)}) collective-permute-start(f32[24,16,256]{2,1,0:T(8,128)S(1)} %get-tuple-element.45), channel_id=1, source_target_pairs={{4,0},{8,4},{12,8},{16,12},{20,16},{24,20},{28,24},{32,28},{36,32}... | collective-permute-start | bytes 1179656 | tf_op jit(solution)/shard_map/ppermute | solution.py:530
  35.3 8.6 %collective-permute-start.5 = (f32[6,4,8,128]{3,2,1,0:T(8,128)S(1)}, f32[6,4,8,128]{3,2,1,0:T(8,128)S(1)}, u32[]{:S(2)}, u32[]{:S(2)}) collective-permute-start(f32[6,4,8,128]{3,2,1,0:T(8,128)S(1)} %get-tuple-element.75.refs_0_.refs_8_), channel_id=1, source_target_pairs={{16,32},{48,64},{80,96},{112,128},{144,160},{176,192},{208,224},{3... | collective-permute-start | bytes 294920 | tf_op jit(solution)/shard_map/ppermute | solution.py:508
  36.0 9.0 %collective-permute-start.4 = (f32[6,4,8,128]{3,2,1,0:T(8,128)S(1)}, f32[6,4,8,128]{3,2,1,0:T(8,128)S(1)}, u32[]{:S(2)}, u32[]{:S(2)}) collective-permute-start(f32[6,4,8,128]{3,2,1,0:T(8,128)S(1)} %get-tuple-element.75.refs_0_.refs_8_), channel_id=1, source_target_pairs={{0,16},{32,48},{64,80},{96,112},{128,144},{160,176},{192,208},{224... | collective-permute-start | bytes 294920 | tf_op jit(solution)/shard_map/ppermute | solution.py:508
  64.8 8.3 %collective-permute-start.7 = (f32[3,4,8,128]{3,2,1,0:T(8,128)S(1)}, f32[3,4,8,128]{3,2,1,0:T(8,128)S(1)}, u32[]{:S(2)}, u32[]{:S(2)}) collective-permute-start(f32[3,4,8,128]{3,2,1,0:T(8,128)S(1)} %get-tuple-element.81.refs_0_.refs_13_), channel_id=1, source_target_pairs={{16,32},{48,64},{80,96},{112,128},{144,160},{176,192},{208,224},{3... | collective-permute-start | bytes 147464 | tf_op jit(solution)/shard_map/ppermute | solution.py:508
  65.5 9.1 %collective-permute-start.6 = (f32[3,4,8,128]{3,2,1,0:T(8,128)S(1)}, f32[3,4,8,128]{3,2,1,0:T(8,128)S(1)}, u32[]{:S(2)}, u32[]{:S(2)}) collective-permute-start(f32[3,4,8,128]{3,2,1,0:T(8,128)S(1)} %get-tuple-element.81.refs_0_.refs_13_), channel_id=1, source_target_pairs={{0,16},{32,48},{64,80},{96,112},{128,144},{160,176},{192,208},{224... | collective-permute-start | bytes 147464 | tf_op jit(solution)/shard_map/ppermute | solution.py:508

commit v6 on v5

--- a/solution.py
+++ b/solution.py
@@ -207,18 +207,38 @@
     copies[3].wait()
 
 
-def select_kernel(place_ref, c_ref, a_ref, b_ref, own_ref, up_ref, down_ref):
-    right = (iota((8, 128), 1) < 64) == (place_ref[1] % 2 == 0)
+def halve_kernel(place_ref, c_ref, even_ref, odd_ref):
+    even = place_ref[1] % 2 == 0
+    low = iota((8, 128), 1) < 64
     for f in range(4):
-        for i in range(8):
+        for i in range(4):
             for h in range(2):
-                halo = jnp.where(right, a_ref[h, f, i], b_ref[h, f, i])
-                piece = jnp.concatenate([c_ref[h, f, i], halo], 1)
-                own_ref[f, i, 8 * h : 8 * h + 8, :] = piece
+                near, far = c_ref[h, f, i], c_ref[h, f, i + 4]
+                begin = jnp.where(low, near, rolled(far, 64, 1))
+                end = jnp.where(low, rolled(near, 64, 1), far)
+                even_ref[h, f, i] = jnp.where(even, end, begin)
+                odd_ref[h, f, i] = jnp.where(even, begin, end)
+
+
+def select_kernel(place_ref, c_ref, even_ref, odd_ref, own_ref, up_ref, down_ref):
+    even = place_ref[1] % 2 == 0
+    low = iota((8, 128), 1) < 64
+    for f in range(4):
+        for h in range(2):
+            halos = [None] * 8
+            for i in range(4):
+                a, b = even_ref[h, f, i], odd_ref[h, f, i]
+                after, before = jnp.where(even, a, b), jnp.where(even, b, a)
+                halos[i] = jnp.where(low, after, rolled(before, 64, 1))
+                halos[i + 4] = jnp.where(low, rolled(after, 64, 1), before)
+            for i in range(8):
+                piece = jnp.concatenate([c_ref[h, f, i], halos[i]], 1)
+                rows = slice(8 * h, 8 * h + 8)
+                own_ref[f, i, rows, :] = piece
                 if i >= 8 - REACH[f]:
-                    up_ref[OFFS[f] + i - (8 - REACH[f]), 8 * h : 8 * h + 8, :] = piece
+                    up_ref[OFFS[f] + i - (8 - REACH[f]), rows, :] = piece
                 if i < REACH[f]:
-                    down_ref[OFFS[f] + i, 8 * h : 8 * h + 8, :] = piece
+                    down_ref[OFFS[f] + i, rows, :] = piece
 
 
 def spread_out(own_ref, lo_ref, hi_ref, refs):
@@ -525,7 +545,8 @@
     )(design, void_mask, solid_mask, load)
     both = lax.all_gather(own, "real")
     outs = (shaped(4, 8, 16, 256), shaped(*SLICES), shaped(*SLICES))
-    mine, up, down = call(select_kernel, outs, [], both, *swap(both, both, Y_AXES, 4), place=True)
+    halves = call(halve_kernel, (shaped(2, 4, 4, 8, 128),) * 2, [], both, place=True)
+    mine, up, down = call(select_kernel, outs, [], both, *swap(*halves, Y_AXES, 4), place=True)
     lo = lax.ppermute(up, X_AXES, [(i, i + 1) for i in range(NBX - 1)])
     hi = lax.ppermute(down, X_AXES, [(i + 1, i) for i in range(NBX - 1)])
     fields = (shaped(*SLICES),) + (shaped(*FIELD),) * 9

time: 125 us -> 123 us (0.984)
  starting transfers between devices: 28.5 us -> 26.2 us
    ppermute x1, waiting for transfers between devices: 6.55 us -> 2.68 us  [body(): lo = lax.ppermute(up, X_AXES, [(i, i + 1) for i in range(NBX - 1)])]
    ppermute x6, waiting for transfers between devices: 3.64 us -> 6.86 us  [swap(): got.append(lax.ppermute(v, axes, pairs + [(j, i) for i, j in pairs]))]
    all_to_all x1, blocking collectives: 13.5 us -> 11.3 us  [body(): dots = lax.all_to_all(dots, ('xc', 'yl', 'core'), 0, 0, tiled=True)]
    all_to_all x2, blocking collectives: 24.4 us -> 26.6 us  [fetch(): return (own, even, odd, lax.all_to_all(mixed, 'xc', 0, 0))]
    ppermute x6, starting transfers between devices: 25.7 us -> 23.6 us  [swap(): got.append(lax.ppermute(v, axes, pairs + [(j, i) for i, j in pairs]))]
    pallas_call x10 -> x11, Pallas kernels: 10.6 us -> 10.9 us  [call(): pl.pallas_call(body, out_shape=outs, in_specs=[pl.BlockSpec(memory_space=...]
where the time goes in v6:
time: 123 us
  blocking collectives  69.9 us (57%)
  starting transfers between devices  26.2 us (21%)
  waiting for transfers between devices  13.4 us (11%)
  Pallas kernels  12.4 us (10%)
    all_to_all x2, blocking collectives, fetch(): return (own, even, odd, lax.all_to_all(mixed, 'xc', 0, 0))  26.6 us
    all_to_all x1, blocking collectives, body(): dots = lax.all_to_all(dots, ('zh', 'zl'), 0, 0, tiled=True)  25 us
    ppermute x6, starting transfers between devices, swap(): got.append(lax.ppermute(v, axes, pairs + [(j, i) for i, j in pairs]))  23.6 us
    all_to_all x1, blocking collectives, body(): dots = lax.all_to_all(dots, ('xc', 'yl', 'core'), 0, 0, tiled=True)  11.3 us
    pallas_call x11, Pallas kernels, call(): pl.pallas_call(body, out_shape=outs, in_specs=[pl.BlockSpec(memory_space=...  10.9 us
    all_gather x1, blocking collectives, body(): both = lax.all_gather(own, 'real')  7.03 us
    ppermute x6, waiting for transfers between devices, swap(): got.append(lax.ppermute(v, axes, pairs + [(j, i) for i, j in pairs]))  6.86 us
    ppermute x1, waiting for transfers between devices, body(): hi = lax.ppermute(down, X_AXES, [(i + 1, i) for i in range(NBX - 1)])  3.84 us
  transfers between devices with their start and end apart: 8, of which 5 were waited for; matrix products, arithmetic and copies ran while one was open for 0% of the time, Pallas kernels for 1%

profile of v6, /device:TPU:1, one launch (start us, length us, event | category | flops | bytes accessed | tf_op | source)
XLA Modules:
  0.0 122.7 jit_solution(14638360802810535506)
XLA Ops:
  0.6 1.5 %shard_map.59 = f32[4,8,8,128]{3,2,1,0:T(8,128)} custom-call(f32[8,8,128]{2,1,0:T(8,128)} %d_ref.1, s32[8,8,128]{2,1,0:T(8,128)} %v_ref.1, s32[8,8,128]{2,1,0:T(8,128)} %s_ref.1, f32[8,8,128]{2,1,0:T(8,128)} %load_ref.1), custom_call_target="tpu_custom_call" | custom-call | tf_op jit(solution)/shard_map/pallas_call | solution.py:539
  2.1 7.0 %all-gather = f32[8,8,8,128]{3,2,1,0:T(8,128)S(1)} all-gather(f32[4,8,8,128]{3,2,1,0:T(8,128)} %shard_map.59), channel_id=2, replica_groups=mesh['real'=2,'zh'=4,'zl'=4,'xc'=4,'yl'=2,'core'=2] {'real'}, dimensions={0}, use_global_device_ids=true | all-gather | bytes 393216 | tf_op jit(solution)/shard_map/all_gather | solution.py:546
  9.2 0.1 shard_map.60
  9.3 9.1 %collective-permute-start = (f32[2,4,4,8,128]{4,3,2,1,0:T(8,128)S(1)}, f32[2,4,4,8,128]{4,3,2,1,0:T(8,128)S(1)}, u32[]{:S(2)}, u32[]{:S(2)}) collective-permute-start(f32[2,4,4,8,128]{4,3,2,1,0:T(8,128)S(1)} %get-tuple-element.45), channel_id=1, source_target_pairs={{0,1},{2,3},{1,0},{3,2},{4,5},{6,7},{5,4},{7,6},{8,9},{10,11},{9,8... | collective-permute-start | bytes 393224 | tf_op jit(solution)/shard_map/ppermute | solution.py:528
  18.4 1.9 %collective-permute-start.1 = (f32[2,4,4,8,128]{4,3,2,1,0:T(8,128)S(1)}, f32[2,4,4,8,128]{4,3,2,1,0:T(8,128)S(1)}, u32[]{:S(2)}, u32[]{:S(2)}) collective-permute-start(f32[2,4,4,8,128]{4,3,2,1,0:T(8,128)S(1)} %get-tuple-element.46), channel_id=1, source_target_pairs={{1,2},{2,1},{5,6},{6,5},{9,10},{10,9},{13,14},{14,13},{17,18},{18,... | collective-permute-start | bytes 393224 | tf_op jit(solution)/shard_map/ppermute | solution.py:528
  20.4 0.0 collective-permute-done.refs_1_
  20.4 4.3 %collective-permute-done.1.refs_2_ = f32[2,4,4,8,128]{4,3,2,1,0:T(8,128)S(1)} collective-permute-done((f32[2,4,4,8,128]{4,3,2,1,0:T(8,128)S(1)}, f32[2,4,4,8,128]{4,3,2,1,0:T(8,128)S(1)}, u32[]{:S(2)}, u32[]{:S(2)}) %collective-permute-start.1) | collective-permute-done | bytes 131104 | tf_op jit(solution)/shard_map/ppermute | solution.py:528
  24.7 0.2 shard_map.61
  24.9 1.3 %collective-permute-start.2 = (f32[24,16,256]{2,1,0:T(8,128)S(1)}, f32[24,16,256]{2,1,0:T(8,128)S(1)}, u32[]{:S(2)}, u32[]{:S(2)}) collective-permute-start(f32[24,16,256]{2,1,0:T(8,128)S(1)} %get-tuple-element.48), channel_id=1, source_target_pairs={{0,4},{4,8},{8,12},{12,16},{16,20},{20,24},{24,28},{28,32},{32,36}... | collective-permute-start | bytes 1179656 | tf_op jit(solution)/shard_map/ppermute | solution.py:550
  26.2 1.3 %collective-permute-start.3 = (f32[24,16,256]{2,1,0:T(8,128)S(1)}, f32[24,16,256]{2,1,0:T(8,128)S(1)}, u32[]{:S(2)}, u32[]{:S(2)}) collective-permute-start(f32[24,16,256]{2,1,0:T(8,128)S(1)} %get-tuple-element.49), channel_id=1, source_target_pairs={{4,0},{8,4},{12,8},{16,12},{20,16},{24,20},{28,24},{32,28},{36,32}... | collective-permute-start | bytes 1179656 | tf_op jit(solution)/shard_map/ppermute | solution.py:551
  27.5 0.7 shard_map.62
  28.2 2.7 %collective-permute-done.2.refs_1_ = f32[24,16,256]{2,1,0:T(8,128)S(1)} collective-permute-done((f32[24,16,256]{2,1,0:T(8,128)S(1)}, f32[24,16,256]{2,1,0:T(8,128)S(1)}, u32[]{:S(2)}, u32[]{:S(2)}) %collective-permute-start.2) | collective-permute-done | bytes 393248 | tf_op jit(solution)/shard_map/ppermute | solution.py:550
  30.9 3.8 %collective-permute-done.3.refs_2_ = f32[24,16,256]{2,1,0:T(8,128)S(1)} collective-permute-done((f32[24,16,256]{2,1,0:T(8,128)S(1)}, f32[24,16,256]{2,1,0:T(8,128)S(1)}, u32[]{:S(2)}, u32[]{:S(2)}) %collective-permute-start.3) | collective-permute-done | bytes 393248 | tf_op jit(solution)/shard_map/ppermute | solution.py:551
  34.8 1.3 %shard_map.63 = (f32[6,4,8,128]{3,2,1,0:T(8,128)S(1)}, f32[24,16,256]{2,1,0:T(8,128)S(1)}, f32[3,24,16,256]{3,2,1,0:T(8,128)S(1)}, f32[3,24,16,256]{3,2,1,0:T(8,...) custom-call(f32[4,8,16,256]{3,2,1,0:T(8,128)S(1)} %get-tuple-element, ...), custom_call_target="tpu_custom_call", output_to_operand_aliasing={{1}: (3, {}), {2}: (4, {}), {3}: (5, {}), {4}: (6, {}), {5}... | custom-call | tf_op jit(solution)/shard_map/pallas_call | solution.py:505
  36.1 0.7 collective-permute-start.5
  36.7 3.6 %collective-permute-start.4 = (f32[6,4,8,128]{3,2,1,0:T(8,128)S(1)}, f32[6,4,8,128]{3,2,1,0:T(8,128)S(1)}, u32[]{:S(2)}, u32[]{:S(2)}) collective-permute-start(f32[6,4,8,128]{3,2,1,0:T(8,128)S(1)} %get-tuple-element.79.refs_0_.refs_8_), channel_id=1, source_target_pairs={{0,16},{32,48},{64,80},{96,112},{128,144},{160,176},{192,208},{224... | collective-permute-start | bytes 294920 | tf_op jit(solution)/shard_map/ppermute | solution.py:528
  40.3 0.9 shard_map.64
  41.3 0.0 collective-permute-done.5.refs_2_.refs_10_
  41.3 1.0 collective-permute-done.4.refs_1_.refs_9_
  42.3 0.1 shard_map.65
  42.4 16.5 %all_to_all.20.refs_11_ = f32[4,2,6,4,8,128]{5,4,3,2,1,0:T(8,128)S(1)} all-to-all(f32[4,2,6,4,8,128]{5,4,3,2,1,0:T(8,128)S(1)} %shard_map.65), channel_id=1, replica_groups=mesh['real'=2,'zh'=4,'zl'=4,'xc'=4,'yl'=2,'core'=2] {'xc'}, dimensions={0} | all-to-all | bytes 1572864 | tf_op jit(solution)/shard_map/all_to_all | solution.py:535
  58.8 4.0 %shard_map.66 = (f32[7,3,36,8,128]{4,3,2,1,0:T(8,128)S(1)}, f32[7,3,18,8,128]{4,3,2,1,0:T(8,128)S(1)}, f32[7,3,9,8,128]{4,3,2,1,0:T(8,128)S(1)}, f32[3,24,16,256...) custom-call(f32[24,16,256]{2,1,0:T(8,128)S(1)} %get-tuple-element.71.refs_3_.refs_0_, ...), custom_call_target="tpu_custom_call" | custom-call | tf_op jit(solution)/shard_map/pallas_call | solution.py:505
  62.8 0.7 collective-permute-start.7
  63.5 7.6 %collective-permute-start.6 = (f32[3,4,8,128]{3,2,1,0:T(8,128)S(1)}, f32[3,4,8,128]{3,2,1,0:T(8,128)S(1)}, u32[]{:S(2)}, u32[]{:S(2)}) collective-permute-start(f32[3,4,8,128]{3,2,1,0:T(8,128)S(1)} %get-tuple-element.85.refs_0_.refs_13_), channel_id=1, source_target_pairs={{0,16},{32,48},{64,80},{96,112},{128,144},{160,176},{192,208},{224... | collective-permute-start | bytes 147464 | tf_op jit(solution)/shard_map/ppermute | solution.py:528
  71.2 0.0 collective-permute-done.7.refs_2_.refs_15_
  71.2 1.5 %collective-permute-done.6.refs_1_.refs_14_ = f32[3,4,8,128]{3,2,1,0:T(8,128)S(1)} collective-permute-done((f32[3,4,8,128]{3,2,1,0:T(8,128)S(1)}, f32[3,4,8,128]{3,2,1,0:T(8,128)S(1)}, u32[]{:S(2)}, u32[]{:S(2)}) %collective-permute-start.6) | collective-permute-done | bytes 49184 | tf_op jit(solution)/shard_map/ppermute | solution.py:528
  72.7 10.2 %all_to_all.21.refs_16_ = f32[4,2,3,4,8,128]{5,4,3,2,1,0:T(8,128)S(1)} all-to-all(f32[4,2,3,4,8,128]{5,4,3,2,1,0:T(8,128)S(1)} %shard_map.67), channel_id=1, replica_groups=mesh['real'=2,'zh'=4,'zl'=4,'xc'=4,'yl'=2,'core'=2] {'xc'}, dimensions={0} | all-to-all | bytes 786432 | tf_op jit(solution)/shard_map/all_to_all | solution.py:535
  82.9 2.2 %shard_map.68 = (f32[3,24,16,256]{3,2,1,0:T(8,128)S(1)}, f32[16,1,128]{2,1,0:T(1,128)S(1)}) custom-call(f32[24,16,256]{2,1,0:T(8,128)S(1)} %get-tuple-element.71.refs_3_.refs_0_, f32[3,24,16,256]{3,2,1,0:T(8,128)S(1)} %get-tuple-element.72.refs_1_, f32[3,24,16,256]{3,2,1,0:T(8,128)S(1)} %get-tuple-element.73.refs_2_, ...), custom_call_target="tpu_custom_call" | custom-call | tf_op jit(solution)/shard_map/pallas_call | solution.py:505
  85.1 11.3 %all_to_all.22.in_ref = f32[16,1,128]{2,1,0:T(1,128)S(1)} all-to-all(f32[16,1,128]{2,1,0:T(1,128)S(1)} %get-tuple-element.87), channel_id=1, replica_groups=mesh['real'=2,'zh'=4,'zl'=4,'xc'=4,'yl'=2,'core'=2] {'xc','yl','core'}, dimensions={0} | all-to-all | bytes 16384 | tf_op jit(solution)/shard_map/all_to_all | solution.py:580
  96.4 25.0 %all_to_all.23.refs_3_ = f32[16,1,128]{2,1,0:T(1,128)S(1)} all-to-all(f32[16,1,128]{2,1,0:T(1,128)S(1)} %shard_map.69), channel_id=1, replica_groups=mesh['real'=2,'zh'=4,'zl'=4,'xc'=4,'yl'=2,'core'=2] {'zh','zl'}, dimensions={0} | all-to-all | bytes 16384 | tf_op jit(solution)/shard_map/all_to_all | solution.py:582
  121.4 1.3 %shard_map.70 = (f32[8,8,128]{2,1,0:T(8,128)}, f32[3]{0:T(128)}) custom-call(f32[3,24,16,256]{3,2,1,0:T(8,128)S(1)} %get-tuple-element.70.refs_0_, f32[3,24,16,256]{3,2,1,0:T(8,128)S(1)} %get-tuple-element.80.refs_11_.refs_1_, f32[3,24,16,256]{3,2,1,0:T(8,128)S(1)} %get-tuple-element.86.refs_2_, f32[16,1,128]{2,1,0:T(1,128)S(1)} %all_to_all.23.refs_3_), custom_call_target="tpu_custom_call" | custom-call | tf_op jit(solution)/shard_map/pallas_call | solution.py:505
  (2 shorter events, 0.1 us)
Async XLA Ops:
  9.3 11.1 %collective-permute-start = (f32[2,4,4,8,128]{4,3,2,1,0:T(8,128)S(1)}, f32[2,4,4,8,128]{4,3,2,1,0:T(8,128)S(1)}, u32[]{:S(2)}, u32[]{:S(2)}) collective-permute-start(f32[2,4,4,8,128]{4,3,2,1,0:T(8,128)S(1)} %get-tuple-element.45), channel_id=1, source_target_pairs={{0,1},{2,3},{1,0},{3,2},{4,5},{6,7},{5,4},{7,6},{8,9},{10,11},{9,8... | collective-permute-start | bytes 393224 | tf_op jit(solution)/shard_map/ppermute | solution.py:528
  18.4 6.3 %collective-permute-start.1 = (f32[2,4,4,8,128]{4,3,2,1,0:T(8,128)S(1)}, f32[2,4,4,8,128]{4,3,2,1,0:T(8,128)S(1)}, u32[]{:S(2)}, u32[]{:S(2)}) collective-permute-start(f32[2,4,4,8,128]{4,3,2,1,0:T(8,128)S(1)} %get-tuple-element.46), channel_id=1, source_target_pairs={{1,2},{2,1},{5,6},{6,5},{9,10},{10,9},{13,14},{14,13},{17,18},{18,... | collective-permute-start | bytes 393224 | tf_op jit(solution)/shard_map/ppermute | solution.py:528
  24.9 6.0 %collective-permute-start.2 = (f32[24,16,256]{2,1,0:T(8,128)S(1)}, f32[24,16,256]{2,1,0:T(8,128)S(1)}, u32[]{:S(2)}, u32[]{:S(2)}) collective-permute-start(f32[24,16,256]{2,1,0:T(8,128)S(1)} %get-tuple-element.48), channel_id=1, source_target_pairs={{0,4},{4,8},{8,12},{12,16},{16,20},{20,24},{24,28},{28,32},{32,36}... | collective-permute-start | bytes 1179656 | tf_op jit(solution)/shard_map/ppermute | solution.py:550
  26.2 8.5 %collective-permute-start.3 = (f32[24,16,256]{2,1,0:T(8,128)S(1)}, f32[24,16,256]{2,1,0:T(8,128)S(1)}, u32[]{:S(2)}, u32[]{:S(2)}) collective-permute-start(f32[24,16,256]{2,1,0:T(8,128)S(1)} %get-tuple-element.49), channel_id=1, source_target_pairs={{4,0},{8,4},{12,8},{16,12},{20,16},{24,20},{28,24},{32,28},{36,32}... | collective-permute-start | bytes 1179656 | tf_op jit(solution)/shard_map/ppermute | solution.py:551
  36.1 5.2 %collective-permute-start.5 = (f32[6,4,8,128]{3,2,1,0:T(8,128)S(1)}, f32[6,4,8,128]{3,2,1,0:T(8,128)S(1)}, u32[]{:S(2)}, u32[]{:S(2)}) collective-permute-start(f32[6,4,8,128]{3,2,1,0:T(8,128)S(1)} %get-tuple-element.79.refs_0_.refs_8_), channel_id=1, source_target_pairs={{16,32},{48,64},{80,96},{112,128},{144,160},{176,192},{208,224},{3... | collective-permute-start | bytes 294920 | tf_op jit(solution)/shard_map/ppermute | solution.py:528
  36.7 5.6 %collective-permute-start.4 = (f32[6,4,8,128]{3,2,1,0:T(8,128)S(1)}, f32[6,4,8,128]{3,2,1,0:T(8,128)S(1)}, u32[]{:S(2)}, u32[]{:S(2)}) collective-permute-start(f32[6,4,8,128]{3,2,1,0:T(8,128)S(1)} %get-tuple-element.79.refs_0_.refs_8_), channel_id=1, source_target_pairs={{0,16},{32,48},{64,80},{96,112},{128,144},{160,176},{192,208},{224... | collective-permute-start | bytes 294920 | tf_op jit(solution)/shard_map/ppermute | solution.py:528
  62.8 8.3 %collective-permute-start.7 = (f32[3,4,8,128]{3,2,1,0:T(8,128)S(1)}, f32[3,4,8,128]{3,2,1,0:T(8,128)S(1)}, u32[]{:S(2)}, u32[]{:S(2)}) collective-permute-start(f32[3,4,8,128]{3,2,1,0:T(8,128)S(1)} %get-tuple-element.85.refs_0_.refs_13_), channel_id=1, source_target_pairs={{16,32},{48,64},{80,96},{112,128},{144,160},{176,192},{208,224},{3... | collective-permute-start | bytes 147464 | tf_op jit(solution)/shard_map/ppermute | solution.py:528
  63.5 9.1 %collective-permute-start.6 = (f32[3,4,8,128]{3,2,1,0:T(8,128)S(1)}, f32[3,4,8,128]{3,2,1,0:T(8,128)S(1)}, u32[]{:S(2)}, u32[]{:S(2)}) collective-permute-start(f32[3,4,8,128]{3,2,1,0:T(8,128)S(1)} %get-tuple-element.85.refs_0_.refs_13_), channel_id=1, source_target_pairs={{0,16},{32,48},{64,80},{96,112},{128,144},{160,176},{192,208},{224... | collective-permute-start | bytes 147464 | tf_op jit(solution)/shard_map/ppermute | solution.py:528

commit v7 on v6

--- a/solution.py
+++ b/solution.py
@@ -191,7 +191,9 @@
 
 
 REACH = (7, 6, 6, 5)
-OFFS = (0, 7, 13, 19)
+WIDE = (5, 4, 4, 3)
+WIDE_AT = (0, 5, 9, 13)
+SENT = (41, 16, 128)
 
 
 def pack_kernel(d_ref, v_ref, s_ref, load_ref, out_ref, v_in, s_in, sems):
@@ -222,9 +224,12 @@
 
 def select_kernel(place_ref, c_ref, even_ref, odd_ref, own_ref, up_ref, down_ref):
     even = place_ref[1] % 2 == 0
-    low = iota((8, 128), 1) < 64
-    for f in range(4):
-        for h in range(2):
+    lane = iota((8, 128), 1)
+    low = lane < 64
+    for h in range(2):
+        rows = slice(8 * h, 8 * h + 8)
+        packed = [jnp.zeros((8, 128), F32)] * 2
+        for f in range(4):
             halos = [None] * 8
             for i in range(4):
                 a, b = even_ref[h, f, i], odd_ref[h, f, i]
@@ -232,20 +237,35 @@
                 halos[i] = jnp.where(low, after, rolled(before, 64, 1))
                 halos[i + 4] = jnp.where(low, rolled(after, 64, 1), before)
             for i in range(8):
-                piece = jnp.concatenate([c_ref[h, f, i], halos[i]], 1)
-                rows = slice(8 * h, 8 * h + 8)
-                own_ref[f, i, rows, :] = piece
-                if i >= 8 - REACH[f]:
-                    up_ref[OFFS[f] + i - (8 - REACH[f]), rows, :] = piece
-                if i < REACH[f]:
-                    down_ref[OFFS[f] + i, rows, :] = piece
+                own_ref[f, i, rows, :] = jnp.concatenate([c_ref[h, f, i], halos[i]], 1)
+            for depth in range(REACH[f]):
+                for side, (i, ref) in enumerate(((7 - depth, up_ref), (depth, down_ref))):
+                    if depth < WIDE[f]:
+                        at = 2 * (WIDE_AT[f] + depth)
+                        ref[at, rows, :] = c_ref[h, f, i]
+                        ref[at + 1, rows, :] = halos[i]
+                    else:
+                        k = 2 * f + depth - WIDE[f]
+                        ref[32 + k, rows, :] = c_ref[h, f, i]
+                        packed[side] = jnp.where(lane // 16 == k, rolled(halos[i], 16 * k + 8, 1), packed[side])
+        up_ref[40, rows, :] = packed[0]
+        down_ref[40, rows, :] = packed[1]
 
 
 def spread_out(own_ref, lo_ref, hi_ref, refs):
-    for f, (ref, n) in enumerate(zip(refs, REACH)):
-        ref[8 - n : 8] = lo_ref[OFFS[f] : OFFS[f] + n]
+    lane = iota((16, 128), 1)
+    edge = (lane < 8) | (lane >= 120)
+    for f, ref in enumerate(refs):
         ref[8:16] = own_ref[f]
-        ref[16 : 16 + n] = hi_ref[OFFS[f] : OFFS[f] + n]
+        for depth in range(REACH[f]):
+            for i, got in ((7 - depth, lo_ref), (16 + depth, hi_ref)):
+                if depth < WIDE[f]:
+                    at = 2 * (WIDE_AT[f] + depth)
+                    main, halo = got[at], got[at + 1]
+                else:
+                    k = 2 * f + depth - WIDE[f]
+                    main, halo = got[32 + k], jnp.where(edge, rolled(got[40], -(16 * k + 8), 1), 0.0)
+                ref[i] = jnp.concatenate([main, halo], 1)
 
 
 def stiffness(place_ref, d_ref, v_ref, s_ref, e_ref, f_ref, first, last, group=None):
@@ -544,7 +564,7 @@
         scratch_shapes=[pltpu.VMEM((8, 8, 128), jnp.int32)] * 2 + [pltpu.SemaphoreType.DMA((4,))],
     )(design, void_mask, solid_mask, load)
     both = lax.all_gather(own, "real")
-    outs = (shaped(4, 8, 16, 256), shaped(*SLICES), shaped(*SLICES))
+    outs = (shaped(4, 8, 16, 256), shaped(*SENT), shaped(*SENT))
     halves = call(halve_kernel, (shaped(2, 4, 4, 8, 128),) * 2, [], both, place=True)
     mine, up, down = call(select_kernel, outs, [], both, *swap(*halves, Y_AXES, 4), place=True)
     lo = lax.ppermute(up, X_AXES, [(i, i + 1) for i in range(NBX - 1)])

time: 123 us -> 123 us (level)
  no operation moved by 1% of the time
where the time goes in v7:
time: 123 us; the launch traced here: 122 us
  blocking collectives  69.9 us (57%)
  starting transfers between devices  26.2 us (21%)
  Pallas kernels  12.6 us (10%)
  waiting for transfers between devices  12.6 us (10%)
    all_to_all x2, blocking collectives, fetch(): return (own, even, odd, lax.all_to_all(mixed, 'xc', 0, 0))  26.6 us
    all_to_all x1, blocking collectives, body(): dots = lax.all_to_all(dots, ('zh', 'zl'), 0, 0, tiled=True)  25 us
    ppermute x6, starting transfers between devices, swap(): got.append(lax.ppermute(v, axes, pairs + [(j, i) for i, j in pairs]))  23.6 us
    all_to_all x1, blocking collectives, body(): dots = lax.all_to_all(dots, ('xc', 'yl', 'core'), 0, 0, tiled=True)  11.3 us
    pallas_call x11, Pallas kernels, call(): pl.pallas_call(body, out_shape=outs, in_specs=[pl.BlockSpec(memory_space=...  11.1 us
    all_gather x1, blocking collectives, body(): both = lax.all_gather(own, 'real')  7.03 us
    ppermute x6, waiting for transfers between devices, swap(): got.append(lax.ppermute(v, axes, pairs + [(j, i) for i, j in pairs]))  6.7 us
    ppermute x1, waiting for transfers between devices, body(): hi = lax.ppermute(down, X_AXES, [(i + 1, i) for i in range(NBX - 1)])  3.84 us
  transfers between devices with their start and end apart: 8, of which 5 were waited for; matrix products, arithmetic and copies ran while one was open for 0% of the time, Pallas kernels for 1%

profile of v7, /device:TPU:1, one launch (start us, length us, event | category | flops | bytes accessed | tf_op | source)
XLA Modules:
  0.0 122.1 jit_solution(5559807271448732258)
XLA Ops:
  0.6 1.5 %shard_map.59 = f32[4,8,8,128]{3,2,1,0:T(8,128)} custom-call(f32[8,8,128]{2,1,0:T(8,128)} %d_ref.1, s32[8,8,128]{2,1,0:T(8,128)} %v_ref.1, s32[8,8,128]{2,1,0:T(8,128)} %s_ref.1, f32[8,8,128]{2,1,0:T(8,128)} %load_ref.1), custom_call_target="tpu_custom_call" | custom-call | tf_op jit(solution)/shard_map/pallas_call | solution.py:559
  2.1 7.0 %all-gather = f32[8,8,8,128]{3,2,1,0:T(8,128)S(1)} all-gather(f32[4,8,8,128]{3,2,1,0:T(8,128)} %shard_map.59), channel_id=2, replica_groups=mesh['real'=2,'zh'=4,'zl'=4,'xc'=4,'yl'=2,'core'=2] {'real'}, dimensions={0}, use_global_device_ids=true | all-gather | bytes 393216 | tf_op jit(solution)/shard_map/all_gather | solution.py:566
  9.2 0.1 shard_map.60
  9.3 9.1 %collective-permute-start = (f32[2,4,4,8,128]{4,3,2,1,0:T(8,128)S(1)}, f32[2,4,4,8,128]{4,3,2,1,0:T(8,128)S(1)}, u32[]{:S(2)}, u32[]{:S(2)}) collective-permute-start(f32[2,4,4,8,128]{4,3,2,1,0:T(8,128)S(1)} %get-tuple-element.45), channel_id=1, source_target_pairs={{0,1},{2,3},{1,0},{3,2},{4,5},{6,7},{5,4},{7,6},{8,9},{10,11},{9,8... | collective-permute-start | bytes 393224 | tf_op jit(solution)/shard_map/ppermute | solution.py:548
  18.4 1.9 %collective-permute-start.1 = (f32[2,4,4,8,128]{4,3,2,1,0:T(8,128)S(1)}, f32[2,4,4,8,128]{4,3,2,1,0:T(8,128)S(1)}, u32[]{:S(2)}, u32[]{:S(2)}) collective-permute-start(f32[2,4,4,8,128]{4,3,2,1,0:T(8,128)S(1)} %get-tuple-element.46), channel_id=1, source_target_pairs={{1,2},{2,1},{5,6},{6,5},{9,10},{10,9},{13,14},{14,13},{17,18},{18,... | collective-permute-start | bytes 393224 | tf_op jit(solution)/shard_map/ppermute | solution.py:548
  20.4 0.0 collective-permute-done.refs_1_
  20.4 4.3 %collective-permute-done.1.refs_2_ = f32[2,4,4,8,128]{4,3,2,1,0:T(8,128)S(1)} collective-permute-done((f32[2,4,4,8,128]{4,3,2,1,0:T(8,128)S(1)}, f32[2,4,4,8,128]{4,3,2,1,0:T(8,128)S(1)}, u32[]{:S(2)}, u32[]{:S(2)}) %collective-permute-start.1) | collective-permute-done | bytes 131104 | tf_op jit(solution)/shard_map/ppermute | solution.py:548
  24.7 0.2 shard_map.61
  24.9 1.3 %collective-permute-start.2 = (f32[41,16,128]{2,1,0:T(8,128)S(1)}, f32[41,16,128]{2,1,0:T(8,128)S(1)}, u32[]{:S(2)}, u32[]{:S(2)}) collective-permute-start(f32[41,16,128]{2,1,0:T(8,128)S(1)} %get-tuple-element.48), channel_id=1, source_target_pairs={{0,4},{4,8},{8,12},{12,16},{16,20},{20,24},{24,28},{28,32},{32,36}... | collective-permute-start | bytes 1007624 | tf_op jit(solution)/shard_map/ppermute | solution.py:570
  26.3 1.3 %collective-permute-start.3 = (f32[41,16,128]{2,1,0:T(8,128)S(1)}, f32[41,16,128]{2,1,0:T(8,128)S(1)}, u32[]{:S(2)}, u32[]{:S(2)}) collective-permute-start(f32[41,16,128]{2,1,0:T(8,128)S(1)} %get-tuple-element.49), channel_id=1, source_target_pairs={{4,0},{8,4},{12,8},{16,12},{20,16},{24,20},{28,24},{32,28},{36,32}... | collective-permute-start | bytes 1007624 | tf_op jit(solution)/shard_map/ppermute | solution.py:571
  27.6 0.7 shard_map.62
  28.2 2.1 %collective-permute-done.2.refs_1_ = f32[41,16,128]{2,1,0:T(8,128)S(1)} collective-permute-done((f32[41,16,128]{2,1,0:T(8,128)S(1)}, f32[41,16,128]{2,1,0:T(8,128)S(1)}, u32[]{:S(2)}, u32[]{:S(2)}) %collective-permute-start.2) | collective-permute-done | bytes 335904 | tf_op jit(solution)/shard_map/ppermute | solution.py:570
  30.3 3.8 %collective-permute-done.3.refs_2_ = f32[41,16,128]{2,1,0:T(8,128)S(1)} collective-permute-done((f32[41,16,128]{2,1,0:T(8,128)S(1)}, f32[41,16,128]{2,1,0:T(8,128)S(1)}, u32[]{:S(2)}, u32[]{:S(2)}) %collective-permute-start.3) | collective-permute-done | bytes 335904 | tf_op jit(solution)/shard_map/ppermute | solution.py:571
  34.2 1.3 %shard_map.63 = (f32[6,4,8,128]{3,2,1,0:T(8,128)S(1)}, f32[24,16,256]{2,1,0:T(8,128)S(1)}, f32[3,24,16,256]{3,2,1,0:T(8,128)S(1)}, f32[3,24,16,256]{3,2,1,0:T(8,...) custom-call(f32[4,8,16,256]{3,2,1,0:T(8,128)S(1)} %get-tuple-element, ...), custom_call_target="tpu_custom_call", output_to_operand_aliasing={{1}: (3, {}), {2}: (4, {}), {3}: (5, {}), {4}: (6, {}), {5}... | custom-call | tf_op jit(solution)/shard_map/pallas_call | solution.py:525
  35.5 0.7 collective-permute-start.5
  36.1 3.6 %collective-permute-start.4 = (f32[6,4,8,128]{3,2,1,0:T(8,128)S(1)}, f32[6,4,8,128]{3,2,1,0:T(8,128)S(1)}, u32[]{:S(2)}, u32[]{:S(2)}) collective-permute-start(f32[6,4,8,128]{3,2,1,0:T(8,128)S(1)} %get-tuple-element.79.refs_0_.refs_8_), channel_id=1, source_target_pairs={{0,16},{32,48},{64,80},{96,112},{128,144},{160,176},{192,208},{224... | collective-permute-start | bytes 294920 | tf_op jit(solution)/shard_map/ppermute | solution.py:548
  39.7 1.1 shard_map.64
  40.8 0.0 collective-permute-done.5.refs_2_.refs_10_
  40.8 0.9 collective-permute-done.4.refs_1_.refs_9_
  41.7 0.1 shard_map.65
  41.8 16.5 %all_to_all.20.refs_11_ = f32[4,2,6,4,8,128]{5,4,3,2,1,0:T(8,128)S(1)} all-to-all(f32[4,2,6,4,8,128]{5,4,3,2,1,0:T(8,128)S(1)} %shard_map.65), channel_id=1, replica_groups=mesh['real'=2,'zh'=4,'zl'=4,'xc'=4,'yl'=2,'core'=2] {'xc'}, dimensions={0} | all-to-all | bytes 1572864 | tf_op jit(solution)/shard_map/all_to_all | solution.py:555
  58.2 4.0 %shard_map.66 = (f32[7,3,36,8,128]{4,3,2,1,0:T(8,128)S(1)}, f32[7,3,18,8,128]{4,3,2,1,0:T(8,128)S(1)}, f32[7,3,9,8,128]{4,3,2,1,0:T(8,128)S(1)}, f32[3,24,16,256...) custom-call(f32[24,16,256]{2,1,0:T(8,128)S(1)} %get-tuple-element.71.refs_3_.refs_0_, ...), custom_call_target="tpu_custom_call" | custom-call | tf_op jit(solution)/shard_map/pallas_call | solution.py:525
  62.3 0.7 collective-permute-start.7
  62.9 7.6 %collective-permute-start.6 = (f32[3,4,8,128]{3,2,1,0:T(8,128)S(1)}, f32[3,4,8,128]{3,2,1,0:T(8,128)S(1)}, u32[]{:S(2)}, u32[]{:S(2)}) collective-permute-start(f32[3,4,8,128]{3,2,1,0:T(8,128)S(1)} %get-tuple-element.85.refs_0_.refs_13_), channel_id=1, source_target_pairs={{0,16},{32,48},{64,80},{96,112},{128,144},{160,176},{192,208},{224... | collective-permute-start | bytes 147464 | tf_op jit(solution)/shard_map/ppermute | solution.py:548
  70.6 0.0 collective-permute-done.7.refs_2_.refs_15_
  70.6 1.5 %collective-permute-done.6.refs_1_.refs_14_ = f32[3,4,8,128]{3,2,1,0:T(8,128)S(1)} collective-permute-done((f32[3,4,8,128]{3,2,1,0:T(8,128)S(1)}, f32[3,4,8,128]{3,2,1,0:T(8,128)S(1)}, u32[]{:S(2)}, u32[]{:S(2)}) %collective-permute-start.6) | collective-permute-done | bytes 49184 | tf_op jit(solution)/shard_map/ppermute | solution.py:548
  72.1 10.2 %all_to_all.21.refs_16_ = f32[4,2,3,4,8,128]{5,4,3,2,1,0:T(8,128)S(1)} all-to-all(f32[4,2,3,4,8,128]{5,4,3,2,1,0:T(8,128)S(1)} %shard_map.67), channel_id=1, replica_groups=mesh['real'=2,'zh'=4,'zl'=4,'xc'=4,'yl'=2,'core'=2] {'xc'}, dimensions={0} | all-to-all | bytes 786432 | tf_op jit(solution)/shard_map/all_to_all | solution.py:555
  82.3 2.2 %shard_map.68 = (f32[3,24,16,256]{3,2,1,0:T(8,128)S(1)}, f32[16,1,128]{2,1,0:T(1,128)S(1)}) custom-call(f32[24,16,256]{2,1,0:T(8,128)S(1)} %get-tuple-element.71.refs_3_.refs_0_, f32[3,24,16,256]{3,2,1,0:T(8,128)S(1)} %get-tuple-element.72.refs_1_, f32[3,24,16,256]{3,2,1,0:T(8,128)S(1)} %get-tuple-element.73.refs_2_, ...), custom_call_target="tpu_custom_call" | custom-call | tf_op jit(solution)/shard_map/pallas_call | solution.py:525
  84.5 11.3 %all_to_all.22.in_ref = f32[16,1,128]{2,1,0:T(1,128)S(1)} all-to-all(f32[16,1,128]{2,1,0:T(1,128)S(1)} %get-tuple-element.87), channel_id=1, replica_groups=mesh['real'=2,'zh'=4,'zl'=4,'xc'=4,'yl'=2,'core'=2] {'xc','yl','core'}, dimensions={0} | all-to-all | bytes 16384 | tf_op jit(solution)/shard_map/all_to_all | solution.py:600
  95.8 25.0 %all_to_all.23.refs_3_ = f32[16,1,128]{2,1,0:T(1,128)S(1)} all-to-all(f32[16,1,128]{2,1,0:T(1,128)S(1)} %shard_map.69), channel_id=1, replica_groups=mesh['real'=2,'zh'=4,'zl'=4,'xc'=4,'yl'=2,'core'=2] {'zh','zl'}, dimensions={0} | all-to-all | bytes 16384 | tf_op jit(solution)/shard_map/all_to_all | solution.py:602
  120.8 1.3 %shard_map.70 = (f32[8,8,128]{2,1,0:T(8,128)}, f32[3]{0:T(128)}) custom-call(f32[3,24,16,256]{3,2,1,0:T(8,128)S(1)} %get-tuple-element.70.refs_0_, f32[3,24,16,256]{3,2,1,0:T(8,128)S(1)} %get-tuple-element.80.refs_11_.refs_1_, f32[3,24,16,256]{3,2,1,0:T(8,128)S(1)} %get-tuple-element.86.refs_2_, f32[16,1,128]{2,1,0:T(1,128)S(1)} %all_to_all.23.refs_3_), custom_call_target="tpu_custom_call" | custom-call | tf_op jit(solution)/shard_map/pallas_call | solution.py:525
  (2 shorter events, 0.1 us)
Async XLA Ops:
  9.3 11.1 %collective-permute-start = (f32[2,4,4,8,128]{4,3,2,1,0:T(8,128)S(1)}, f32[2,4,4,8,128]{4,3,2,1,0:T(8,128)S(1)}, u32[]{:S(2)}, u32[]{:S(2)}) collective-permute-start(f32[2,4,4,8,128]{4,3,2,1,0:T(8,128)S(1)} %get-tuple-element.45), channel_id=1, source_target_pairs={{0,1},{2,3},{1,0},{3,2},{4,5},{6,7},{5,4},{7,6},{8,9},{10,11},{9,8... | collective-permute-start | bytes 393224 | tf_op jit(solution)/shard_map/ppermute | solution.py:548
  18.4 6.3 %collective-permute-start.1 = (f32[2,4,4,8,128]{4,3,2,1,0:T(8,128)S(1)}, f32[2,4,4,8,128]{4,3,2,1,0:T(8,128)S(1)}, u32[]{:S(2)}, u32[]{:S(2)}) collective-permute-start(f32[2,4,4,8,128]{4,3,2,1,0:T(8,128)S(1)} %get-tuple-element.46), channel_id=1, source_target_pairs={{1,2},{2,1},{5,6},{6,5},{9,10},{10,9},{13,14},{14,13},{17,18},{18,... | collective-permute-start | bytes 393224 | tf_op jit(solution)/shard_map/ppermute | solution.py:548
  24.9 5.4 %collective-permute-start.2 = (f32[41,16,128]{2,1,0:T(8,128)S(1)}, f32[41,16,128]{2,1,0:T(8,128)S(1)}, u32[]{:S(2)}, u32[]{:S(2)}) collective-permute-start(f32[41,16,128]{2,1,0:T(8,128)S(1)} %get-tuple-element.48), channel_id=1, source_target_pairs={{0,4},{4,8},{8,12},{12,16},{16,20},{20,24},{24,28},{28,32},{32,36}... | collective-permute-start | bytes 1007624 | tf_op jit(solution)/shard_map/ppermute | solution.py:570
  26.3 7.9 %collective-permute-start.3 = (f32[41,16,128]{2,1,0:T(8,128)S(1)}, f32[41,16,128]{2,1,0:T(8,128)S(1)}, u32[]{:S(2)}, u32[]{:S(2)}) collective-permute-start(f32[41,16,128]{2,1,0:T(8,128)S(1)} %get-tuple-element.49), channel_id=1, source_target_pairs={{4,0},{8,4},{12,8},{16,12},{20,16},{24,20},{28,24},{32,28},{36,32}... | collective-permute-start | bytes 1007624 | tf_op jit(solution)/shard_map/ppermute | solution.py:571
  35.5 5.4 %collective-permute-start.5 = (f32[6,4,8,128]{3,2,1,0:T(8,128)S(1)}, f32[6,4,8,128]{3,2,1,0:T(8,128)S(1)}, u32[]{:S(2)}, u32[]{:S(2)}) collective-permute-start(f32[6,4,8,128]{3,2,1,0:T(8,128)S(1)} %get-tuple-element.79.refs_0_.refs_8_), channel_id=1, source_target_pairs={{16,32},{48,64},{80,96},{112,128},{144,160},{176,192},{208,224},{3... | collective-permute-start | bytes 294920 | tf_op jit(solution)/shard_map/ppermute | solution.py:548
  36.1 5.6 %collective-permute-start.4 = (f32[6,4,8,128]{3,2,1,0:T(8,128)S(1)}, f32[6,4,8,128]{3,2,1,0:T(8,128)S(1)}, u32[]{:S(2)}, u32[]{:S(2)}) collective-permute-start(f32[6,4,8,128]{3,2,1,0:T(8,128)S(1)} %get-tuple-element.79.refs_0_.refs_8_), channel_id=1, source_target_pairs={{0,16},{32,48},{64,80},{96,112},{128,144},{160,176},{192,208},{224... | collective-permute-start | bytes 294920 | tf_op jit(solution)/shard_map/ppermute | solution.py:548
  62.3 8.3 %collective-permute-start.7 = (f32[3,4,8,128]{3,2,1,0:T(8,128)S(1)}, f32[3,4,8,128]{3,2,1,0:T(8,128)S(1)}, u32[]{:S(2)}, u32[]{:S(2)}) collective-permute-start(f32[3,4,8,128]{3,2,1,0:T(8,128)S(1)} %get-tuple-element.85.refs_0_.refs_13_), channel_id=1, source_target_pairs={{16,32},{48,64},{80,96},{112,128},{144,160},{176,192},{208,224},{3... | collective-permute-start | bytes 147464 | tf_op jit(solution)/shard_map/ppermute | solution.py:548
  62.9 9.1 %collective-permute-start.6 = (f32[3,4,8,128]{3,2,1,0:T(8,128)S(1)}, f32[3,4,8,128]{3,2,1,0:T(8,128)S(1)}, u32[]{:S(2)}, u32[]{:S(2)}) collective-permute-start(f32[3,4,8,128]{3,2,1,0:T(8,128)S(1)} %get-tuple-element.85.refs_0_.refs_13_), channel_id=1, source_target_pairs={{0,16},{32,48},{64,80},{96,112},{128,144},{160,176},{192,208},{224... | collective-permute-start | bytes 147464 | tf_op jit(solution)/shard_map/ppermute | solution.py:548

commit v8 on v6

--- a/solution.py
+++ b/solution.py
@@ -192,19 +192,6 @@
 
 REACH = (7, 6, 6, 5)
 OFFS = (0, 7, 13, 19)
-
-
-def pack_kernel(d_ref, v_ref, s_ref, load_ref, out_ref, v_in, s_in, sems):
-    pairs = ((d_ref, out_ref.at[0]), (v_ref, v_in), (s_ref, s_in), (load_ref, out_ref.at[3]))
-    copies = [pltpu.make_async_copy(src, dst, sems.at[q]) for q, (src, dst) in enumerate(pairs)]
-    for copy in copies:
-        copy.start()
-    copies[1].wait()
-    out_ref[1] = v_in[...].astype(F32)
-    copies[2].wait()
-    out_ref[2] = s_in[...].astype(F32)
-    copies[0].wait()
-    copies[3].wait()
 
 
 def halve_kernel(place_ref, c_ref, even_ref, odd_ref):
@@ -536,13 +523,9 @@
 
 
 def body(design, load, void_mask, solid_mask):
-    own = pl.pallas_call(
-        pack_kernel,
-        out_shape=shaped(4, 8, 8, 128),
-        in_specs=[pl.BlockSpec(memory_space=pl.ANY)] * 4,
-        out_specs=pl.BlockSpec(memory_space=pltpu.VMEM),
-        scratch_shapes=[pltpu.VMEM((8, 8, 128), jnp.int32)] * 2 + [pltpu.SemaphoreType.DMA((4,))],
-    )(design, void_mask, solid_mask, load)
+    which = iota((4, 8, 8, 128), 0)
+    masks = jnp.where(which == 1, void_mask[None], solid_mask[None]).astype(F32)
+    own = jnp.where(which == 0, design[None], jnp.where(which == 3, load[None], masks))
     both = lax.all_gather(own, "real")
     outs = (shaped(4, 8, 16, 256), shaped(*SLICES), shaped(*SLICES))
     halves = call(halve_kernel, (shaped(2, 4, 4, 8, 128),) * 2, [], both, place=True)

time: 123 us -> 123 us (level)
    pallas_call x1 -> x0, Pallas kernels: 1.49 us -> none  [body(): pl.pallas_call(pack_kernel, out_shape=shaped(4, 8, 8, 128), in_specs=[pl....]
where the time goes in v8:
time: 123 us; the launch traced here: 122 us
  blocking collectives  69.6 us (57%)
  starting transfers between devices  26.3 us (21%)
  waiting for transfers between devices  13.4 us (11%)
  Pallas kernels  11.4 us (9%)
    all_to_all x2, blocking collectives, fetch(): return (own, even, odd, lax.all_to_all(mixed, 'xc', 0, 0))  26.6 us
    all_to_all x1, blocking collectives, body(): dots = lax.all_to_all(dots, ('zh', 'zl'), 0, 0, tiled=True)  24.9 us
    ppermute x6, starting transfers between devices, swap(): got.append(lax.ppermute(v, axes, pairs + [(j, i) for i, j in pairs]))  23.7 us
    pallas_call x11, Pallas kernels, call(): pl.pallas_call(body, out_shape=outs, in_specs=[pl.BlockSpec(memory_space=...  11.4 us
    all_to_all x1, blocking collectives, body(): dots = lax.all_to_all(dots, ('xc', 'yl', 'core'), 0, 0, tiled=True)  11.3 us
    ppermute x6, waiting for transfers between devices, swap(): got.append(lax.ppermute(v, axes, pairs + [(j, i) for i, j in pairs]))  6.85 us
    all_gather x1, blocking collectives, body(): both = lax.all_gather(own, 'real')  6.76 us
    ppermute x1, waiting for transfers between devices, body(): hi = lax.ppermute(down, X_AXES, [(i + 1, i) for i in range(NBX - 1)])  3.84 us
  transfers between devices with their start and end apart: 8, of which 5 were waited for; matrix products, arithmetic and copies ran while one was open for 0% of the time, Pallas kernels for 1%

profile of v8, /device:TPU:1, one launch (start us, length us, event | category | flops | bytes accessed | tf_op | source)
XLA Modules:
  0.0 122.4 jit_solution(15263900194906001461)
XLA Ops:
  0.7 0.9 select_select_fusion
  1.6 6.8 %all_gather.4.refs_0_ = f32[2,4,8,8,128]{4,3,2,1,0:T(8,128)S(1)} all-gather(f32[1,4,8,8,128]{4,3,2,1,0:T(8,128)S(1)} %select_select_fusion), channel_id=1, replica_groups=mesh['real'=2,'zh'=4,'zl'=4,'xc'=4,'yl'=2,'core'=2] {'real'}, dimensions={0}, use_global_device_ids=true | all-gather | bytes 393216 | tf_op jit(solution)/shard_map/all_gather | solution.py:529
  8.3 0.1 shard_map.59
  8.5 9.2 %collective-permute-start = (f32[2,4,4,8,128]{4,3,2,1,0:T(8,128)S(1)}, f32[2,4,4,8,128]{4,3,2,1,0:T(8,128)S(1)}, u32[]{:S(2)}, u32[]{:S(2)}) collective-permute-start(f32[2,4,4,8,128]{4,3,2,1,0:T(8,128)S(1)} %get-tuple-element.45), channel_id=1, source_target_pairs={{0,1},{2,3},{1,0},{3,2},{4,5},{6,7},{5,4},{7,6},{8,9},{10,11},{9,8... | collective-permute-start | bytes 393224 | tf_op jit(solution)/shard_map/ppermute | solution.py:515
  17.6 1.9 %collective-permute-start.1 = (f32[2,4,4,8,128]{4,3,2,1,0:T(8,128)S(1)}, f32[2,4,4,8,128]{4,3,2,1,0:T(8,128)S(1)}, u32[]{:S(2)}, u32[]{:S(2)}) collective-permute-start(f32[2,4,4,8,128]{4,3,2,1,0:T(8,128)S(1)} %get-tuple-element.46), channel_id=1, source_target_pairs={{1,2},{2,1},{5,6},{6,5},{9,10},{10,9},{13,14},{14,13},{17,18},{18,... | collective-permute-start | bytes 393224 | tf_op jit(solution)/shard_map/ppermute | solution.py:515
  19.6 0.0 collective-permute-done.refs_1_
  19.6 4.3 %collective-permute-done.1.refs_2_ = f32[2,4,4,8,128]{4,3,2,1,0:T(8,128)S(1)} collective-permute-done((f32[2,4,4,8,128]{4,3,2,1,0:T(8,128)S(1)}, f32[2,4,4,8,128]{4,3,2,1,0:T(8,128)S(1)}, u32[]{:S(2)}, u32[]{:S(2)}) %collective-permute-start.1) | collective-permute-done | bytes 131104 | tf_op jit(solution)/shard_map/ppermute | solution.py:515
  23.9 0.2 shard_map.60
  24.1 1.3 %collective-permute-start.2 = (f32[24,16,256]{2,1,0:T(8,128)S(1)}, f32[24,16,256]{2,1,0:T(8,128)S(1)}, u32[]{:S(2)}, u32[]{:S(2)}) collective-permute-start(f32[24,16,256]{2,1,0:T(8,128)S(1)} %get-tuple-element.48), channel_id=1, source_target_pairs={{0,4},{4,8},{8,12},{12,16},{16,20},{20,24},{24,28},{28,32},{32,36}... | collective-permute-start | bytes 1179656 | tf_op jit(solution)/shard_map/ppermute | solution.py:533
  25.5 1.3 %collective-permute-start.3 = (f32[24,16,256]{2,1,0:T(8,128)S(1)}, f32[24,16,256]{2,1,0:T(8,128)S(1)}, u32[]{:S(2)}, u32[]{:S(2)}) collective-permute-start(f32[24,16,256]{2,1,0:T(8,128)S(1)} %get-tuple-element.49), channel_id=1, source_target_pairs={{4,0},{8,4},{12,8},{16,12},{20,16},{24,20},{28,24},{32,28},{36,32}... | collective-permute-start | bytes 1179656 | tf_op jit(solution)/shard_map/ppermute | solution.py:534
  26.8 0.7 shard_map.61
  27.5 2.7 %collective-permute-done.2.refs_1_ = f32[24,16,256]{2,1,0:T(8,128)S(1)} collective-permute-done((f32[24,16,256]{2,1,0:T(8,128)S(1)}, f32[24,16,256]{2,1,0:T(8,128)S(1)}, u32[]{:S(2)}, u32[]{:S(2)}) %collective-permute-start.2) | collective-permute-done | bytes 393248 | tf_op jit(solution)/shard_map/ppermute | solution.py:533
  30.1 3.8 %collective-permute-done.3.refs_2_ = f32[24,16,256]{2,1,0:T(8,128)S(1)} collective-permute-done((f32[24,16,256]{2,1,0:T(8,128)S(1)}, f32[24,16,256]{2,1,0:T(8,128)S(1)}, u32[]{:S(2)}, u32[]{:S(2)}) %collective-permute-start.3) | collective-permute-done | bytes 393248 | tf_op jit(solution)/shard_map/ppermute | solution.py:534
  34.0 1.3 %shard_map.62 = (f32[6,4,8,128]{3,2,1,0:T(8,128)S(1)}, f32[24,16,256]{2,1,0:T(8,128)S(1)}, f32[3,24,16,256]{3,2,1,0:T(8,128)S(1)}, f32[3,24,16,256]{3,2,1,0:T(8,...) custom-call(f32[4,8,16,256]{3,2,1,0:T(8,128)S(1)} %get-tuple-element, ...), custom_call_target="tpu_custom_call", output_to_operand_aliasing={{1}: (3, {}), {2}: (4, {}), {3}: (5, {}), {4}: (6, {}), {5}... | custom-call | tf_op jit(solution)/shard_map/pallas_call | solution.py:492
  35.3 0.7 collective-permute-start.5
  36.0 3.6 %collective-permute-start.4 = (f32[6,4,8,128]{3,2,1,0:T(8,128)S(1)}, f32[6,4,8,128]{3,2,1,0:T(8,128)S(1)}, u32[]{:S(2)}, u32[]{:S(2)}) collective-permute-start(f32[6,4,8,128]{3,2,1,0:T(8,128)S(1)} %get-tuple-element.79.refs_0_.refs_8_), channel_id=1, source_target_pairs={{0,16},{32,48},{64,80},{96,112},{128,144},{160,176},{192,208},{224... | collective-permute-start | bytes 294920 | tf_op jit(solution)/shard_map/ppermute | solution.py:515
  39.6 0.9 shard_map.63
  40.5 0.0 collective-permute-done.5.refs_2_.refs_10_
  40.5 1.0 collective-permute-done.4.refs_1_.refs_9_
  41.6 0.1 shard_map.64
  41.6 16.5 %all_to_all.20.refs_11_ = f32[4,2,6,4,8,128]{5,4,3,2,1,0:T(8,128)S(1)} all-to-all(f32[4,2,6,4,8,128]{5,4,3,2,1,0:T(8,128)S(1)} %shard_map.64), channel_id=1, replica_groups=mesh['real'=2,'zh'=4,'zl'=4,'xc'=4,'yl'=2,'core'=2] {'xc'}, dimensions={0} | all-to-all | bytes 1572864 | tf_op jit(solution)/shard_map/all_to_all | solution.py:522
  58.1 4.3 %shard_map.65 = (f32[7,3,36,8,128]{4,3,2,1,0:T(8,128)S(1)}, f32[7,3,18,8,128]{4,3,2,1,0:T(8,128)S(1)}, f32[7,3,9,8,128]{4,3,2,1,0:T(8,128)S(1)}, f32[3,24,16,256...) custom-call(f32[24,16,256]{2,1,0:T(8,128)S(1)} %get-tuple-element.71.refs_3_.refs_0_, ...), custom_call_target="tpu_custom_call" | custom-call | tf_op jit(solution)/shard_map/pallas_call | solution.py:492
  62.4 0.7 collective-permute-start.7
  63.1 7.6 %collective-permute-start.6 = (f32[3,4,8,128]{3,2,1,0:T(8,128)S(1)}, f32[3,4,8,128]{3,2,1,0:T(8,128)S(1)}, u32[]{:S(2)}, u32[]{:S(2)}) collective-permute-start(f32[3,4,8,128]{3,2,1,0:T(8,128)S(1)} %get-tuple-element.85.refs_0_.refs_13_), channel_id=1, source_target_pairs={{0,16},{32,48},{64,80},{96,112},{128,144},{160,176},{192,208},{224... | collective-permute-start | bytes 147464 | tf_op jit(solution)/shard_map/ppermute | solution.py:515
  70.7 0.0 collective-permute-done.7.refs_2_.refs_15_
  70.7 1.5 %collective-permute-done.6.refs_1_.refs_14_ = f32[3,4,8,128]{3,2,1,0:T(8,128)S(1)} collective-permute-done((f32[3,4,8,128]{3,2,1,0:T(8,128)S(1)}, f32[3,4,8,128]{3,2,1,0:T(8,128)S(1)}, u32[]{:S(2)}, u32[]{:S(2)}) %collective-permute-start.6) | collective-permute-done | bytes 49184 | tf_op jit(solution)/shard_map/ppermute | solution.py:515
  72.2 10.2 %all_to_all.21.refs_16_ = f32[4,2,3,4,8,128]{5,4,3,2,1,0:T(8,128)S(1)} all-to-all(f32[4,2,3,4,8,128]{5,4,3,2,1,0:T(8,128)S(1)} %shard_map.66), channel_id=1, replica_groups=mesh['real'=2,'zh'=4,'zl'=4,'xc'=4,'yl'=2,'core'=2] {'xc'}, dimensions={0} | all-to-all | bytes 786432 | tf_op jit(solution)/shard_map/all_to_all | solution.py:522
  82.4 2.4 %shard_map.67 = (f32[3,24,16,256]{3,2,1,0:T(8,128)S(1)}, f32[16,1,128]{2,1,0:T(1,128)S(1)}) custom-call(f32[24,16,256]{2,1,0:T(8,128)S(1)} %get-tuple-element.71.refs_3_.refs_0_, f32[3,24,16,256]{3,2,1,0:T(8,128)S(1)} %get-tuple-element.72.refs_1_, f32[3,24,16,256]{3,2,1,0:T(8,128)S(1)} %get-tuple-element.73.refs_2_, ...), custom_call_target="tpu_custom_call" | custom-call | tf_op jit(solution)/shard_map/pallas_call | solution.py:492
  84.8 11.3 %all_to_all.22.in_ref = f32[16,1,128]{2,1,0:T(1,128)S(1)} all-to-all(f32[16,1,128]{2,1,0:T(1,128)S(1)} %get-tuple-element.87), channel_id=1, replica_groups=mesh['real'=2,'zh'=4,'zl'=4,'xc'=4,'yl'=2,'core'=2] {'xc','yl','core'}, dimensions={0} | all-to-all | bytes 16384 | tf_op jit(solution)/shard_map/all_to_all | solution.py:563
  96.1 24.9 %all_to_all.23.refs_3_ = f32[16,1,128]{2,1,0:T(1,128)S(1)} all-to-all(f32[16,1,128]{2,1,0:T(1,128)S(1)} %shard_map.68), channel_id=1, replica_groups=mesh['real'=2,'zh'=4,'zl'=4,'xc'=4,'yl'=2,'core'=2] {'zh','zl'}, dimensions={0} | all-to-all | bytes 16384 | tf_op jit(solution)/shard_map/all_to_all | solution.py:565
  121.1 1.3 %shard_map.69 = (f32[8,8,128]{2,1,0:T(8,128)}, f32[3]{0:T(128)}) custom-call(f32[3,24,16,256]{3,2,1,0:T(8,128)S(1)} %get-tuple-element.70.refs_0_, f32[3,24,16,256]{3,2,1,0:T(8,128)S(1)} %get-tuple-element.80.refs_11_.refs_1_, f32[3,24,16,256]{3,2,1,0:T(8,128)S(1)} %get-tuple-element.86.refs_2_, f32[16,1,128]{2,1,0:T(1,128)S(1)} %all_to_all.23.refs_3_), custom_call_target="tpu_custom_call" | custom-call | tf_op jit(solution)/shard_map/pallas_call | solution.py:492
  (4 shorter events, 0.1 us)
Async XLA Ops:
  8.5 11.1 %collective-permute-start = (f32[2,4,4,8,128]{4,3,2,1,0:T(8,128)S(1)}, f32[2,4,4,8,128]{4,3,2,1,0:T(8,128)S(1)}, u32[]{:S(2)}, u32[]{:S(2)}) collective-permute-start(f32[2,4,4,8,128]{4,3,2,1,0:T(8,128)S(1)} %get-tuple-element.45), channel_id=1, source_target_pairs={{0,1},{2,3},{1,0},{3,2},{4,5},{6,7},{5,4},{7,6},{8,9},{10,11},{9,8... | collective-permute-start | bytes 393224 | tf_op jit(solution)/shard_map/ppermute | solution.py:515
  17.6 6.3 %collective-permute-start.1 = (f32[2,4,4,8,128]{4,3,2,1,0:T(8,128)S(1)}, f32[2,4,4,8,128]{4,3,2,1,0:T(8,128)S(1)}, u32[]{:S(2)}, u32[]{:S(2)}) collective-permute-start(f32[2,4,4,8,128]{4,3,2,1,0:T(8,128)S(1)} %get-tuple-element.46), channel_id=1, source_target_pairs={{1,2},{2,1},{5,6},{6,5},{9,10},{10,9},{13,14},{14,13},{17,18},{18,... | collective-permute-start | bytes 393224 | tf_op jit(solution)/shard_map/ppermute | solution.py:515
  24.1 6.0 %collective-permute-start.2 = (f32[24,16,256]{2,1,0:T(8,128)S(1)}, f32[24,16,256]{2,1,0:T(8,128)S(1)}, u32[]{:S(2)}, u32[]{:S(2)}) collective-permute-start(f32[24,16,256]{2,1,0:T(8,128)S(1)} %get-tuple-element.48), channel_id=1, source_target_pairs={{0,4},{4,8},{8,12},{12,16},{16,20},{20,24},{24,28},{28,32},{32,36}... | collective-permute-start | bytes 1179656 | tf_op jit(solution)/shard_map/ppermute | solution.py:533
  25.5 8.5 %collective-permute-start.3 = (f32[24,16,256]{2,1,0:T(8,128)S(1)}, f32[24,16,256]{2,1,0:T(8,128)S(1)}, u32[]{:S(2)}, u32[]{:S(2)}) collective-permute-start(f32[24,16,256]{2,1,0:T(8,128)S(1)} %get-tuple-element.49), channel_id=1, source_target_pairs={{4,0},{8,4},{12,8},{16,12},{20,16},{24,20},{28,24},{32,28},{36,32}... | collective-permute-start | bytes 1179656 | tf_op jit(solution)/shard_map/ppermute | solution.py:534
  35.3 5.2 %collective-permute-start.5 = (f32[6,4,8,128]{3,2,1,0:T(8,128)S(1)}, f32[6,4,8,128]{3,2,1,0:T(8,128)S(1)}, u32[]{:S(2)}, u32[]{:S(2)}) collective-permute-start(f32[6,4,8,128]{3,2,1,0:T(8,128)S(1)} %get-tuple-element.79.refs_0_.refs_8_), channel_id=1, source_target_pairs={{16,32},{48,64},{80,96},{112,128},{144,160},{176,192},{208,224},{3... | collective-permute-start | bytes 294920 | tf_op jit(solution)/shard_map/ppermute | solution.py:515
  36.0 5.6 %collective-permute-start.4 = (f32[6,4,8,128]{3,2,1,0:T(8,128)S(1)}, f32[6,4,8,128]{3,2,1,0:T(8,128)S(1)}, u32[]{:S(2)}, u32[]{:S(2)}) collective-permute-start(f32[6,4,8,128]{3,2,1,0:T(8,128)S(1)} %get-tuple-element.79.refs_0_.refs_8_), channel_id=1, source_target_pairs={{0,16},{32,48},{64,80},{96,112},{128,144},{160,176},{192,208},{224... | collective-permute-start | bytes 294920 | tf_op jit(solution)/shard_map/ppermute | solution.py:515
  62.4 8.3 %collective-permute-start.7 = (f32[3,4,8,128]{3,2,1,0:T(8,128)S(1)}, f32[3,4,8,128]{3,2,1,0:T(8,128)S(1)}, u32[]{:S(2)}, u32[]{:S(2)}) collective-permute-start(f32[3,4,8,128]{3,2,1,0:T(8,128)S(1)} %get-tuple-element.85.refs_0_.refs_13_), channel_id=1, source_target_pairs={{16,32},{48,64},{80,96},{112,128},{144,160},{176,192},{208,224},{3... | collective-permute-start | bytes 147464 | tf_op jit(solution)/shard_map/ppermute | solution.py:515
  63.1 9.1 %collective-permute-start.6 = (f32[3,4,8,128]{3,2,1,0:T(8,128)S(1)}, f32[3,4,8,128]{3,2,1,0:T(8,128)S(1)}, u32[]{:S(2)}, u32[]{:S(2)}) collective-permute-start(f32[3,4,8,128]{3,2,1,0:T(8,128)S(1)} %get-tuple-element.85.refs_0_.refs_13_), channel_id=1, source_target_pairs={{0,16},{32,48},{64,80},{96,112},{128,144},{160,176},{192,208},{224... | collective-permute-start | bytes 147464 | tf_op jit(solution)/shard_map/ppermute | solution.py:515

commit v9 on v7

--- a/solution.py
+++ b/solution.py
@@ -194,19 +194,6 @@
 WIDE = (5, 4, 4, 3)
 WIDE_AT = (0, 5, 9, 13)
 SENT = (41, 16, 128)
-
-
-def pack_kernel(d_ref, v_ref, s_ref, load_ref, out_ref, v_in, s_in, sems):
-    pairs = ((d_ref, out_ref.at[0]), (v_ref, v_in), (s_ref, s_in), (load_ref, out_ref.at[3]))
-    copies = [pltpu.make_async_copy(src, dst, sems.at[q]) for q, (src, dst) in enumerate(pairs)]
-    for copy in copies:
-        copy.start()
-    copies[1].wait()
-    out_ref[1] = v_in[...].astype(F32)
-    copies[2].wait()
-    out_ref[2] = s_in[...].astype(F32)
-    copies[0].wait()
-    copies[3].wait()
 
 
 def halve_kernel(place_ref, c_ref, even_ref, odd_ref):
@@ -556,13 +543,9 @@
 
 
 def body(design, load, void_mask, solid_mask):
-    own = pl.pallas_call(
-        pack_kernel,
-        out_shape=shaped(4, 8, 8, 128),
-        in_specs=[pl.BlockSpec(memory_space=pl.ANY)] * 4,
-        out_specs=pl.BlockSpec(memory_space=pltpu.VMEM),
-        scratch_shapes=[pltpu.VMEM((8, 8, 128), jnp.int32)] * 2 + [pltpu.SemaphoreType.DMA((4,))],
-    )(design, void_mask, solid_mask, load)
+    which = iota((4, 8, 8, 128), 0)
+    masks = jnp.where(which == 1, void_mask[None], solid_mask[None]).astype(F32)
+    own = jnp.where(which == 0, design[None], jnp.where(which == 3, load[None], masks))
     both = lax.all_gather(own, "real")
     outs = (shaped(4, 8, 16, 256), shaped(*SENT), shaped(*SENT))
     halves = call(halve_kernel, (shaped(2, 4, 4, 8, 128),) * 2, [], both, place=True)

time: 123 us -> 123 us (level)
    pallas_call x1 -> x0, Pallas kernels: 1.49 us -> none  [body(): pl.pallas_call(pack_kernel, out_shape=shaped(4, 8, 8, 128), in_specs=[pl....]
where the time goes in v9:
time: 123 us; the launch traced here: 122 us
  blocking collectives  69.6 us (57%)
  starting transfers between devices  26.3 us (21%)
  waiting for transfers between devices  12.6 us (10%)
  Pallas kernels  11.6 us (9%)
    all_to_all x2, blocking collectives, fetch(): return (own, even, odd, lax.all_to_all(mixed, 'xc', 0, 0))  26.6 us
    all_to_all x1, blocking collectives, body(): dots = lax.all_to_all(dots, ('zh', 'zl'), 0, 0, tiled=True)  25 us
    ppermute x6, starting transfers between devices, swap(): got.append(lax.ppermute(v, axes, pairs + [(j, i) for i, j in pairs]))  23.7 us
    pallas_call x11, Pallas kernels, call(): pl.pallas_call(body, out_shape=outs, in_specs=[pl.BlockSpec(memory_space=...  11.6 us
    all_to_all x1, blocking collectives, body(): dots = lax.all_to_all(dots, ('xc', 'yl', 'core'), 0, 0, tiled=True)  11.3 us
    all_gather x1, blocking collectives, body(): both = lax.all_gather(own, 'real')  6.76 us
    ppermute x6, waiting for transfers between devices, swap(): got.append(lax.ppermute(v, axes, pairs + [(j, i) for i, j in pairs]))  6.7 us
    ppermute x1, waiting for transfers between devices, body(): hi = lax.ppermute(down, X_AXES, [(i + 1, i) for i in range(NBX - 1)])  3.84 us
  transfers between devices with their start and end apart: 8, of which 5 were waited for; matrix products, arithmetic and copies ran while one was open for 0% of the time, Pallas kernels for 1%

profile of v9, /device:TPU:1, one launch (start us, length us, event | category | flops | bytes accessed | tf_op | source)
XLA Modules:
  0.0 121.8 jit_solution(2509738189126757865)
XLA Ops:
  0.7 0.9 select_select_fusion
  1.6 6.8 %all_gather.4.refs_0_ = f32[2,4,8,8,128]{4,3,2,1,0:T(8,128)S(1)} all-gather(f32[1,4,8,8,128]{4,3,2,1,0:T(8,128)S(1)} %select_select_fusion), channel_id=1, replica_groups=mesh['real'=2,'zh'=4,'zl'=4,'xc'=4,'yl'=2,'core'=2] {'real'}, dimensions={0}, use_global_device_ids=true | all-gather | bytes 393216 | tf_op jit(solution)/shard_map/all_gather | solution.py:549
  8.3 0.1 shard_map.59
  8.5 9.2 %collective-permute-start = (f32[2,4,4,8,128]{4,3,2,1,0:T(8,128)S(1)}, f32[2,4,4,8,128]{4,3,2,1,0:T(8,128)S(1)}, u32[]{:S(2)}, u32[]{:S(2)}) collective-permute-start(f32[2,4,4,8,128]{4,3,2,1,0:T(8,128)S(1)} %get-tuple-element.45), channel_id=1, source_target_pairs={{0,1},{2,3},{1,0},{3,2},{4,5},{6,7},{5,4},{7,6},{8,9},{10,11},{9,8... | collective-permute-start | bytes 393224 | tf_op jit(solution)/shard_map/ppermute | solution.py:535
  17.6 1.9 %collective-permute-start.1 = (f32[2,4,4,8,128]{4,3,2,1,0:T(8,128)S(1)}, f32[2,4,4,8,128]{4,3,2,1,0:T(8,128)S(1)}, u32[]{:S(2)}, u32[]{:S(2)}) collective-permute-start(f32[2,4,4,8,128]{4,3,2,1,0:T(8,128)S(1)} %get-tuple-element.46), channel_id=1, source_target_pairs={{1,2},{2,1},{5,6},{6,5},{9,10},{10,9},{13,14},{14,13},{17,18},{18,... | collective-permute-start | bytes 393224 | tf_op jit(solution)/shard_map/ppermute | solution.py:535
  19.6 0.0 collective-permute-done.refs_1_
  19.6 4.3 %collective-permute-done.1.refs_2_ = f32[2,4,4,8,128]{4,3,2,1,0:T(8,128)S(1)} collective-permute-done((f32[2,4,4,8,128]{4,3,2,1,0:T(8,128)S(1)}, f32[2,4,4,8,128]{4,3,2,1,0:T(8,128)S(1)}, u32[]{:S(2)}, u32[]{:S(2)}) %collective-permute-start.1) | collective-permute-done | bytes 131104 | tf_op jit(solution)/shard_map/ppermute | solution.py:535
  23.9 0.2 shard_map.60
  24.2 1.3 %collective-permute-start.2 = (f32[41,16,128]{2,1,0:T(8,128)S(1)}, f32[41,16,128]{2,1,0:T(8,128)S(1)}, u32[]{:S(2)}, u32[]{:S(2)}) collective-permute-start(f32[41,16,128]{2,1,0:T(8,128)S(1)} %get-tuple-element.48), channel_id=1, source_target_pairs={{0,4},{4,8},{8,12},{12,16},{16,20},{20,24},{24,28},{28,32},{32,36}... | collective-permute-start | bytes 1007624 | tf_op jit(solution)/shard_map/ppermute | solution.py:553
  25.5 1.3 %collective-permute-start.3 = (f32[41,16,128]{2,1,0:T(8,128)S(1)}, f32[41,16,128]{2,1,0:T(8,128)S(1)}, u32[]{:S(2)}, u32[]{:S(2)}) collective-permute-start(f32[41,16,128]{2,1,0:T(8,128)S(1)} %get-tuple-element.49), channel_id=1, source_target_pairs={{4,0},{8,4},{12,8},{16,12},{20,16},{24,20},{28,24},{32,28},{36,32}... | collective-permute-start | bytes 1007624 | tf_op jit(solution)/shard_map/ppermute | solution.py:554
  26.8 0.7 shard_map.61
  27.5 2.1 %collective-permute-done.2.refs_1_ = f32[41,16,128]{2,1,0:T(8,128)S(1)} collective-permute-done((f32[41,16,128]{2,1,0:T(8,128)S(1)}, f32[41,16,128]{2,1,0:T(8,128)S(1)}, u32[]{:S(2)}, u32[]{:S(2)}) %collective-permute-start.2) | collective-permute-done | bytes 335904 | tf_op jit(solution)/shard_map/ppermute | solution.py:553
  29.5 3.8 %collective-permute-done.3.refs_2_ = f32[41,16,128]{2,1,0:T(8,128)S(1)} collective-permute-done((f32[41,16,128]{2,1,0:T(8,128)S(1)}, f32[41,16,128]{2,1,0:T(8,128)S(1)}, u32[]{:S(2)}, u32[]{:S(2)}) %collective-permute-start.3) | collective-permute-done | bytes 335904 | tf_op jit(solution)/shard_map/ppermute | solution.py:554
  33.4 1.3 %shard_map.62 = (f32[6,4,8,128]{3,2,1,0:T(8,128)S(1)}, f32[24,16,256]{2,1,0:T(8,128)S(1)}, f32[3,24,16,256]{3,2,1,0:T(8,128)S(1)}, f32[3,24,16,256]{3,2,1,0:T(8,...) custom-call(f32[4,8,16,256]{3,2,1,0:T(8,128)S(1)} %get-tuple-element, ...), custom_call_target="tpu_custom_call", output_to_operand_aliasing={{1}: (3, {}), {2}: (4, {}), {3}: (5, {}), {4}: (6, {}), {5}... | custom-call | tf_op jit(solution)/shard_map/pallas_call | solution.py:512
  34.7 0.7 collective-permute-start.5
  35.4 3.6 %collective-permute-start.4 = (f32[6,4,8,128]{3,2,1,0:T(8,128)S(1)}, f32[6,4,8,128]{3,2,1,0:T(8,128)S(1)}, u32[]{:S(2)}, u32[]{:S(2)}) collective-permute-start(f32[6,4,8,128]{3,2,1,0:T(8,128)S(1)} %get-tuple-element.79.refs_0_.refs_8_), channel_id=1, source_target_pairs={{0,16},{32,48},{64,80},{96,112},{128,144},{160,176},{192,208},{224... | collective-permute-start | bytes 294920 | tf_op jit(solution)/shard_map/ppermute | solution.py:535
  39.0 1.1 shard_map.63
  40.1 0.0 collective-permute-done.5.refs_2_.refs_10_
  40.1 0.9 collective-permute-done.4.refs_1_.refs_9_
  41.0 0.1 shard_map.64
  41.0 16.5 %all_to_all.20.refs_11_ = f32[4,2,6,4,8,128]{5,4,3,2,1,0:T(8,128)S(1)} all-to-all(f32[4,2,6,4,8,128]{5,4,3,2,1,0:T(8,128)S(1)} %shard_map.64), channel_id=1, replica_groups=mesh['real'=2,'zh'=4,'zl'=4,'xc'=4,'yl'=2,'core'=2] {'xc'}, dimensions={0} | all-to-all | bytes 1572864 | tf_op jit(solution)/shard_map/all_to_all | solution.py:542
  57.5 4.3 %shard_map.65 = (f32[7,3,36,8,128]{4,3,2,1,0:T(8,128)S(1)}, f32[7,3,18,8,128]{4,3,2,1,0:T(8,128)S(1)}, f32[7,3,9,8,128]{4,3,2,1,0:T(8,128)S(1)}, f32[3,24,16,256...) custom-call(f32[24,16,256]{2,1,0:T(8,128)S(1)} %get-tuple-element.71.refs_3_.refs_0_, ...), custom_call_target="tpu_custom_call" | custom-call | tf_op jit(solution)/shard_map/pallas_call | solution.py:512
  61.8 0.7 collective-permute-start.7
  62.5 7.6 %collective-permute-start.6 = (f32[3,4,8,128]{3,2,1,0:T(8,128)S(1)}, f32[3,4,8,128]{3,2,1,0:T(8,128)S(1)}, u32[]{:S(2)}, u32[]{:S(2)}) collective-permute-start(f32[3,4,8,128]{3,2,1,0:T(8,128)S(1)} %get-tuple-element.85.refs_0_.refs_13_), channel_id=1, source_target_pairs={{0,16},{32,48},{64,80},{96,112},{128,144},{160,176},{192,208},{224... | collective-permute-start | bytes 147464 | tf_op jit(solution)/shard_map/ppermute | solution.py:535
  70.1 0.0 collective-permute-done.7.refs_2_.refs_15_
  70.1 1.5 %collective-permute-done.6.refs_1_.refs_14_ = f32[3,4,8,128]{3,2,1,0:T(8,128)S(1)} collective-permute-done((f32[3,4,8,128]{3,2,1,0:T(8,128)S(1)}, f32[3,4,8,128]{3,2,1,0:T(8,128)S(1)}, u32[]{:S(2)}, u32[]{:S(2)}) %collective-permute-start.6) | collective-permute-done | bytes 49184 | tf_op jit(solution)/shard_map/ppermute | solution.py:535
  71.6 10.2 %all_to_all.21.refs_16_ = f32[4,2,3,4,8,128]{5,4,3,2,1,0:T(8,128)S(1)} all-to-all(f32[4,2,3,4,8,128]{5,4,3,2,1,0:T(8,128)S(1)} %shard_map.66), channel_id=1, replica_groups=mesh['real'=2,'zh'=4,'zl'=4,'xc'=4,'yl'=2,'core'=2] {'xc'}, dimensions={0} | all-to-all | bytes 786432 | tf_op jit(solution)/shard_map/all_to_all | solution.py:542
  81.8 2.4 %shard_map.67 = (f32[3,24,16,256]{3,2,1,0:T(8,128)S(1)}, f32[16,1,128]{2,1,0:T(1,128)S(1)}) custom-call(f32[24,16,256]{2,1,0:T(8,128)S(1)} %get-tuple-element.71.refs_3_.refs_0_, f32[3,24,16,256]{3,2,1,0:T(8,128)S(1)} %get-tuple-element.72.refs_1_, f32[3,24,16,256]{3,2,1,0:T(8,128)S(1)} %get-tuple-element.73.refs_2_, ...), custom_call_target="tpu_custom_call" | custom-call | tf_op jit(solution)/shard_map/pallas_call | solution.py:512
  84.2 11.3 %all_to_all.22.in_ref = f32[16,1,128]{2,1,0:T(1,128)S(1)} all-to-all(f32[16,1,128]{2,1,0:T(1,128)S(1)} %get-tuple-element.87), channel_id=1, replica_groups=mesh['real'=2,'zh'=4,'zl'=4,'xc'=4,'yl'=2,'core'=2] {'xc','yl','core'}, dimensions={0} | all-to-all | bytes 16384 | tf_op jit(solution)/shard_map/all_to_all | solution.py:583
  95.5 25.0 %all_to_all.23.refs_3_ = f32[16,1,128]{2,1,0:T(1,128)S(1)} all-to-all(f32[16,1,128]{2,1,0:T(1,128)S(1)} %shard_map.68), channel_id=1, replica_groups=mesh['real'=2,'zh'=4,'zl'=4,'xc'=4,'yl'=2,'core'=2] {'zh','zl'}, dimensions={0} | all-to-all | bytes 16384 | tf_op jit(solution)/shard_map/all_to_all | solution.py:585
  120.5 1.3 %shard_map.69 = (f32[8,8,128]{2,1,0:T(8,128)}, f32[3]{0:T(128)}) custom-call(f32[3,24,16,256]{3,2,1,0:T(8,128)S(1)} %get-tuple-element.70.refs_0_, f32[3,24,16,256]{3,2,1,0:T(8,128)S(1)} %get-tuple-element.80.refs_11_.refs_1_, f32[3,24,16,256]{3,2,1,0:T(8,128)S(1)} %get-tuple-element.86.refs_2_, f32[16,1,128]{2,1,0:T(1,128)S(1)} %all_to_all.23.refs_3_), custom_call_target="tpu_custom_call" | custom-call | tf_op jit(solution)/shard_map/pallas_call | solution.py:512
  (4 shorter events, 0.1 us)
Async XLA Ops:
  8.5 11.1 %collective-permute-start = (f32[2,4,4,8,128]{4,3,2,1,0:T(8,128)S(1)}, f32[2,4,4,8,128]{4,3,2,1,0:T(8,128)S(1)}, u32[]{:S(2)}, u32[]{:S(2)}) collective-permute-start(f32[2,4,4,8,128]{4,3,2,1,0:T(8,128)S(1)} %get-tuple-element.45), channel_id=1, source_target_pairs={{0,1},{2,3},{1,0},{3,2},{4,5},{6,7},{5,4},{7,6},{8,9},{10,11},{9,8... | collective-permute-start | bytes 393224 | tf_op jit(solution)/shard_map/ppermute | solution.py:535
  17.6 6.3 %collective-permute-start.1 = (f32[2,4,4,8,128]{4,3,2,1,0:T(8,128)S(1)}, f32[2,4,4,8,128]{4,3,2,1,0:T(8,128)S(1)}, u32[]{:S(2)}, u32[]{:S(2)}) collective-permute-start(f32[2,4,4,8,128]{4,3,2,1,0:T(8,128)S(1)} %get-tuple-element.46), channel_id=1, source_target_pairs={{1,2},{2,1},{5,6},{6,5},{9,10},{10,9},{13,14},{14,13},{17,18},{18,... | collective-permute-start | bytes 393224 | tf_op jit(solution)/shard_map/ppermute | solution.py:535
  24.2 5.4 %collective-permute-start.2 = (f32[41,16,128]{2,1,0:T(8,128)S(1)}, f32[41,16,128]{2,1,0:T(8,128)S(1)}, u32[]{:S(2)}, u32[]{:S(2)}) collective-permute-start(f32[41,16,128]{2,1,0:T(8,128)S(1)} %get-tuple-element.48), channel_id=1, source_target_pairs={{0,4},{4,8},{8,12},{12,16},{16,20},{20,24},{24,28},{28,32},{32,36}... | collective-permute-start | bytes 1007624 | tf_op jit(solution)/shard_map/ppermute | solution.py:553
  25.5 7.9 %collective-permute-start.3 = (f32[41,16,128]{2,1,0:T(8,128)S(1)}, f32[41,16,128]{2,1,0:T(8,128)S(1)}, u32[]{:S(2)}, u32[]{:S(2)}) collective-permute-start(f32[41,16,128]{2,1,0:T(8,128)S(1)} %get-tuple-element.49), channel_id=1, source_target_pairs={{4,0},{8,4},{12,8},{16,12},{20,16},{24,20},{28,24},{32,28},{36,32}... | collective-permute-start | bytes 1007624 | tf_op jit(solution)/shard_map/ppermute | solution.py:554
  34.7 5.4 %collective-permute-start.5 = (f32[6,4,8,128]{3,2,1,0:T(8,128)S(1)}, f32[6,4,8,128]{3,2,1,0:T(8,128)S(1)}, u32[]{:S(2)}, u32[]{:S(2)}) collective-permute-start(f32[6,4,8,128]{3,2,1,0:T(8,128)S(1)} %get-tuple-element.79.refs_0_.refs_8_), channel_id=1, source_target_pairs={{16,32},{48,64},{80,96},{112,128},{144,160},{176,192},{208,224},{3... | collective-permute-start | bytes 294920 | tf_op jit(solution)/shard_map/ppermute | solution.py:535
  35.4 5.6 %collective-permute-start.4 = (f32[6,4,8,128]{3,2,1,0:T(8,128)S(1)}, f32[6,4,8,128]{3,2,1,0:T(8,128)S(1)}, u32[]{:S(2)}, u32[]{:S(2)}) collective-permute-start(f32[6,4,8,128]{3,2,1,0:T(8,128)S(1)} %get-tuple-element.79.refs_0_.refs_8_), channel_id=1, source_target_pairs={{0,16},{32,48},{64,80},{96,112},{128,144},{160,176},{192,208},{224... | collective-permute-start | bytes 294920 | tf_op jit(solution)/shard_map/ppermute | solution.py:535
  61.8 8.3 %collective-permute-start.7 = (f32[3,4,8,128]{3,2,1,0:T(8,128)S(1)}, f32[3,4,8,128]{3,2,1,0:T(8,128)S(1)}, u32[]{:S(2)}, u32[]{:S(2)}) collective-permute-start(f32[3,4,8,128]{3,2,1,0:T(8,128)S(1)} %get-tuple-element.85.refs_0_.refs_13_), channel_id=1, source_target_pairs={{16,32},{48,64},{80,96},{112,128},{144,160},{176,192},{208,224},{3... | collective-permute-start | bytes 147464 | tf_op jit(solution)/shard_map/ppermute | solution.py:535
  62.5 9.1 %collective-permute-start.6 = (f32[3,4,8,128]{3,2,1,0:T(8,128)S(1)}, f32[3,4,8,128]{3,2,1,0:T(8,128)S(1)}, u32[]{:S(2)}, u32[]{:S(2)}) collective-permute-start(f32[3,4,8,128]{3,2,1,0:T(8,128)S(1)} %get-tuple-element.85.refs_0_.refs_13_), channel_id=1, source_target_pairs={{0,16},{32,48},{64,80},{96,112},{128,144},{160,176},{192,208},{224... | collective-permute-start | bytes 147464 | tf_op jit(solution)/shard_map/ppermute | solution.py:535
